TPU v7x, 256 devices: a whole 4x4x8 slice. The times are simulated.
256 devices in a mesh: slab: 4 (over x), xs: 64 (over z, y, core).
Axes of the slice: x: 4, y: 4, z: 8, core: 2. Of those that a mesh axis runs over, the one named last changes fastest.
Arguments:
- perturbation: int32 [4, 1024, 1024], P('slab', 'xs'), may hold values from 0 to 15
- seeds: int32 [4, 32, 2], P('slab'), may hold values from 1 to 8, as said below
Outputs:
- modes: float32 [4, 32, 1024, 1024], P('slab', None, 'xs')
- projected: float32 [4, 32, 32], P('slab')
- correlations: float32 [4, 32, 32], P('slab')
Inputs may be any that keep to these rules, and one draw needn't show every extreme that they name: `seeds`: within one slice the 32 pairs (first, second) are distinct; the pairs (1, 1) and (8, 8) occur in every slice.
All inputs are finite; a program needn't handle non-finite values.
Results may differ from a plain program's by a relative error of at most 0.0003.
Values sent between devices are 32-bit elements; how exact they have to be, the bound alone decides.
No kernel may reach another device: no remote copies, remote signals or barrier semaphores. Data moves between devices by JAX's collectives and lax.ppermute only.
A program may use at most 64 MiB of HBM per device.

v0:
```python
import math

import jax
import jax.numpy as jnp
from jax import lax
from jax.sharding import PartitionSpec as P

NX = 1024
SWEEPS = 4


def padded_2(array, sides, width):
    for axis, dim in sides:
        size, length = (lax.axis_size(axis), array.shape[dim])
        up = [(i, (i + 1) % size) for i in range(size - 1)]
        down = [(j, i) for i, j in up]
        last = lax.slice_in_dim(array, length - width, length, axis=dim)
        first = lax.slice_in_dim(array, 0, width, axis=dim)
        before = lax.ppermute(last, axis, up)
        after = lax.ppermute(first, axis, down)
        array = jnp.concatenate([before, array, after], axis=dim)
    return array


def from_behind(block, axis, distance):
    devices = range(lax.axis_size(axis))
    route = [(i - distance, i) for i in devices if i - distance in devices]
    return lax.ppermute(block, axis, route)


def potential(pert, row_ids, width):
    xpos = (row_ids.astype(jnp.float32)[:, None] + 0.5) / NX - 0.5
    ypos = (jnp.arange(width).astype(jnp.float32)[None, :] + 0.5) / width - 0.5
    conf = 4.0 * (xpos * xpos + 0.6 * ypos * ypos + 0.5 * xpos)
    return conf[None] + 0.1 * pert.astype(jnp.float32)


def start_basis(seeds_f, row_ids, width):
    scale = 2.0 / math.sqrt((NX + 1) * (width + 1))
    rows_f = row_ids.astype(jnp.float32) + 1.0
    cols_f = jnp.arange(width).astype(jnp.float32) + 1.0
    along_x = jnp.sin(math.pi * seeds_f[:, :, 0:1] * rows_f[None, None, :] / (NX + 1))
    along_y = jnp.sin(math.pi * seeds_f[:, :, 1:2] * cols_f[None, None, :] / (width + 1))
    return scale * along_x[:, :, :, None] * along_y[:, :, None, :]


def apply_ham(basis, pot):
    padded = padded_2(basis, (("xs", 2),), 1)
    sided = jnp.pad(basis, ((0, 0), (0, 0), (0, 0), (1, 1)))
    beside = padded[:, :, 2:, :] + padded[:, :, :-2, :] + sided[:, :, :, 2:] + sided[:, :, :, :-2]
    return 4.0 * basis - beside + pot[:, None] * basis


def orthonormal(trial, gram):
    lower = jnp.linalg.cholesky(gram)
    identity = jnp.broadcast_to(jnp.eye(gram.shape[1], dtype=gram.dtype), gram.shape)
    inverse = lax.linalg.triangular_solve(lower, identity, left_side=True, lower=True)
    return jnp.einsum("skij,smk->smij", trial, inverse, precision=lax.Precision.HIGHEST)


def local(perturbation, seeds):
    rows = perturbation.shape[1]
    width = perturbation.shape[2]
    row_ids = lax.axis_index("xs") * rows + jnp.arange(rows)
    pot = potential(perturbation, row_ids, width)
    seeds_f = seeds.astype(jnp.float32)
    basis = start_basis(seeds_f, row_ids, width)
    for sweep in range(SWEEPS):
        trial = 13.0 * basis - apply_ham(basis, pot)
        part_gram = jnp.einsum("mij,nij->mn", trial[0], trial[0], precision=lax.Precision.HIGHEST)
        pieces = [lax.psum(part_gram, "xs")]
        gram = jnp.stack(pieces, axis=0)
        basis = orthonormal(trial, gram)
    image = apply_ham(basis, pot)
    ham_part = jnp.einsum("smij,snij->smn", basis, image, precision=lax.Precision.HIGHEST)
    next_basis = from_behind(basis[0], "slab", -1)
    following = jnp.concatenate([basis[1:], next_basis[None]], axis=0)
    over_part = jnp.einsum("smij,snij->smn", basis, following, precision=lax.Precision.HIGHEST)
    projected, correlations = lax.psum((ham_part, over_part), "xs")
    modes = basis * math.sqrt(NX * width)
    return (modes, projected, correlations)


def solution(mesh):
    placed = (P("slab", "xs", None), P("slab", None, None))
    return jax.shard_map(
        local,
        mesh=mesh,
        in_specs=placed,
        out_specs=(P("slab", None, "xs", None), P("slab", None, None), P("slab", None, None)),
        check_vma=False,
    )
```

profile of v0, /device:TPU:132, one launch (start us, length us, event | category | flops | bytes accessed | tf_op | source)
XLA Modules:
  0.0 1377.9 jit_solution(3904637582738356508)
XLA Ops:
  2.2 3.9 collective-permute-start
  6.1 1.9 collective-permute-start.1
  8.6 7.1 collective-permute-done.1
  18.9 246.2 %psum.42 = f32[1,32,32]{1,2,0:T(8,128)S(1)} all-reduce(f32[1,32,32]{1,2,0:T(8,128)S(1)} %convolution_bitcast_fusion.8), channel_id=1, replica_groups=mesh['slab'=4,'xs'=64] {'xs'}, use_global_device_ids=true, to_apply=%region_0.1 | all-reduce | flops 1024 | bytes 8192 | tf_op jit(solution)/shard_map/psum | solution.py:71
  265.2 2.9 custom-call.12
  269.4 2.4 custom-call.13
  274.0 1.9 collective-permute-start.2
  276.0 2.4 collective-permute-start.3
  278.5 7.1 collective-permute-done.3
  288.5 246.4 %psum.43 = f32[1,32,32]{1,2,0:T(8,128)S(1)} all-reduce(f32[1,32,32]{1,2,0:T(8,128)S(1)} %convolution_bitcast_fusion.6), channel_id=1, replica_groups=mesh['slab'=4,'xs'=64] {'xs'}, use_global_device_ids=true, to_apply=%region_3.0 | all-reduce | flops 1024 | bytes 8192 | tf_op jit(solution)/shard_map/psum | solution.py:71
  535.0 2.9 custom-call.14
  539.2 2.4 custom-call.15
  543.8 1.9 collective-permute-start.4
  545.8 2.4 collective-permute-start.5
  548.3 7.1 collective-permute-done.5
  558.3 246.2 %psum.44 = f32[1,32,32]{1,2,0:T(8,128)S(1)} all-reduce(f32[1,32,32]{1,2,0:T(8,128)S(1)} %convolution_bitcast_fusion.4), channel_id=1, replica_groups=mesh['slab'=4,'xs'=64] {'xs'}, use_global_device_ids=true, to_apply=%region_4.0 | all-reduce | flops 1024 | bytes 8192 | tf_op jit(solution)/shard_map/psum | solution.py:71
  804.6 2.9 custom-call.16
  808.9 2.4 custom-call.17
  813.5 1.9 collective-permute-start.6
  815.4 2.6 collective-permute-start.7
  818.0 7.0 collective-permute-done.7
  827.9 246.2 %psum.45 = f32[1,32,32]{1,2,0:T(8,128)S(1)} all-reduce(f32[1,32,32]{1,2,0:T(8,128)S(1)} %convolution_bitcast_fusion.2), channel_id=1, replica_groups=mesh['slab'=4,'xs'=64] {'xs'}, use_global_device_ids=true, to_apply=%region_5.0 | all-reduce | flops 1024 | bytes 8192 | tf_op jit(solution)/shard_map/psum | solution.py:71
  1074.2 2.9 custom-call.18
  1078.5 2.4 custom-call.19
  1083.0 2.4 collective-permute-start.10
  1085.5 1.9 collective-permute-start.8
  1087.4 2.7 collective-permute-start.9
  1090.3 2.5 copy.13
  1092.8 4.2 collective-permute-done.9
  1097.0 2.5 fusion.43
  1099.6 27.7 %collective-permute-done.10 = f32[32,16,1024]{2,0,1:T(8,128)S(1)} collective-permute-done((f32[32,16,1024]{2,0,1:T(8,128)S(1)}, f32[32,16,1024]{2,0,1:T(8,128)S(1)}, u32[]{:S(2)}, u32[]{:S(2)}) %collective-permute-start.10) | collective-permute-done | bytes 2097184 | tf_op jit(solution)/shard_map/ppermute | solution.py:28
  1129.1 248.7 %all-reduce.5 = (f32[1,32,32]{2,1,0:T(8,128)}, f32[1,32,32]{2,1,0:T(8,128)}) all-reduce(f32[1,32,32]{2,1,0:T(8,128)S(1)} %fusion.43, f32[1,32,32]{2,1,0:T(8,128)S(1)} %convolution_bitcast_fusion), channel_id=1, replica_groups=mesh['slab'=4,'xs'=64] {'xs'}, use_global_device_ids=true, to_apply=%region_6.9 | all-reduce | flops 2048 | bytes 16384 | tf_op jit(solution)/shard_map/psum | solution.py:79
  (60 shorter events, 30.4 us)
Async XLA Ops:
  0.6 7.5 copy-start
  2.2 6.4 collective-permute-start
  6.1 9.6 collective-permute-start.1
  274.0 4.4 collective-permute-start.2
  276.0 9.6 collective-permute-start.3
  543.8 4.4 collective-permute-start.4
  545.8 9.6 collective-permute-start.5
  813.5 4.6 collective-permute-start.6
  815.4 9.6 collective-permute-start.7
  1083.0 44.3 %collective-permute-start.10 = (f32[32,16,1024]{2,0,1:T(8,128)S(1)}, f32[32,16,1024]{2,0,1:T(8,128)S(1)}, u32[]{:S(2)}, u32[]{:S(2)}) collective-permute-start(f32[32,16,1024]{2,0,1:T(8,128)S(1)} %fusion.86), channel_id=1, source_target_pairs={{64,0},{128,64},{192,128},{65,1},{129,65},{193,129},{66,2},{130,66... | collective-permute-start | bytes 6291464 | tf_op jit(solution)/shard_map/ppermute | solution.py:28
  1085.5 7.3 collective-permute-start.8
  1087.4 9.6 collective-permute-start.9
where the time goes:
time: 1380 us
  blocking collectives  1230 us (89%)
  waiting for transfers between devices  60.8 us (4%)
  other arithmetic  33.4 us (2%)
  starting transfers between devices  26.1 us (2%)
  matrix products  19.9 us (1%)
    psum x4, blocking collectives, local(): pieces = [lax.psum(part_gram, 'xs')]  985 us
    psum x1, blocking collectives, local(): projected, correlations = lax.psum((ham_part, over_part), 'xs')  249 us
    ppermute x5, waiting for transfers between devices, padded_2(): before = lax.ppermute(last, axis, up)  32.5 us
    ppermute x1, waiting for transfers between devices, from_behind(): return lax.ppermute(block, axis, route)  27.7 us
  transfers between devices with their start and end apart: 11, of which 9 were waited for; matrix products, arithmetic and copies ran while one was open for 0% of the time, Pallas kernels for 0%

commit v1 on v0

v1 whole, which is shorter than its diff:
```python
import functools
import math

import jax
import jax.numpy as jnp
from jax import lax
from jax.experimental import pallas as pl
from jax.experimental.pallas import tpu as pltpu
from jax.sharding import PartitionSpec as P

NX = 1024
NY = 1024
M = 32
KMAX = 8
ROWS = 16
HALO = 4
EXT = ROWS + 2 * HALO
LANES = 128
TILES = NY // LANES
F32 = jnp.float32
BF16 = jnp.bfloat16


def lane_tile(v):
    return slice(v * LANES, (v + 1) * LANES)


def split(x):
    high = x.astype(BF16)
    return high, (x - high.astype(F32)).astype(BF16)


def dot_t(a, b):
    return lax.dot_general(a, b, (((1,), (1,)), ((), ())), preferred_element_type=F32)


def prepare(k, strip_ref, xtab_ref, ytab_ref, w_ref, sy_ref, sx_ref):
    row = lax.broadcasted_iota(jnp.int32, (EXT, LANES), 0) + (k * ROWS - HALO)
    xpos = (row.astype(F32) + 0.5) / NX - 0.5
    for v in range(TILES):
        col = lax.broadcasted_iota(jnp.int32, (EXT, LANES), 1) + v * LANES
        ypos = (col.astype(F32) + 0.5) / NY - 0.5
        pert = strip_ref[0:EXT, lane_tile(v)].astype(F32)
        pot = 4.0 * (xpos * xpos + 0.6 * ypos * ypos + 0.5 * xpos) + 0.1 * pert
        rest = 9.0 - pot
        for r in range(EXT):
            w_ref[r, :, lane_tile(v)] = jnp.broadcast_to(rest[r : r + 1], (8, LANES))
    seeds = strip_ref[EXT : EXT + 1, 0:LANES].astype(F32)
    spread = jnp.transpose(jnp.broadcast_to(seeds, (LANES, LANES)))
    first, second = spread[0:M], spread[M : 2 * M]
    shift = jnp.zeros((M, LANES), F32)
    along_x = jnp.zeros((M, LANES), F32)
    for a in range(1, KMAX + 1):
        twice = 2.0 * math.cos(math.pi * a / (NX + 1))
        shift += jnp.where(first == a, twice, 0.0) + jnp.where(second == a, twice, 0.0)
        along_x = jnp.where(first == a, xtab_ref[a - 1 : a, :], along_x)
    for r in range(EXT):
        sx_ref[r] = jnp.broadcast_to(along_x[:, r : r + 1], (M, LANES))
    for v in range(TILES):
        along_y = jnp.zeros((M, LANES), F32)
        for b in range(1, KMAX + 1):
            along_y = jnp.where(second == b, ytab_ref[b - 1 : b, lane_tile(v)], along_y)
        sy_ref[:, lane_tile(v)] = along_y
    return shift


def first_sweep(shift, w_ref, sy_ref, sx_ref, out_ref):
    def row(r, carry):
        for t in range(M // 8):
            modes = slice(8 * t, 8 * t + 8)
            sx = sx_ref[r, modes, :]
            for v in range(TILES):
                w = w_ref[r, :, lane_tile(v)]
                out_ref[r, modes, lane_tile(v)] = (w + shift[modes]) * (sx * sy_ref[modes, lane_tile(v)])
        return carry

    lax.fori_loop(0, EXT, row, 0)


def sweep(first_row, last_row, w_ref, in_ref, out_ref):
    lane = lax.broadcasted_iota(jnp.int32, (8, LANES), 1)
    at_left, at_right = lane == 0, lane == LANES - 1
    zero = jnp.zeros((8, LANES), F32)

    def row(r, carry):
        for t in range(M // 8):
            modes = slice(8 * t, 8 * t + 8)
            here = [in_ref[r, modes, lane_tile(v)] for v in range(TILES)]
            fore = [zero] + [pltpu.roll(x, 1, 1) for x in here]
            back = [pltpu.roll(x, LANES - 1, 1) for x in here] + [zero]
            for v in range(TILES):
                left = jnp.where(at_left, fore[v], fore[v + 1])
                right = jnp.where(at_right, back[v + 1], back[v])
                above = in_ref[r - 1, modes, lane_tile(v)]
                below = in_ref[r + 1, modes, lane_tile(v)]
                w = w_ref[r, :, lane_tile(v)]
                out_ref[r, modes, lane_tile(v)] = (w * here[v] + (left + right)) + (above + below)
        return carry

    lax.fori_loop(first_row, last_row + 1, row, 0)


def keep_ends(k, ref):
    ref[HALO - 1] = ref[HALO - 1] * (k > 0).astype(F32)
    ref[EXT - HALO] = ref[EXT - HALO] * (k < NX // ROWS - 1).astype(F32)


def trial(k, margin, strip_ref, xtab_ref, ytab_ref, w_ref, sy_ref, sx_ref, one_ref, two_ref):
    shift = prepare(k, strip_ref, xtab_ref, ytab_ref, w_ref, sy_ref, sx_ref)
    first_sweep(shift, w_ref, sy_ref, sx_ref, one_ref)
    keep_ends(k, one_ref)
    low, high = HALO - margin, EXT - HALO - 1 + margin
    sweep(low - 2, high + 2, w_ref, one_ref, two_ref)
    keep_ends(k, two_ref)
    sweep(low - 1, high + 1, w_ref, two_ref, one_ref)
    keep_ends(k, one_ref)
    sweep(low, high, w_ref, one_ref, two_ref)
    keep_ends(k, two_ref)


def own_kernel(k_ref, strip_ref, xtab_ref, ytab_ref, parts_ref, sums_ref, w_ref, sy_ref, sx_ref, one_ref, two_ref):
    k = k_ref[0]
    trial(k, 1, strip_ref, xtab_ref, ytab_ref, w_ref, sy_ref, sx_ref, one_ref, two_ref)
    sweep(HALO, EXT - HALO - 1, w_ref, two_ref, one_ref)

    def row(r, total):
        high, low = split(two_ref[r + HALO])
        image_high, image_low = split(one_ref[r + HALO])
        parts_ref[r] = jnp.concatenate([high, low, high], axis=0)
        left = jnp.concatenate([high, low], axis=0)
        right = jnp.concatenate([high, image_high, low, image_low], axis=0)
        return total + dot_t(left, right)

    total = lax.fori_loop(0, ROWS, row, jnp.zeros((2 * M, 4 * M), F32))
    total = total[:, 0 : 2 * M] + total[:, 2 * M : 4 * M]
    sums_ref[...] = total[0:M] + total[M : 2 * M]


def next_kernel(k_ref, strip_ref, xtab_ref, ytab_ref, parts_ref, own_ref, sums_ref, w_ref, sy_ref, sx_ref, one_ref, two_ref):
    k = k_ref[0]
    trial(k, 0, strip_ref, xtab_ref, ytab_ref, w_ref, sy_ref, sx_ref, one_ref, two_ref)

    def row(r, total):
        high, low = split(two_ref[r + HALO])
        right = jnp.concatenate([high, low], axis=0)
        left = jnp.concatenate([right, parts_ref[r, 0 : 2 * M, :]], axis=0)
        return total + dot_t(left, right)

    total = lax.fori_loop(0, ROWS, row, jnp.zeros((4 * M, 2 * M), F32))
    total = total[:, 0:M] + total[:, M : 2 * M]
    gram, across = total[0:M] + total[M : 2 * M], total[2 * M : 3 * M] + total[3 * M : 4 * M]
    sums_ref[...] = jnp.concatenate([own_ref[...], gram, across], axis=1)


def finish_kernel(keep_ref, sums_ref, parts_ref, modes_ref, proj_ref, corr_ref, held_ref, sem):
    sums = sums_ref[...]
    row = lax.broadcasted_iota(jnp.int32, (M, LANES), 0)
    lane = lax.broadcasted_iota(jnp.int32, (M, LANES), 1)
    is_gram = (lane // M) % 2 == 0
    work = jnp.where(is_gram, sums, (lane % M == row).astype(F32))
    pivots = jnp.ones((M, LANES), F32)
    for j in range(M):
        column = jnp.where(lane < 2 * M, work[:, j : j + 1], work[:, 2 * M + j : 2 * M + j + 1])
        pivots = jnp.where(row == j, column, pivots)
        scaled = work[j : j + 1, :] / column[j : j + 1, :]
        work = work - jnp.where(row > j, column, 0.0) * scaled
    inverse = work / jnp.sqrt(pivots)
    own, following = inverse[:, M : 2 * M], inverse[:, 3 * M : 4 * M]
    high, low = split(own * math.sqrt(NX * NY))
    factors = jnp.concatenate([high, high, low], axis=1)

    copies = []
    width = NY // 4
    for c in range(4):
        cols = slice(c * width, (c + 1) * width)
        for r in range(ROWS):
            held_ref[:, r, cols] = jnp.dot(factors, parts_ref[r, :, cols], preferred_element_type=F32)
        copy = pltpu.make_async_copy(held_ref.at[:, :, cols], modes_ref.at[:, :, cols], sem.at[c])
        copy.start()
        copies.append(copy)

    exact = functools.partial(jnp.dot, precision=lax.Precision.HIGHEST, preferred_element_type=F32)
    image, across = sums[:, M : 2 * M], sums[:, 3 * M : 4 * M]
    eye = (row == lane)[:, 0:M].astype(F32)
    proj_ref[...] = 13.0 * eye - exact(exact(own, image), own.T)
    corr_ref[...] = jnp.where(keep_ref[0] > 0, exact(exact(own, across), following.T), 0.0)
    for copy in copies:
        copy.wait()


def add_over_strips(v):
    def others(x, *masks):
        return [lax.ppermute(x, "xs", [(i, i ^ mask) for i in range(64)]) for mask in masks]

    v = v + others(v, 1)[0]
    for unit in (2, 8):
        one, two, three = others(v, unit, 2 * unit, 3 * unit)
        v = (v + one) + (two + three)
    return v + others(v, 7 * 8)[0]


def local(perturbation, seeds):
    k = lax.axis_index("xs")
    slab = lax.axis_index("slab")
    strips = NX // ROWS
    pert = perturbation[0]
    before = lax.ppermute(pert[ROWS - HALO :], "xs", [(i, i + 1) for i in range(strips - 1)])
    after = lax.ppermute(pert[:HALO], "xs", [(i + 1, i) for i in range(strips - 1)])
    flat = jnp.pad(seeds[0].T.reshape(1, 2 * M), ((0, 7), (0, NY - 2 * M)))
    strip = jnp.concatenate([before, pert, after, flat], axis=0)
    following = lax.ppermute(strip, "slab", [((i + 1) % 4, i) for i in range(4)])

    index = jnp.arange(1, KMAX + 1).astype(F32)[:, None]
    rows = (k * ROWS - HALO + jnp.arange(LANES)).astype(F32)[None, :] + 1.0
    cols = jnp.arange(NY).astype(F32)[None, :] + 1.0
    scale = 2.0 / math.sqrt((NX + 1) * (NY + 1))
    xtab = scale * jnp.sin(math.pi * index * rows / (NX + 1))
    ytab = jnp.sin(math.pi * index * cols / (NY + 1))
    kk = k.reshape(1).astype(jnp.int32)

    smem = pl.BlockSpec(memory_space=pltpu.SMEM)
    vmem = pl.BlockSpec(memory_space=pltpu.VMEM)
    scratch = [
        pltpu.VMEM((EXT, 8, NY), F32),
        pltpu.VMEM((M, NY), F32),
        pltpu.VMEM((EXT, M, LANES), F32),
        pltpu.VMEM((EXT, M, NY), F32),
        pltpu.VMEM((EXT, M, NY), F32),
    ]
    parts, own = pl.pallas_call(
        own_kernel,
        name="own_trial",
        out_shape=(jax.ShapeDtypeStruct((ROWS, 3 * M, NY), BF16), jax.ShapeDtypeStruct((M, 2 * M), F32)),
        in_specs=[smem, vmem, vmem, vmem],
        out_specs=(vmem, vmem),
        scratch_shapes=scratch,
        compiler_params=pltpu.CompilerParams(vmem_limit_bytes=24 * 2**20),
        cost_estimate=pl.CostEstimate(flops=2 * 2**28, bytes_accessed=2**23, transcendentals=0),
    )(kk, strip, xtab, ytab)
    sums = pl.pallas_call(
        next_kernel,
        name="next_trial",
        out_shape=jax.ShapeDtypeStruct((M, 4 * M), F32),
        in_specs=[smem, vmem, vmem, vmem, vmem, vmem],
        out_specs=vmem,
        scratch_shapes=scratch,
        compiler_params=pltpu.CompilerParams(vmem_limit_bytes=24 * 2**20),
        cost_estimate=pl.CostEstimate(flops=2 * 2**28, bytes_accessed=2**23, transcendentals=0),
    )(kk, following, xtab, ytab, parts, own)
    sums = add_over_strips(sums)
    keep = (slab < 3).reshape(1).astype(jnp.int32)
    modes, projected, correlations = pl.pallas_call(
        finish_kernel,
        name="finish",
        out_shape=(
            jax.ShapeDtypeStruct((M, ROWS, NY), F32),
            jax.ShapeDtypeStruct((M, M), F32),
            jax.ShapeDtypeStruct((M, M), F32),
        ),
        in_specs=[smem, vmem, vmem],
        out_specs=(pl.BlockSpec(memory_space=pl.ANY), vmem, vmem),
        scratch_shapes=[pltpu.VMEM((M, ROWS, NY), F32), pltpu.SemaphoreType.DMA((4,))],
        compiler_params=pltpu.CompilerParams(vmem_limit_bytes=24 * 2**20),
        cost_estimate=pl.CostEstimate(flops=2 * 2**26, bytes_accessed=2**23, transcendentals=0),
    )(keep, sums, parts)
    return modes[None], projected[None], correlations[None]


def solution(mesh):
    return jax.shard_map(
        local,
        mesh=mesh,
        in_specs=(P("slab", "xs", None), P("slab", None, None)),
        out_specs=(P("slab", None, "xs", None), P("slab", None, None), P("slab", None, None)),
        check_vma=False,
    )
```

time: 1380 us -> 75.2 us (0.05)
  the two profiles are of different devices: /device:TPU:132 before, /device:TPU:64 now
where the time goes in v1:
time: 75.2 us; the launch traced here: 74.9 us
  Pallas kernels  32.6 us (43%)
  starting transfers between devices  23.1 us (31%)
  waiting for transfers between devices  15.7 us (21%)
  local copies, waits for them, and re-layouts  1.55 us (2%)
  other arithmetic  1.2 us (2%)
    ppermute x8, waiting for transfers between devices, others(): lax.ppermute(x, 'xs', [(i, i ^ mask) for i in range(64)])  15.2 us
    pallas_call x1, Pallas kernels, local(): pl.pallas_call(own_kernel, name='own_trial', out_shape=(jax.ShapeDtypeStr...  15.1 us
    ppermute x8, starting transfers between devices, others(): lax.ppermute(x, 'xs', [(i, i ^ mask) for i in range(64)])  12.6 us
    pallas_call x1, Pallas kernels, local(): pl.pallas_call(next_kernel, name='next_trial', out_shape=jax.ShapeDtypeSt...  12.1 us
    ppermute x1, starting transfers between devices, local(): lax.ppermute(pert[:HALO], 'xs', [(i + 1, i) for i in range(strips - 1)])  5.75 us
    pallas_call x1, Pallas kernels, local(): pl.pallas_call(finish_kernel, name='finish', out_shape=(jax.ShapeDtypeStr...  5.47 us
    ppermute x1, starting transfers between devices, local(): lax.ppermute(strip, 'slab', [((i + 1) % 4, i) for i in range(4)])  2.84 us
    ppermute x1, starting transfers between devices, local(): lax.ppermute(pert[ROWS - HALO:], 'xs', [(i, i + 1) for i in range(strips...  1.91 us
  transfers between devices with their start and end apart: 11, of which 7 were waited for; matrix products, arithmetic and copies ran while one was open for 1% of the time, Pallas kernels for 20%

profile of v1, /device:TPU:64, one launch (start us, length us, event | category | flops | bytes accessed | tf_op | source)
XLA Modules:
  0.0 74.9 jit_solution(8632753921167751879)
XLA Ops:
  0.6 0.8 %slice_bitcast_fusion.1 = (s32[4,1024]{1,0:T(4,128)S(1)}, s32[4,1024]{1,0:T(4,128)S(1)}) fusion(s32[1,16,1024]{2,1,0:T(8,128)} %param.2), kind=kLoop, calls=%fused_computation.5 | loop fusion | bytes 65536 | tf_op jit(solution)/shard_map/slice | solution.py:207
  1.4 1.9 %collective-permute-start = (s32[4,1024]{1,0:T(4,128)S(1)}, s32[4,1024]{1,0:T(4,128)S(1)}, u32[]{:S(2)}, u32[]{:S(2)}) collective-permute-start(s32[4,1024]{1,0:T(4,128)S(1)} %get-tuple-element.13), channel_id=1, source_target_pairs={{0,1},{1,2},{2,3},{3,4},{4,5},{5,6},{6,7},{7,8},{8,9},{9,10},{10,1... | collective-permute-start | bytes 49160 | tf_op jit(solution)/shard_map/ppermute | solution.py:207
  3.3 5.8 %collective-permute-start.1 = (s32[4,1024]{1,0:T(4,128)S(1)}, s32[4,1024]{1,0:T(4,128)S(1)}, u32[]{:S(2)}, u32[]{:S(2)}) collective-permute-start(s32[4,1024]{1,0:T(4,128)S(1)} %get-tuple-element.14), channel_id=1, source_target_pairs={{1,0},{2,1},{3,2},{4,3},{5,4},{6,5},{7,6},{8,7},{9,8},{10,9},{11,1... | collective-permute-start | bytes 49160 | tf_op jit(solution)/shard_map/ppermute | solution.py:208
  9.1 0.2 multiply_sine_fusion.ytab_ref
  9.3 0.8 %reshape.38 = s32[1,64]{1,0:T(1,128)S(1)} reshape(s32[2,32]{1,0:T(2,128)} %bitcast.17) | data formatting | bytes 512 | tf_op jit(solution)/shard_map/reshape | solution.py:209
  10.1 0.0 collective-permute-done
  10.1 0.4 collective-permute-done.1
  10.5 0.9 %pad_add_fusion.strip_ref = s32[32,1024]{1,0:T(8,128)S(1)} fusion(s32[1,64]{1,0:T(1,128)S(1)} %reshape.38, s32[4,1024]{1,0:T(4,128)S(1)} %collective-permute-done.1, s32[16,1024]{1,0:T(8,128)} %bitcast.13, s32[4,1024]{1,0:T(4,128)S(1)} %collective-permute-done), kind=kLoop, calls=%fused_computation | loop fusion | flops 98304 | bytes 229632 | tf_op jit(solution)/shard_map/concatenate | solution.py:210
  11.4 2.8 %collective-permute-start.2 = (s32[32,1024]{1,0:T(8,128)S(1)}, s32[32,1024]{1,0:T(8,128)S(1)}, u32[]{:S(2)}, u32[]{:S(2)}) collective-permute-start(s32[32,1024]{1,0:T(8,128)S(1)} %pad_add_fusion.strip_ref), channel_id=1, source_target_pairs={{64,0},{128,64},{192,128},{0,192},{65,1},{129,65},{193,129},{1,193... | collective-permute-start | bytes 393224 | tf_op jit(solution)/shard_map/ppermute | solution.py:211
  14.2 0.1 sine_multiply_fusion.xtab_ref
  14.3 15.1 %own_trial.1 = (bf16[16,96,1024]{2,1,0:T(8,128)(2,1)S(1)}, f32[32,64]{1,0:T(8,128)S(1)}) custom-call(s32[1]{0:T(128)} %bitcast.1.k_ref, s32[32,1024]{1,0:T(8,128)S(1)} %pad_add_fusion.strip_ref, f32[8,128]{1,0:T(8,128)S(1)} %sine_multiply_fusion.xtab_ref, f32[8,1024]{1,0:T(8,128)S(1)} %multiply_sine_fusion.ytab_ref), custom_call_target="tpu_custom_call" | custom-call | flops 536870912 | bytes 8388608 | tf_op jit(solution)/shard_map/own_trial/pallas_call | solution.py:230
  29.4 0.0 collective-permute-done.2.strip_ref
  29.4 12.1 %next_trial.1 = f32[32,128]{1,0:T(8,128)S(1)} custom-call(s32[1]{0:T(128)} %bitcast.1.k_ref, s32[32,1024]{1,0:T(8,128)S(1)} %collective-permute-done.2.strip_ref, f32[8,128]{1,0:T(8,128)S(1)} %sine_multiply_fusion.xtab_ref, f32[8,1024]{1,0:T(8,128)S(1)} %multiply_sine_fusion.ytab_ref, bf16[16,96,1024]{2,1,0:T(8,128)(2,1)S(1)} %get-tuple-element.8.parts_ref, ...), custom_call_target="tpu_custom_call" | custom-call | flops 536870912 | bytes 8388608 | tf_op jit(solution)/shard_map/next_trial/pallas_call | solution.py:240
  41.5 0.1 collective-permute-start.3
  41.6 1.2 %collective-permute-done.3 = f32[32,128]{1,0:T(8,128)S(1)} collective-permute-done((f32[32,128]{1,0:T(8,128)S(1)}, f32[32,128]{1,0:T(8,128)S(1)}, u32[]{:S(2)}, u32[]{:S(2)}) %collective-permute-start.3) | collective-permute-done | bytes 16416 | tf_op jit(solution)/shard_map/ppermute | solution.py:193
  42.8 4.1 %collective-permute-start.6 = (f32[32,128]{1,0:T(8,128)S(1)}, f32[32,128]{1,0:T(8,128)S(1)}, u32[]{:S(2)}, u32[]{:S(2)}) collective-permute-start(f32[32,128]{1,0:T(8,128)S(1)} %add.79), channel_id=1, source_target_pairs={{0,6},{1,7},{2,4},{3,5},{4,2},{5,3},{6,0},{7,1},{8,14},{9,15},{10,... | collective-permute-start | bytes 49160 | tf_op jit(solution)/shard_map/ppermute | solution.py:193
  46.8 0.0 collective-permute-start.5
  46.8 0.9 %collective-permute-start.4 = (f32[32,128]{1,0:T(8,128)S(1)}, f32[32,128]{1,0:T(8,128)S(1)}, u32[]{:S(2)}, u32[]{:S(2)}) collective-permute-start(f32[32,128]{1,0:T(8,128)S(1)} %add.79), channel_id=1, source_target_pairs={{0,2},{1,3},{2,0},{3,1},{4,6},{5,7},{6,4},{7,5},{8,10},{9,11},{10,... | collective-permute-start | bytes 49160 | tf_op jit(solution)/shard_map/ppermute | solution.py:193
  47.8 0.8 %collective-permute-done.6 = f32[32,128]{1,0:T(8,128)S(1)} collective-permute-done((f32[32,128]{1,0:T(8,128)S(1)}, f32[32,128]{1,0:T(8,128)S(1)}, u32[]{:S(2)}, u32[]{:S(2)}) %collective-permute-start.6) | collective-permute-done | bytes 16416 | tf_op jit(solution)/shard_map/ppermute | solution.py:193
  48.5 3.5 %collective-permute-done.5 = f32[32,128]{1,0:T(8,128)S(1)} collective-permute-done((f32[32,128]{1,0:T(8,128)S(1)}, f32[32,128]{1,0:T(8,128)S(1)}, u32[]{:S(2)}, u32[]{:S(2)}) %collective-permute-start.5) | collective-permute-done | bytes 16416 | tf_op jit(solution)/shard_map/ppermute | solution.py:193
  52.1 0.0 collective-permute-done.4
  52.1 0.2 collective-permute-start.9
  52.3 6.6 %collective-permute-start.8 = (f32[32,128]{1,0:T(8,128)S(1)}, f32[32,128]{1,0:T(8,128)S(1)}, u32[]{:S(2)}, u32[]{:S(2)}) collective-permute-start(f32[32,128]{1,0:T(8,128)S(1)} %add_add_fusion.1), channel_id=1, source_target_pairs={{0,16},{1,17},{2,18},{3,19},{4,20},{5,21},{6,22},{7,23},{8,24},{9,... | collective-permute-start | bytes 49160 | tf_op jit(solution)/shard_map/ppermute | solution.py:193
  58.9 0.0 collective-permute-start.7
  58.9 0.0 collective-permute-done.9
  58.9 1.9 %collective-permute-done.8 = f32[32,128]{1,0:T(8,128)S(1)} collective-permute-done((f32[32,128]{1,0:T(8,128)S(1)}, f32[32,128]{1,0:T(8,128)S(1)}, u32[]{:S(2)}, u32[]{:S(2)}) %collective-permute-start.8) | collective-permute-done | bytes 16416 | tf_op jit(solution)/shard_map/ppermute | solution.py:193
  60.7 1.9 %collective-permute-done.7 = f32[32,128]{1,0:T(8,128)S(1)} collective-permute-done((f32[32,128]{1,0:T(8,128)S(1)}, f32[32,128]{1,0:T(8,128)S(1)}, u32[]{:S(2)}, u32[]{:S(2)}) %collective-permute-start.7) | collective-permute-done | bytes 16416 | tf_op jit(solution)/shard_map/ppermute | solution.py:193
  62.6 0.8 %collective-permute-start.10 = (f32[32,128]{1,0:T(8,128)S(1)}, f32[32,128]{1,0:T(8,128)S(1)}, u32[]{:S(2)}, u32[]{:S(2)}) collective-permute-start(f32[32,128]{1,0:T(8,128)S(1)} %add_add_fusion), channel_id=1, source_target_pairs={{0,56},{1,57},{2,58},{3,59},{4,60},{5,61},{6,62},{7,63},{8,48},{9,... | collective-permute-start | bytes 49160 | tf_op jit(solution)/shard_map/ppermute | solution.py:193
  63.4 6.0 %collective-permute-done.10 = f32[32,128]{1,0:T(8,128)S(1)} collective-permute-done((f32[32,128]{1,0:T(8,128)S(1)}, f32[32,128]{1,0:T(8,128)S(1)}, u32[]{:S(2)}, u32[]{:S(2)}) %collective-permute-start.10) | collective-permute-done | bytes 16416 | tf_op jit(solution)/shard_map/ppermute | solution.py:193
  69.4 5.5 %finish.1 = (f32[32,16,1024]{2,1,0:T(8,128)}, f32[32,32]{1,0:T(8,128)}, f32[32,32]{1,0:T(8,128)}) custom-call(s32[1]{0:T(128)} %bitcast.keep_ref, f32[32,128]{1,0:T(8,128)S(1)} %add.86.sums_ref, bf16[16,96,1024]{2,1,0:T(8,128)(2,1)S(1)} %get-tuple-element.8.parts_ref), custom_call_target="tpu_custom_call" | custom-call | flops 134217728 | bytes 8388608 | tf_op jit(solution)/shard_map/finish/pallas_call | solution.py:252
  (7 shorter events, 0.0 us)
Async XLA Ops:
  1.4 8.7 %collective-permute-start = (s32[4,1024]{1,0:T(4,128)S(1)}, s32[4,1024]{1,0:T(4,128)S(1)}, u32[]{:S(2)}, u32[]{:S(2)}) collective-permute-start(s32[4,1024]{1,0:T(4,128)S(1)} %get-tuple-element.13), channel_id=1, source_target_pairs={{0,1},{1,2},{2,3},{3,4},{4,5},{5,6},{6,7},{7,8},{8,9},{9,10},{10,1... | collective-permute-start | bytes 49160 | tf_op jit(solution)/shard_map/ppermute | solution.py:207
  3.3 7.2 %collective-permute-start.1 = (s32[4,1024]{1,0:T(4,128)S(1)}, s32[4,1024]{1,0:T(4,128)S(1)}, u32[]{:S(2)}, u32[]{:S(2)}) collective-permute-start(s32[4,1024]{1,0:T(4,128)S(1)} %get-tuple-element.14), channel_id=1, source_target_pairs={{1,0},{2,1},{3,2},{4,3},{5,4},{6,5},{7,6},{8,7},{9,8},{10,9},{11,1... | collective-permute-start | bytes 49160 | tf_op jit(solution)/shard_map/ppermute | solution.py:208
  11.4 18.0 %collective-permute-start.2 = (s32[32,1024]{1,0:T(8,128)S(1)}, s32[32,1024]{1,0:T(8,128)S(1)}, u32[]{:S(2)}, u32[]{:S(2)}) collective-permute-start(s32[32,1024]{1,0:T(8,128)S(1)} %pad_add_fusion.strip_ref), channel_id=1, source_target_pairs={{64,0},{128,64},{192,128},{0,192},{65,1},{129,65},{193,129},{1,193... | collective-permute-start | bytes 393224 | tf_op jit(solution)/shard_map/ppermute | solution.py:211
  41.5 1.3 %collective-permute-start.3 = (f32[32,128]{1,0:T(8,128)S(1)}, f32[32,128]{1,0:T(8,128)S(1)}, u32[]{:S(2)}, u32[]{:S(2)}) collective-permute-start(f32[32,128]{1,0:T(8,128)S(1)} %next_trial.1), channel_id=1, source_target_pairs={{0,1},{1,0},{2,3},{3,2},{4,5},{5,4},{6,7},{7,6},{8,9},{9,8},{10,11... | collective-permute-start | bytes 49160 | tf_op jit(solution)/shard_map/ppermute | solution.py:193
  42.8 5.8 %collective-permute-start.6 = (f32[32,128]{1,0:T(8,128)S(1)}, f32[32,128]{1,0:T(8,128)S(1)}, u32[]{:S(2)}, u32[]{:S(2)}) collective-permute-start(f32[32,128]{1,0:T(8,128)S(1)} %add.79), channel_id=1, source_target_pairs={{0,6},{1,7},{2,4},{3,5},{4,2},{5,3},{6,0},{7,1},{8,14},{9,15},{10,... | collective-permute-start | bytes 49160 | tf_op jit(solution)/shard_map/ppermute | solution.py:193
  46.8 5.2 %collective-permute-start.5 = (f32[32,128]{1,0:T(8,128)S(1)}, f32[32,128]{1,0:T(8,128)S(1)}, u32[]{:S(2)}, u32[]{:S(2)}) collective-permute-start(f32[32,128]{1,0:T(8,128)S(1)} %add.79), channel_id=1, source_target_pairs={{0,4},{1,5},{2,6},{3,7},{4,0},{5,1},{6,2},{7,3},{8,12},{9,13},{10,... | collective-permute-start | bytes 49160 | tf_op jit(solution)/shard_map/ppermute | solution.py:193
  46.8 5.2 %collective-permute-start.4 = (f32[32,128]{1,0:T(8,128)S(1)}, f32[32,128]{1,0:T(8,128)S(1)}, u32[]{:S(2)}, u32[]{:S(2)}) collective-permute-start(f32[32,128]{1,0:T(8,128)S(1)} %add.79), channel_id=1, source_target_pairs={{0,2},{1,3},{2,0},{3,1},{4,6},{5,7},{6,4},{7,5},{8,10},{9,11},{10,... | collective-permute-start | bytes 49160 | tf_op jit(solution)/shard_map/ppermute | solution.py:193
  52.1 6.8 %collective-permute-start.9 = (f32[32,128]{1,0:T(8,128)S(1)}, f32[32,128]{1,0:T(8,128)S(1)}, u32[]{:S(2)}, u32[]{:S(2)}) collective-permute-start(f32[32,128]{1,0:T(8,128)S(1)} %add_add_fusion.1), channel_id=1, source_target_pairs={{0,24},{1,25},{2,26},{3,27},{4,28},{5,29},{6,30},{7,31},{8,16},{9,... | collective-permute-start | bytes 49160 | tf_op jit(solution)/shard_map/ppermute | solution.py:193
  52.3 8.5 %collective-permute-start.8 = (f32[32,128]{1,0:T(8,128)S(1)}, f32[32,128]{1,0:T(8,128)S(1)}, u32[]{:S(2)}, u32[]{:S(2)}) collective-permute-start(f32[32,128]{1,0:T(8,128)S(1)} %add_add_fusion.1), channel_id=1, source_target_pairs={{0,16},{1,17},{2,18},{3,19},{4,20},{5,21},{6,22},{7,23},{8,24},{9,... | collective-permute-start | bytes 49160 | tf_op jit(solution)/shard_map/ppermute | solution.py:193
  58.9 3.7 %collective-permute-start.7 = (f32[32,128]{1,0:T(8,128)S(1)}, f32[32,128]{1,0:T(8,128)S(1)}, u32[]{:S(2)}, u32[]{:S(2)}) collective-permute-start(f32[32,128]{1,0:T(8,128)S(1)} %add_add_fusion.1), channel_id=1, source_target_pairs={{0,8},{1,9},{2,10},{3,11},{4,12},{5,13},{6,14},{7,15},{8,0},{9,1},... | collective-permute-start | bytes 49160 | tf_op jit(solution)/shard_map/ppermute | solution.py:193
  62.6 6.8 %collective-permute-start.10 = (f32[32,128]{1,0:T(8,128)S(1)}, f32[32,128]{1,0:T(8,128)S(1)}, u32[]{:S(2)}, u32[]{:S(2)}) collective-permute-start(f32[32,128]{1,0:T(8,128)S(1)} %add_add_fusion), channel_id=1, source_target_pairs={{0,56},{1,57},{2,58},{3,59},{4,60},{5,61},{6,62},{7,63},{8,48},{9,... | collective-permute-start | bytes 49160 | tf_op jit(solution)/shard_map/ppermute | solution.py:193

commit v2 on v0

v2 whole, which is shorter than its diff:
```python
import functools
import math

import jax
import jax.numpy as jnp
from jax import lax
from jax.experimental import pallas as pl
from jax.experimental.pallas import tpu as pltpu
from jax.sharding import PartitionSpec as P

NX = 1024
NY = 1024
M = 32
ROWS = 16
HALO = 4
EXT = ROWS + 2 * HALO
LANES = 128
GROUPS = LANES // M
SPAN = NY // GROUPS
STEPS = SPAN // 8
F32 = jnp.float32
BF16 = jnp.bfloat16


def split(x):
    high = x.astype(BF16)
    return high, (x - high.astype(F32)).astype(BF16)


def iota(shape, axis):
    return lax.broadcasted_iota(jnp.int32, shape, axis)


def assemble_kernel(k_ref, inner_ref, outer_ref, pert_ref, seeds_ref, strip_ref):
    even = k_ref[0] % 2 == 0
    before = jnp.where(even, outer_ref[ROWS - HALO :, :], inner_ref[ROWS - HALO :, :])
    after = jnp.where(even, inner_ref[:HALO, :], outer_ref[:HALO, :])
    strip_ref[0:HALO, :] = before
    strip_ref[HALO : HALO + ROWS, :] = pert_ref[...]
    strip_ref[HALO + ROWS : EXT, :] = after
    strip_ref[EXT : EXT + 2, 0:LANES] = jnp.concatenate([seeds_ref[...]] * GROUPS, axis=1)


def first_trial(k, strip_ref, w_ref, pert_ref, out_ref):
    unit = math.pi / (NX + 1)
    first = strip_ref[EXT : EXT + 1, 0:LANES].astype(F32)
    second = strip_ref[EXT + 1 : EXT + 2, 0:LANES].astype(F32)
    shift = 2.0 * jnp.cos(unit * first) + 2.0 * jnp.cos(unit * second)

    group, s = iota((8, LANES), 1) // M, iota((8, LANES), 0)
    base = (group * SPAN + s * STEPS).astype(F32)
    scale = 2.0 / math.sqrt((NX + 1) * (NY + 1))
    angle = unit * second * (base + 1.0)
    sin_base, cos_base = scale * jnp.sin(angle), scale * jnp.cos(angle)
    step = unit * second * iota((STEPS, LANES), 0).astype(F32)
    sin_step, cos_step = jnp.sin(step), jnp.cos(step)
    row = iota((EXT, LANES), 0) + (k * ROWS - HALO)
    along_x = jnp.sin(unit * first * (row.astype(F32) + 1.0))
    along_x = jnp.where((row >= 0) & (row < NX), along_x, 0.0)
    xpos = (row.astype(F32) + 0.5) / NX - 0.5
    x_part = 9.0 - 4.0 * (xpos * xpos + 0.5 * xpos)

    pert = strip_ref[0:EXT, :].astype(F32)
    stacked = [pert[:, g * SPAN : (g + 1) * SPAN] for g in range(GROUPS)]
    stacked = jnp.concatenate(stacked + [jnp.zeros((LANES - GROUPS * EXT, SPAN), F32)], axis=0)
    pert_ref[...] = jnp.transpose(stacked)
    spread = jnp.concatenate([pert_ref[pl.ds(q, 8, stride=STEPS), :] for q in range(STEPS)], axis=0).astype(BF16)
    source = iota((LANES, LANES), 0) - EXT * (iota((LANES, LANES), 1) // M)

    sines, y_parts = [], []
    for q in range(STEPS):
        sines.append(sin_base * cos_step[q : q + 1] + cos_base * sin_step[q : q + 1])
        ypos = (base + (q + 0.5)) / NY - 0.5
        y_parts.append(2.4 * ypos * ypos)
    for r in range(EXT):
        here = jnp.dot(spread, (source == r).astype(BF16), preferred_element_type=F32)
        x_row = jnp.broadcast_to(x_part[r : r + 1], (8, LANES))
        sine_row = jnp.broadcast_to(along_x[r : r + 1], (8, LANES))
        for q in range(STEPS):
            w = (x_row - y_parts[q]) - 0.1 * here[8 * q : 8 * q + 8]
            w_ref[r, q] = w
            out_ref[r, q] = (w + shift) * (sine_row * sines[q])


def beyond(row_first, row_last):
    s, lane = iota((8, LANES), 0), iota((8, LANES), 1)
    down = pltpu.roll(row_last, 1, 0)
    left = jnp.where(s == 0, jnp.where(lane < M, 0.0, pltpu.roll(down, M, 1)), down)
    up = pltpu.roll(row_first, 7, 0)
    right = jnp.where(s == 7, jnp.where(lane >= LANES - M, 0.0, pltpu.roll(up, LANES - M, 1)), up)
    return left, right


def sweep(k, first_row, count, in_ref, w_ref, out_ref, shifted=0, hamiltonian=False):
    batch, chunk = count // 2, 4

    def rows(i, carry):
        r = first_row + i * batch
        ends = [beyond(in_ref[r + j, 0], in_ref[r + j, STEPS - 1]) for j in range(batch)]
        factor = {}
        top, bottom = HALO - 1 - first_row, EXT - HALO - first_row - batch
        if 0 <= top < batch:
            factor[top] = jnp.where((i == 0) & (k == 0), 0.0, 1.0)
        if 0 <= bottom < batch:
            factor[bottom] = jnp.where((i == 1) & (k == NX // ROWS - 1), 0.0, 1.0) * factor.get(bottom, 1.0)
        for q0 in range(0, STEPS, chunk):
            inside = range(q0, q0 + chunk)
            x = {(j, q): in_ref[r + j, q] for j in range(-1, batch + 1) for q in inside}
            for j in range(batch):
                x[j, q0 - 1] = in_ref[r + j, q0 - 1] if q0 > 0 else ends[j][0]
                x[j, q0 + chunk] = in_ref[r + j, q0 + chunk] if q0 + chunk < STEPS else ends[j][1]
            for j in range(batch):
                for q in inside:
                    near = (x[j, q - 1] + x[j, q + 1]) + (x[j - 1, q] + x[j + 1, q])
                    if hamiltonian:
                        value = (13.0 - w_ref[r + j, q]) * x[j, q] - near
                    else:
                        value = w_ref[r + j, q] * x[j, q] + near
                    if j in factor:
                        value = value * factor[j]
                    out_ref[r + j - shifted, q] = value
        return carry

    lax.fori_loop(0, 2, rows, 0)


def blocks(product):
    return sum(product[M * g : M * g + M, M * g : M * g + M] for g in range(GROUPS))


def dot_cells(a, b):
    return lax.dot_general(a, b, (((0,), (0,)), ((), ())), preferred_element_type=F32)


def own_kernel(k_ref, strip_ref, modes_ref, sums_ref, w_ref, pert_ref, one_ref, two_ref):
    k = k_ref[0]
    first_trial(k, strip_ref, w_ref, pert_ref, one_ref)
    sweep(k, 1, EXT - 2, one_ref, w_ref, two_ref)
    sweep(k, 2, EXT - 4, two_ref, w_ref, one_ref)
    sweep(k, 3, EXT - 6, one_ref, w_ref, two_ref)
    sweep(k, 4, ROWS, two_ref, w_ref, one_ref, hamiltonian=True)
    field = two_ref[HALO : HALO + ROWS].reshape(ROWS * SPAN, LANES)
    image = one_ref[HALO : HALO + ROWS].reshape(ROWS * SPAN, LANES)
    modes_ref[...] = field
    high, low = split(field)
    image_high, image_low = split(image)
    main = dot_cells(high, jnp.concatenate([high, low, image_high, image_low], axis=1))
    rest = blocks(dot_cells(low, image_high))
    cross = blocks(main[:, LANES : 2 * LANES])
    gram = blocks(main[:, 0:LANES]) + (cross + cross.T)
    ham = blocks(main[:, 2 * LANES : 3 * LANES]) + (blocks(main[:, 3 * LANES :]) + rest)
    sums_ref[...] = jnp.concatenate([gram, ham], axis=1)


def next_kernel(k_ref, strip_ref, modes_ref, own_ref, sums_ref, w_ref, pert_ref, one_ref, two_ref):
    k = k_ref[0]
    first_trial(k, strip_ref, w_ref, pert_ref, one_ref)
    sweep(k, 2, EXT - 4, one_ref, w_ref, two_ref)
    sweep(k, 3, EXT - 6, two_ref, w_ref, one_ref)
    sweep(k, 4, ROWS, one_ref, w_ref, two_ref)
    field = two_ref[HALO : HALO + ROWS].reshape(ROWS * SPAN, LANES)
    high, low = split(field)
    own_high, own_low = split(modes_ref[...])
    main = dot_cells(jnp.concatenate([high, own_high], axis=1), jnp.concatenate([high, low], axis=1))
    rest = blocks(dot_cells(own_low, high))
    cross = blocks(main[0:LANES, LANES:])
    gram = blocks(main[0:LANES, 0:LANES]) + (cross + cross.T)
    across = blocks(main[LANES:, 0:LANES]) + (blocks(main[LANES:, LANES:]) + rest)
    sums_ref[...] = jnp.concatenate([own_ref[...], gram, across], axis=1)


def parts_kernel(modes_ref, parts_ref):
    def rows(i, carry):
        for j in range(4):
            r = i * 4 + j
            pieces = [
                modes_ref[pl.ds(r * SPAN + q * 8 + s, 8, stride=8), :] for s in range(8) for q in range(0, STEPS, 8)
            ]
            parts_ref[r] = jnp.concatenate(split(jnp.concatenate(pieces, axis=0)), axis=1)
        return carry

    lax.fori_loop(0, ROWS // 4, rows, 0)


def finish_kernel(keep_ref, sums_ref, parts_ref, modes_ref, proj_ref, corr_ref, held_ref, sem):
    sums = sums_ref[...]
    row, lane = iota((M, LANES), 0), iota((M, LANES), 1)
    work = jnp.where((lane // M) % 2 == 0, sums, (lane % M == row).astype(F32))
    pivots = jnp.ones((M, LANES), F32)
    for j in range(M):
        column = jnp.where(lane < 2 * M, work[:, j : j + 1], work[:, 2 * M + j : 2 * M + j + 1])
        pivots = jnp.where(row == j, column, pivots)
        scaled = work[j : j + 1, :] / column[j : j + 1, :]
        work = work - jnp.where(row > j, column, 0.0) * scaled
    inverse = work / jnp.sqrt(pivots)
    own, following = inverse[:, M : 2 * M], inverse[:, 3 * M : 4 * M]
    wide = jnp.concatenate([own * math.sqrt(NX * NY)] * GROUPS, axis=1)
    wide = jnp.concatenate([jnp.where(lane // M == g, wide, 0.0) for g in range(GROUPS)], axis=0)
    high, low = split(wide)
    twice = jnp.concatenate([high, high], axis=1)

    def times(a, b):
        return lax.dot_general(a, b, (((1,), (1,)), ((), ())), preferred_element_type=F32)

    copies = []
    for half in range(2):
        for r in range(8 * half, 8 * half + 8):
            part = parts_ref[r]
            result = times(twice, part) + times(low, part[:, 0:LANES])
            for g in range(GROUPS):
                held_ref[:, r, g * SPAN : (g + 1) * SPAN] = result[M * g : M * g + M]
        rows = slice(8 * half, 8 * half + 8)
        copy = pltpu.make_async_copy(held_ref.at[:, rows], modes_ref.at[:, rows], sem.at[half])
        copy.start()
        copies.append(copy)

    exact = functools.partial(jnp.dot, precision=lax.Precision.HIGHEST, preferred_element_type=F32)
    image, across = sums[:, M : 2 * M], sums[:, 3 * M : 4 * M]
    proj_ref[...] = exact(exact(own, image), own.T)
    corr_ref[...] = jnp.where(keep_ref[0] > 0, exact(exact(own, across), following.T), 0.0)
    for copy in copies:
        copy.wait()


def add_over_strips(v):
    def others(x, *masks):
        return [lax.ppermute(x, "xs", [(i, i ^ mask) for i in range(64)]) for mask in masks]

    v = v + others(v, 1)[0]
    for unit in (2, 8):
        one, two, three = others(v, unit, 2 * unit, 3 * unit)
        v = (v + one) + (two + three)
    return v + others(v, 7 * 8)[0]


def local(perturbation, seeds):
    k = lax.axis_index("xs")
    strips = NX // ROWS
    pert = perturbation[0]
    inner = lax.ppermute(pert, "xs", [(i, i ^ 1) for i in range(strips)])
    outer = lax.ppermute(pert, "xs", [(i, i - 1 if i % 2 == 0 else i + 1) for i in range(1, strips - 1)])
    kk = k.reshape(1).astype(jnp.int32)
    keep = (lax.axis_index("slab") < 3).reshape(1).astype(jnp.int32)

    smem = pl.BlockSpec(memory_space=pltpu.SMEM)
    vmem = pl.BlockSpec(memory_space=pltpu.VMEM)
    params = pltpu.CompilerParams(vmem_limit_bytes=28 * 2**20)
    strip = pl.pallas_call(
        assemble_kernel,
        name="assemble",
        out_shape=jax.ShapeDtypeStruct((32, NY), jnp.int32),
        in_specs=[smem, vmem, vmem, vmem, vmem],
        out_specs=vmem,
        compiler_params=pltpu.CompilerParams(vmem_limit_bytes=4 * 2**20),
    )(kk, inner, outer, pert, seeds[0].T)
    following = lax.ppermute(strip, "slab", [((i + 1) % 4, i) for i in range(4)])

    scratch = [
        pltpu.VMEM((EXT, STEPS, 8, LANES), F32),
        pltpu.VMEM((SPAN, LANES), F32),
        pltpu.VMEM((EXT, STEPS, 8, LANES), F32),
        pltpu.VMEM((EXT, STEPS, 8, LANES), F32),
    ]
    cost = pl.CostEstimate(flops=2**30, bytes_accessed=2**23, transcendentals=0)
    field, own = pl.pallas_call(
        own_kernel,
        name="own_trial",
        out_shape=(jax.ShapeDtypeStruct((ROWS * SPAN, LANES), F32), jax.ShapeDtypeStruct((M, 2 * M), F32)),
        in_specs=[smem, vmem],
        out_specs=(vmem, vmem),
        scratch_shapes=scratch,
        compiler_params=params,
        cost_estimate=cost,
    )(kk, strip)
    sums = pl.pallas_call(
        next_kernel,
        name="next_trial",
        out_shape=jax.ShapeDtypeStruct((M, 4 * M), F32),
        in_specs=[smem, vmem, vmem, vmem],
        out_specs=vmem,
        scratch_shapes=scratch,
        compiler_params=params,
        cost_estimate=cost,
    )(kk, following, field, own)
    parts = pl.pallas_call(
        parts_kernel,
        name="parts",
        out_shape=jax.ShapeDtypeStruct((ROWS, SPAN, 2 * LANES), BF16),
        in_specs=[vmem],
        out_specs=vmem,
        compiler_params=pltpu.CompilerParams(vmem_limit_bytes=12 * 2**20),
        cost_estimate=pl.CostEstimate(flops=2**20, bytes_accessed=2**22, transcendentals=0),
    )(field)
    sums = add_over_strips(sums)
    modes, projected, correlations = pl.pallas_call(
        finish_kernel,
        name="finish",
        out_shape=(
            jax.ShapeDtypeStruct((M, ROWS, NY), F32),
            jax.ShapeDtypeStruct((M, M), F32),
            jax.ShapeDtypeStruct((M, M), F32),
        ),
        in_specs=[smem, vmem, vmem],
        out_specs=(pl.BlockSpec(memory_space=pl.ANY), vmem, vmem),
        scratch_shapes=[pltpu.VMEM((M, ROWS, NY), F32), pltpu.SemaphoreType.DMA((2,))],
        compiler_params=params,
        cost_estimate=pl.CostEstimate(flops=2**28, bytes_accessed=2**23, transcendentals=0),
    )(keep, sums, parts)
    return modes[None], projected[None], correlations[None]


def solution(mesh):
    return jax.shard_map(
        local,
        mesh=mesh,
        in_specs=(P("slab", "xs", None), P("slab", None, None)),
        out_specs=(P("slab", None, "xs", None), P("slab", None, None), P("slab", None, None)),
        check_vma=False,
    )
```

time: 1380 us -> 52 us (0.04)
  the two profiles are of different devices: /device:TPU:132 before, /device:TPU:64 now
where the time goes in v2:
time: 52 us; the launch traced here: 51.9 us
  starting transfers between devices  19.5 us (38%)
  waiting for transfers between devices  15.7 us (30%)
  Pallas kernels  14.4 us (28%)
  local copies, waits for them, and re-layouts  1.52 us (3%)
  between operations  0.71 us (1%)
    ppermute x8, starting transfers between devices, others(): lax.ppermute(x, 'xs', [(i, i ^ mask) for i in range(64)])  12.7 us
    ppermute x8, waiting for transfers between devices, others(): lax.ppermute(x, 'xs', [(i, i ^ mask) for i in range(64)])  11.8 us
    pallas_call x1, Pallas kernels, local(): pl.pallas_call(finish_kernel, name='finish', out_shape=(jax.ShapeDtypeStr...  5.86 us
    pallas_call x1, Pallas kernels, local(): pl.pallas_call(own_kernel, name='own_trial', out_shape=(jax.ShapeDtypeStr...  4.38 us
    ppermute x1, starting transfers between devices, local(): lax.ppermute(pert, 'xs', [(i, i - 1 if i % 2 == 0 else i + 1) for i in ra...  3.91 us
    ppermute x1, waiting for transfers between devices, local(): lax.ppermute(pert, 'xs', [(i, i - 1 if i % 2 == 0 else i + 1) for i in ra...  3.88 us
    pallas_call x1, Pallas kernels, local(): pl.pallas_call(next_kernel, name='next_trial', out_shape=jax.ShapeDtypeSt...  3.77 us
    ppermute x1, starting transfers between devices, local(): lax.ppermute(strip, 'slab', [((i + 1) % 4, i) for i in range(4)])  2.79 us
  transfers between devices with their start and end apart: 11, of which 7 were waited for; matrix products, arithmetic and copies ran while one was open for 0% of the time, Pallas kernels for 9%

profile of v2, /device:TPU:64, one launch (start us, length us, event | category | flops | bytes accessed | tf_op | source)
XLA Modules:
  0.0 51.9 jit_solution(5591686180645907359)
XLA Ops:
  0.6 3.9 %collective-permute-start.1 = (s32[16,1024]{1,0:T(8,128)}, s32[16,1024]{1,0:T(8,128)S(1)}, u32[]{:S(2)}, u32[]{:S(2)}) collective-permute-start(s32[16,1024]{1,0:T(8,128)} %bitcast.9), channel_id=1, source_target_pairs={{1,2},{2,1},{3,4},{4,3},{5,6},{6,5},{7,8},{8,7},{9,10},{10,9},{11,... | collective-permute-start | bytes 196616 | tf_op jit(solution)/shard_map/ppermute | solution.py:241
  4.5 0.1 collective-permute-start
  4.6 3.9 %collective-permute-done.1.outer_ref = s32[16,1024]{1,0:T(8,128)S(1)} collective-permute-done((s32[16,1024]{1,0:T(8,128)}, s32[16,1024]{1,0:T(8,128)S(1)}, u32[]{:S(2)}, u32[]{:S(2)}) %collective-permute-start.1) | collective-permute-done | bytes 65568 | tf_op jit(solution)/shard_map/ppermute | solution.py:241
  8.5 0.0 collective-permute-done.inner_ref
  8.5 0.0 copy-start
  8.5 0.8 %copy-done = s32[1,16,1024]{2,1,0:T(8,128)S(1)} copy-done((s32[1,16,1024]{2,1,0:T(8,128)S(1)}, s32[1,16,1024]{2,1,0:T(8,128)}, u32[]{:S(2)}) %copy-start) | copy-done | bytes 65560
  9.4 0.0 copy-start.1
  9.4 0.7 %copy-done.1 = s32[1,32,2]{1,2,0:T(2,128)S(1)} copy-done((s32[1,32,2]{1,2,0:T(2,128)S(1)}, s32[1,32,2]{1,2,0:T(2,128)}, u32[]{:S(2)}) %copy-start.1) | copy-done | bytes 280
  10.1 0.1 assemble.1.strip_ref
  10.1 2.8 %collective-permute-start.2 = (s32[32,1024]{1,0:T(8,128)S(1)}, s32[32,1024]{1,0:T(8,128)S(1)}, u32[]{:S(2)}, u32[]{:S(2)}) collective-permute-start(s32[32,1024]{1,0:T(8,128)S(1)} %assemble.1.strip_ref), channel_id=1, source_target_pairs={{64,0},{128,64},{192,128},{0,192},{65,1},{129,65},{193,129},{1,193... | collective-permute-start | bytes 393224 | tf_op jit(solution)/shard_map/ppermute | solution.py:256
  12.9 4.4 %own_trial.1 = (f32[4096,128]{1,0:T(8,128)S(1)}, f32[32,64]{1,0:T(8,128)S(1)}) custom-call(s32[1]{0:T(128)} %bitcast.1.k_ref, s32[32,1024]{1,0:T(8,128)S(1)} %assemble.1.strip_ref), custom_call_target="tpu_custom_call" | custom-call | flops 1073741824 | bytes 8388608 | tf_op jit(solution)/shard_map/own_trial/pallas_call | solution.py:265
  17.3 0.0 collective-permute-done.2.strip_ref
  17.3 3.8 %next_trial.1 = f32[32,128]{1,0:T(8,128)S(1)} custom-call(s32[1]{0:T(128)} %bitcast.1.k_ref, s32[32,1024]{1,0:T(8,128)S(1)} %collective-permute-done.2.strip_ref, f32[4096,128]{1,0:T(8,128)S(1)} %get-tuple-element.8.modes_ref, f32[32,64]{1,0:T(8,128)S(1)} %get-tuple-element.9.own_ref), custom_call_target="tpu_custom_call" | custom-call | flops 1073741824 | bytes 8388608 | tf_op jit(solution)/shard_map/next_trial/pallas_call | solution.py:275
  21.1 0.1 collective-permute-start.3
  21.2 1.2 %collective-permute-done.3 = f32[32,128]{1,0:T(8,128)S(1)} collective-permute-done((f32[32,128]{1,0:T(8,128)S(1)}, f32[32,128]{1,0:T(8,128)S(1)}, u32[]{:S(2)}, u32[]{:S(2)}) %collective-permute-start.3) | collective-permute-done | bytes 16416 | tf_op jit(solution)/shard_map/ppermute | solution.py:227
  22.4 2.2 %collective-permute-start.6 = (f32[32,128]{1,0:T(8,128)S(1)}, f32[32,128]{1,0:T(8,128)S(1)}, u32[]{:S(2)}, u32[]{:S(2)}) collective-permute-start(f32[32,128]{1,0:T(8,128)S(1)} %add.24), channel_id=1, source_target_pairs={{0,6},{1,7},{2,4},{3,5},{4,2},{5,3},{6,0},{7,1},{8,14},{9,15},{10,... | collective-permute-start | bytes 49160 | tf_op jit(solution)/shard_map/ppermute | solution.py:227
  24.6 0.0 collective-permute-start.5
  24.6 1.9 %collective-permute-start.4 = (f32[32,128]{1,0:T(8,128)S(1)}, f32[32,128]{1,0:T(8,128)S(1)}, u32[]{:S(2)}, u32[]{:S(2)}) collective-permute-start(f32[32,128]{1,0:T(8,128)S(1)} %add.24), channel_id=1, source_target_pairs={{0,2},{1,3},{2,0},{3,1},{4,6},{5,7},{6,4},{7,5},{8,10},{9,11},{10,... | collective-permute-start | bytes 49160 | tf_op jit(solution)/shard_map/ppermute | solution.py:227
  26.5 0.9 %collective-permute-done.6 = f32[32,128]{1,0:T(8,128)S(1)} collective-permute-done((f32[32,128]{1,0:T(8,128)S(1)}, f32[32,128]{1,0:T(8,128)S(1)}, u32[]{:S(2)}, u32[]{:S(2)}) %collective-permute-start.6) | collective-permute-done | bytes 16416 | tf_op jit(solution)/shard_map/ppermute | solution.py:227
  27.3 2.5 %collective-permute-done.5 = f32[32,128]{1,0:T(8,128)S(1)} collective-permute-done((f32[32,128]{1,0:T(8,128)S(1)}, f32[32,128]{1,0:T(8,128)S(1)}, u32[]{:S(2)}, u32[]{:S(2)}) %collective-permute-start.5) | collective-permute-done | bytes 16416 | tf_op jit(solution)/shard_map/ppermute | solution.py:227
  29.9 0.0 collective-permute-done.4
  29.9 0.2 collective-permute-start.9
  30.1 5.4 %collective-permute-start.8 = (f32[32,128]{1,0:T(8,128)S(1)}, f32[32,128]{1,0:T(8,128)S(1)}, u32[]{:S(2)}, u32[]{:S(2)}) collective-permute-start(f32[32,128]{1,0:T(8,128)S(1)} %add_add_fusion.1), channel_id=1, source_target_pairs={{0,16},{1,17},{2,18},{3,19},{4,20},{5,21},{6,22},{7,23},{8,24},{9,... | collective-permute-start | bytes 49160 | tf_op jit(solution)/shard_map/ppermute | solution.py:227
  35.4 0.0 collective-permute-start.7
  35.4 0.0 collective-permute-done.9
  35.4 1.9 %collective-permute-done.8 = f32[32,128]{1,0:T(8,128)S(1)} collective-permute-done((f32[32,128]{1,0:T(8,128)S(1)}, f32[32,128]{1,0:T(8,128)S(1)}, u32[]{:S(2)}, u32[]{:S(2)}) %collective-permute-start.8) | collective-permute-done | bytes 16416 | tf_op jit(solution)/shard_map/ppermute | solution.py:227
  37.3 1.9 %collective-permute-done.7 = f32[32,128]{1,0:T(8,128)S(1)} collective-permute-done((f32[32,128]{1,0:T(8,128)S(1)}, f32[32,128]{1,0:T(8,128)S(1)}, u32[]{:S(2)}, u32[]{:S(2)}) %collective-permute-start.7) | collective-permute-done | bytes 16416 | tf_op jit(solution)/shard_map/ppermute | solution.py:227
  39.2 2.9 %collective-permute-start.10 = (f32[32,128]{1,0:T(8,128)S(1)}, f32[32,128]{1,0:T(8,128)S(1)}, u32[]{:S(2)}, u32[]{:S(2)}) collective-permute-start(f32[32,128]{1,0:T(8,128)S(1)} %add_add_fusion), channel_id=1, source_target_pairs={{0,56},{1,57},{2,58},{3,59},{4,60},{5,61},{6,62},{7,63},{8,48},{9,... | collective-permute-start | bytes 49160 | tf_op jit(solution)/shard_map/ppermute | solution.py:227
  42.1 0.4 parts.1.parts_ref
  42.5 3.6 %collective-permute-done.10 = f32[32,128]{1,0:T(8,128)S(1)} collective-permute-done((f32[32,128]{1,0:T(8,128)S(1)}, f32[32,128]{1,0:T(8,128)S(1)}, u32[]{:S(2)}, u32[]{:S(2)}) %collective-permute-start.10) | collective-permute-done | bytes 16416 | tf_op jit(solution)/shard_map/ppermute | solution.py:227
  46.0 5.9 %finish.1 = (f32[32,16,1024]{2,1,0:T(8,128)}, f32[32,32]{1,0:T(8,128)}, f32[32,32]{1,0:T(8,128)}) custom-call(s32[1]{0:T(128)} %bitcast.keep_ref, f32[32,128]{1,0:T(8,128)S(1)} %add.31.sums_ref, bf16[16,256,256]{2,1,0:T(8,128)(2,1)S(1)} %parts.1.parts_ref), custom_call_target="tpu_custom_call" | custom-call | flops 268435456 | bytes 8388608 | tf_op jit(solution)/shard_map/finish/pallas_call | solution.py:295
  (4 shorter events, 0.0 us)
Async XLA Ops:
  0.6 7.9 %collective-permute-start.1 = (s32[16,1024]{1,0:T(8,128)}, s32[16,1024]{1,0:T(8,128)S(1)}, u32[]{:S(2)}, u32[]{:S(2)}) collective-permute-start(s32[16,1024]{1,0:T(8,128)} %bitcast.9), channel_id=1, source_target_pairs={{1,2},{2,1},{3,4},{4,3},{5,6},{6,5},{7,8},{8,7},{9,10},{10,9},{11,... | collective-permute-start | bytes 196616 | tf_op jit(solution)/shard_map/ppermute | solution.py:241
  4.5 4.0 %collective-permute-start = (s32[16,1024]{1,0:T(8,128)}, s32[16,1024]{1,0:T(8,128)S(1)}, u32[]{:S(2)}, u32[]{:S(2)}) collective-permute-start(s32[16,1024]{1,0:T(8,128)} %bitcast.10), channel_id=1, source_target_pairs={{0,1},{1,0},{2,3},{3,2},{4,5},{5,4},{6,7},{7,6},{8,9},{9,8},{10,11... | collective-permute-start | bytes 196616 | tf_op jit(solution)/shard_map/ppermute | solution.py:240
  8.5 0.8 %copy-start = (s32[1,16,1024]{2,1,0:T(8,128)S(1)}, s32[1,16,1024]{2,1,0:T(8,128)}, u32[]{:S(2)}) copy-start(s32[1,16,1024]{2,1,0:T(8,128)} %param.2) | copy-start | bytes 196612
  9.4 0.7 %copy-start.1 = (s32[1,32,2]{1,2,0:T(2,128)S(1)}, s32[1,32,2]{1,2,0:T(2,128)}, u32[]{:S(2)}) copy-start(s32[1,32,2]{1,2,0:T(2,128)} %param.3) | copy-start | bytes 772
  10.1 7.2 %collective-permute-start.2 = (s32[32,1024]{1,0:T(8,128)S(1)}, s32[32,1024]{1,0:T(8,128)S(1)}, u32[]{:S(2)}, u32[]{:S(2)}) collective-permute-start(s32[32,1024]{1,0:T(8,128)S(1)} %assemble.1.strip_ref), channel_id=1, source_target_pairs={{64,0},{128,64},{192,128},{0,192},{65,1},{129,65},{193,129},{1,193... | collective-permute-start | bytes 393224 | tf_op jit(solution)/shard_map/ppermute | solution.py:256
  21.1 1.3 %collective-permute-start.3 = (f32[32,128]{1,0:T(8,128)S(1)}, f32[32,128]{1,0:T(8,128)S(1)}, u32[]{:S(2)}, u32[]{:S(2)}) collective-permute-start(f32[32,128]{1,0:T(8,128)S(1)} %next_trial.1), channel_id=1, source_target_pairs={{0,1},{1,0},{2,3},{3,2},{4,5},{5,4},{6,7},{7,6},{8,9},{9,8},{10,11... | collective-permute-start | bytes 49160 | tf_op jit(solution)/shard_map/ppermute | solution.py:227
  22.4 4.9 %collective-permute-start.6 = (f32[32,128]{1,0:T(8,128)S(1)}, f32[32,128]{1,0:T(8,128)S(1)}, u32[]{:S(2)}, u32[]{:S(2)}) collective-permute-start(f32[32,128]{1,0:T(8,128)S(1)} %add.24), channel_id=1, source_target_pairs={{0,6},{1,7},{2,4},{3,5},{4,2},{5,3},{6,0},{7,1},{8,14},{9,15},{10,... | collective-permute-start | bytes 49160 | tf_op jit(solution)/shard_map/ppermute | solution.py:227
  24.6 5.2 %collective-permute-start.5 = (f32[32,128]{1,0:T(8,128)S(1)}, f32[32,128]{1,0:T(8,128)S(1)}, u32[]{:S(2)}, u32[]{:S(2)}) collective-permute-start(f32[32,128]{1,0:T(8,128)S(1)} %add.24), channel_id=1, source_target_pairs={{0,4},{1,5},{2,6},{3,7},{4,0},{5,1},{6,2},{7,3},{8,12},{9,13},{10,... | collective-permute-start | bytes 49160 | tf_op jit(solution)/shard_map/ppermute | solution.py:227
  24.6 5.2 %collective-permute-start.4 = (f32[32,128]{1,0:T(8,128)S(1)}, f32[32,128]{1,0:T(8,128)S(1)}, u32[]{:S(2)}, u32[]{:S(2)}) collective-permute-start(f32[32,128]{1,0:T(8,128)S(1)} %add.24), channel_id=1, source_target_pairs={{0,2},{1,3},{2,0},{3,1},{4,6},{5,7},{6,4},{7,5},{8,10},{9,11},{10,... | collective-permute-start | bytes 49160 | tf_op jit(solution)/shard_map/ppermute | solution.py:227
  29.9 5.6 %collective-permute-start.9 = (f32[32,128]{1,0:T(8,128)S(1)}, f32[32,128]{1,0:T(8,128)S(1)}, u32[]{:S(2)}, u32[]{:S(2)}) collective-permute-start(f32[32,128]{1,0:T(8,128)S(1)} %add_add_fusion.1), channel_id=1, source_target_pairs={{0,24},{1,25},{2,26},{3,27},{4,28},{5,29},{6,30},{7,31},{8,16},{9,... | collective-permute-start | bytes 49160 | tf_op jit(solution)/shard_map/ppermute | solution.py:227
  30.1 7.3 %collective-permute-start.8 = (f32[32,128]{1,0:T(8,128)S(1)}, f32[32,128]{1,0:T(8,128)S(1)}, u32[]{:S(2)}, u32[]{:S(2)}) collective-permute-start(f32[32,128]{1,0:T(8,128)S(1)} %add_add_fusion.1), channel_id=1, source_target_pairs={{0,16},{1,17},{2,18},{3,19},{4,20},{5,21},{6,22},{7,23},{8,24},{9,... | collective-permute-start | bytes 49160 | tf_op jit(solution)/shard_map/ppermute | solution.py:227
  35.4 3.7 %collective-permute-start.7 = (f32[32,128]{1,0:T(8,128)S(1)}, f32[32,128]{1,0:T(8,128)S(1)}, u32[]{:S(2)}, u32[]{:S(2)}) collective-permute-start(f32[32,128]{1,0:T(8,128)S(1)} %add_add_fusion.1), channel_id=1, source_target_pairs={{0,8},{1,9},{2,10},{3,11},{4,12},{5,13},{6,14},{7,15},{8,0},{9,1},... | collective-permute-start | bytes 49160 | tf_op jit(solution)/shard_map/ppermute | solution.py:227
  39.2 6.8 %collective-permute-start.10 = (f32[32,128]{1,0:T(8,128)S(1)}, f32[32,128]{1,0:T(8,128)S(1)}, u32[]{:S(2)}, u32[]{:S(2)}) collective-permute-start(f32[32,128]{1,0:T(8,128)S(1)} %add_add_fusion), channel_id=1, source_target_pairs={{0,56},{1,57},{2,58},{3,59},{4,60},{5,61},{6,62},{7,63},{8,48},{9,... | collective-permute-start | bytes 49160 | tf_op jit(solution)/shard_map/ppermute | solution.py:227

commit v3 on v2

--- a/solution.py
+++ b/solution.py
@@ -31,8 +31,8 @@
     return lax.broadcasted_iota(jnp.int32, shape, axis)
 
 
-def assemble_kernel(k_ref, inner_ref, outer_ref, pert_ref, seeds_ref, strip_ref):
-    even = k_ref[0] % 2 == 0
+def assemble_kernel(inner_ref, outer_ref, pert_ref, seeds_ref, strip_ref):
+    even = lax.axis_index("xs") % 2 == 0
     before = jnp.where(even, outer_ref[ROWS - HALO :, :], inner_ref[ROWS - HALO :, :])
     after = jnp.where(even, inner_ref[:HALO, :], outer_ref[:HALO, :])
     strip_ref[0:HALO, :] = before
@@ -132,8 +132,8 @@
     return lax.dot_general(a, b, (((0,), (0,)), ((), ())), preferred_element_type=F32)
 
 
-def own_kernel(k_ref, strip_ref, modes_ref, sums_ref, w_ref, pert_ref, one_ref, two_ref):
-    k = k_ref[0]
+def own_kernel(strip_ref, modes_ref, sums_ref, w_ref, pert_ref, one_ref, two_ref):
+    k = lax.axis_index("xs")
     first_trial(k, strip_ref, w_ref, pert_ref, one_ref)
     sweep(k, 1, EXT - 2, one_ref, w_ref, two_ref)
     sweep(k, 2, EXT - 4, two_ref, w_ref, one_ref)
@@ -152,8 +152,8 @@
     sums_ref[...] = jnp.concatenate([gram, ham], axis=1)
 
 
-def next_kernel(k_ref, strip_ref, modes_ref, own_ref, sums_ref, w_ref, pert_ref, one_ref, two_ref):
-    k = k_ref[0]
+def next_kernel(strip_ref, modes_ref, own_ref, sums_ref, w_ref, pert_ref, one_ref, two_ref):
+    k = lax.axis_index("xs")
     first_trial(k, strip_ref, w_ref, pert_ref, one_ref)
     sweep(k, 2, EXT - 4, one_ref, w_ref, two_ref)
     sweep(k, 3, EXT - 6, two_ref, w_ref, one_ref)
@@ -182,42 +182,75 @@
     lax.fori_loop(0, ROWS // 4, rows, 0)
 
 
-def finish_kernel(keep_ref, sums_ref, parts_ref, modes_ref, proj_ref, corr_ref, held_ref, sem):
+def inverse_factors(sums):
+    row, lane = iota((8, LANES), 0), iota((8, LANES), 1)
+    start = lane // (2 * M) * (2 * M)
+    tiles = [
+        jnp.where((lane // M) % 2 == 0, sums[8 * t : 8 * t + 8], (lane % M == row + 8 * t).astype(F32))
+        for t in range(M // 8)
+    ]
+    for t in range(M // 8):
+        lanes = [start + (8 * t + i) for i in range(8)]
+        below = range(t + 1, M // 8)
+        columns = [[jnp.take_along_axis(tiles[u], lanes[i], axis=1) for u in below] for i in range(8)]
+        rows = [jnp.broadcast_to(tiles[t][i : i + 1], (8, LANES)) for i in range(8)]
+        corner = {(i, j): jnp.take_along_axis(rows[i], lanes[j], axis=1) for i in range(8) for j in range(i, 8)}
+        inverse, factor = [], {}
+        for i in range(8):
+            inverse.append(1.0 / corner[i, i])
+            for j in range(i + 1, 8):
+                factor[j, i] = corner[i, j] * inverse[i]
+            for j in range(i + 1, 8):
+                for m in range(j, 8):
+                    corner[j, m] = corner[j, m] - factor[j, i] * corner[i, m]
+        for i in range(8):
+            for j in range(i):
+                rows[i] = rows[i] - factor[i, j] * rows[j]
+                columns[i] = [c - factor[i, j] * p for c, p in zip(columns[i], columns[j])]
+        scaled = [rows[i] * inverse[i] for i in range(8)]
+        for u in below:
+            for i in range(8):
+                tiles[u] = tiles[u] - columns[i][u - t - 1] * scaled[i]
+        done = rows[0] / jnp.sqrt(corner[0, 0])
+        for i in range(1, 8):
+            done = jnp.where(row == i, rows[i] / jnp.sqrt(corner[i, i]), done)
+        tiles[t] = done
+    return jnp.concatenate(tiles, axis=0)
+
+
+def finish_kernel(sums_ref, parts_ref, modes_ref, proj_ref, corr_ref, held_ref, small_ref, sem):
     sums = sums_ref[...]
-    row, lane = iota((M, LANES), 0), iota((M, LANES), 1)
-    work = jnp.where((lane // M) % 2 == 0, sums, (lane % M == row).astype(F32))
-    pivots = jnp.ones((M, LANES), F32)
-    for j in range(M):
-        column = jnp.where(lane < 2 * M, work[:, j : j + 1], work[:, 2 * M + j : 2 * M + j + 1])
-        pivots = jnp.where(row == j, column, pivots)
-        scaled = work[j : j + 1, :] / column[j : j + 1, :]
-        work = work - jnp.where(row > j, column, 0.0) * scaled
-    inverse = work / jnp.sqrt(pivots)
+    inverse = inverse_factors(sums)
     own, following = inverse[:, M : 2 * M], inverse[:, 3 * M : 4 * M]
+    group = iota((M, LANES), 1) // M
     wide = jnp.concatenate([own * math.sqrt(NX * NY)] * GROUPS, axis=1)
-    wide = jnp.concatenate([jnp.where(lane // M == g, wide, 0.0) for g in range(GROUPS)], axis=0)
+    wide = jnp.concatenate([jnp.where(group == g, wide, 0.0) for g in range(GROUPS)], axis=0)
     high, low = split(wide)
-    twice = jnp.concatenate([high, high], axis=1)
-
-    def times(a, b):
-        return lax.dot_general(a, b, (((1,), (1,)), ((), ())), preferred_element_type=F32)
+    stack = jnp.concatenate([high, high], axis=1)
+    stack = jnp.concatenate([stack, jnp.concatenate([low, jnp.zeros_like(low)], axis=1)], axis=0)
 
     copies = []
+
+    def send(source, target):
+        copies.append(pltpu.make_async_copy(source, target, sem.at[len(copies)]))
+        copies[-1].start()
+
     for half in range(2):
+        rows = slice(8 * half, 8 * half + 8)
         for r in range(8 * half, 8 * half + 8):
-            part = parts_ref[r]
-            result = times(twice, part) + times(low, part[:, 0:LANES])
+            both = lax.dot_general(stack, parts_ref[r], (((1,), (1,)), ((), ())), preferred_element_type=F32)
+            result = both[0:LANES] + both[LANES:]
             for g in range(GROUPS):
                 held_ref[:, r, g * SPAN : (g + 1) * SPAN] = result[M * g : M * g + M]
-        rows = slice(8 * half, 8 * half + 8)
-        copy = pltpu.make_async_copy(held_ref.at[:, rows], modes_ref.at[:, rows], sem.at[half])
-        copy.start()
-        copies.append(copy)
+        send(held_ref.at[:, rows], modes_ref.at[:, rows])
 
     exact = functools.partial(jnp.dot, precision=lax.Precision.HIGHEST, preferred_element_type=F32)
     image, across = sums[:, M : 2 * M], sums[:, 3 * M : 4 * M]
-    proj_ref[...] = exact(exact(own, image), own.T)
-    corr_ref[...] = jnp.where(keep_ref[0] > 0, exact(exact(own, across), following.T), 0.0)
+    small_ref[0] = exact(exact(own, image), own.T)
+    has_next = lax.axis_index("slab") < lax.axis_size("slab") - 1
+    small_ref[1] = jnp.where(has_next, exact(exact(own, across), following.T), 0.0)
+    send(small_ref.at[0], proj_ref)
+    send(small_ref.at[1], corr_ref)
     for copy in copies:
         copy.wait()
 
@@ -234,25 +267,20 @@
 
 
 def local(perturbation, seeds):
-    k = lax.axis_index("xs")
     strips = NX // ROWS
     pert = perturbation[0]
     inner = lax.ppermute(pert, "xs", [(i, i ^ 1) for i in range(strips)])
     outer = lax.ppermute(pert, "xs", [(i, i - 1 if i % 2 == 0 else i + 1) for i in range(1, strips - 1)])
-    kk = k.reshape(1).astype(jnp.int32)
-    keep = (lax.axis_index("slab") < 3).reshape(1).astype(jnp.int32)
-
-    smem = pl.BlockSpec(memory_space=pltpu.SMEM)
     vmem = pl.BlockSpec(memory_space=pltpu.VMEM)
     params = pltpu.CompilerParams(vmem_limit_bytes=28 * 2**20)
     strip = pl.pallas_call(
         assemble_kernel,
         name="assemble",
         out_shape=jax.ShapeDtypeStruct((32, NY), jnp.int32),
-        in_specs=[smem, vmem, vmem, vmem, vmem],
+        in_specs=[vmem, vmem, vmem, vmem],
         out_specs=vmem,
         compiler_params=pltpu.CompilerParams(vmem_limit_bytes=4 * 2**20),
-    )(kk, inner, outer, pert, seeds[0].T)
+    )(inner, outer, pert, seeds[0].T)
     following = lax.ppermute(strip, "slab", [((i + 1) % 4, i) for i in range(4)])
 
     scratch = [
@@ -266,22 +294,22 @@
         own_kernel,
         name="own_trial",
         out_shape=(jax.ShapeDtypeStruct((ROWS * SPAN, LANES), F32), jax.ShapeDtypeStruct((M, 2 * M), F32)),
-        in_specs=[smem, vmem],
+        in_specs=[vmem],
         out_specs=(vmem, vmem),
         scratch_shapes=scratch,
         compiler_params=params,
         cost_estimate=cost,
-    )(kk, strip)
+    )(strip)
     sums = pl.pallas_call(
         next_kernel,
         name="next_trial",
         out_shape=jax.ShapeDtypeStruct((M, 4 * M), F32),
-        in_specs=[smem, vmem, vmem, vmem],
+        in_specs=[vmem, vmem, vmem],
         out_specs=vmem,
         scratch_shapes=scratch,
         compiler_params=params,
         cost_estimate=cost,
-    )(kk, following, field, own)
+    )(following, field, own)
     parts = pl.pallas_call(
         parts_kernel,
         name="parts",
@@ -300,12 +328,16 @@
             jax.ShapeDtypeStruct((M, M), F32),
             jax.ShapeDtypeStruct((M, M), F32),
         ),
-        in_specs=[smem, vmem, vmem],
-        out_specs=(pl.BlockSpec(memory_space=pl.ANY), vmem, vmem),
-        scratch_shapes=[pltpu.VMEM((M, ROWS, NY), F32), pltpu.SemaphoreType.DMA((2,))],
+        in_specs=[vmem, vmem],
+        out_specs=(pl.BlockSpec(memory_space=pl.ANY),) * 3,
+        scratch_shapes=[
+            pltpu.VMEM((M, ROWS, NY), F32),
+            pltpu.VMEM((2, M, M), F32),
+            pltpu.SemaphoreType.DMA((4,)),
+        ],
         compiler_params=params,
         cost_estimate=pl.CostEstimate(flops=2**28, bytes_accessed=2**23, transcendentals=0),
-    )(keep, sums, parts)
+    )(sums, parts)
     return modes[None], projected[None], correlations[None]
 
 

time: 52 us -> 49.1 us (0.944)
  Pallas kernels: 14.4 us -> 11.5 us
    pallas_call x1, Pallas kernels: 5.86 us -> 2.89 us  [local(): pl.pallas_call(finish_kernel, name='finish', out_shape=(jax.ShapeDtypeStr...]
  transfers between devices with their start and end apart: 11 -> 11, of which waited for: 7 -> 7; matrix products, arithmetic and copies ran while one was open for 0% -> 0% of each run, Pallas kernels for 9% -> 10%
where the time goes in v3:
time: 49.1 us; the launch traced here: 48.9 us
  starting transfers between devices  19.5 us (40%)
  waiting for transfers between devices  15.7 us (32%)
  Pallas kernels  11.5 us (23%)
  local copies, waits for them, and re-layouts  1.52 us (3%)
  between operations  0.7 us (1%)
    ppermute x8, starting transfers between devices, others(): lax.ppermute(x, 'xs', [(i, i ^ mask) for i in range(64)])  12.7 us
    ppermute x8, waiting for transfers between devices, others(): lax.ppermute(x, 'xs', [(i, i ^ mask) for i in range(64)])  11.8 us
    pallas_call x1, Pallas kernels, local(): pl.pallas_call(own_kernel, name='own_trial', out_shape=(jax.ShapeDtypeStr...  4.38 us
    ppermute x1, starting transfers between devices, local(): lax.ppermute(pert, 'xs', [(i, i - 1 if i % 2 == 0 else i + 1) for i in ra...  3.91 us
    ppermute x1, waiting for transfers between devices, local(): lax.ppermute(pert, 'xs', [(i, i - 1 if i % 2 == 0 else i + 1) for i in ra...  3.89 us
    pallas_call x1, Pallas kernels, local(): pl.pallas_call(next_kernel, name='next_trial', out_shape=jax.ShapeDtypeSt...  3.76 us
    pallas_call x1, Pallas kernels, local(): pl.pallas_call(finish_kernel, name='finish', out_shape=(jax.ShapeDtypeStr...  2.89 us
    ppermute x1, starting transfers between devices, local(): lax.ppermute(strip, 'slab', [((i + 1) % 4, i) for i in range(4)])  2.79 us
  transfers between devices with their start and end apart: 11, of which 7 were waited for; matrix products, arithmetic and copies ran while one was open for 0% of the time, Pallas kernels for 10%

profile of v3, /device:TPU:64, one launch (start us, length us, event | category | flops | bytes accessed | tf_op | source)
XLA Modules:
  0.0 48.9 jit_solution(17692182649572642693)
XLA Ops:
  0.6 3.9 %collective-permute-start.1 = (s32[16,1024]{1,0:T(8,128)}, s32[16,1024]{1,0:T(8,128)S(1)}, u32[]{:S(2)}, u32[]{:S(2)}) collective-permute-start(s32[16,1024]{1,0:T(8,128)} %bitcast.7), channel_id=1, source_target_pairs={{1,2},{2,1},{3,4},{4,3},{5,6},{6,5},{7,8},{8,7},{9,10},{10,9},{11,... | collective-permute-start | bytes 196616 | tf_op jit(solution)/shard_map/ppermute | solution.py:273
  4.5 0.1 collective-permute-start
  4.6 3.9 %collective-permute-done.1.outer_ref = s32[16,1024]{1,0:T(8,128)S(1)} collective-permute-done((s32[16,1024]{1,0:T(8,128)}, s32[16,1024]{1,0:T(8,128)S(1)}, u32[]{:S(2)}, u32[]{:S(2)}) %collective-permute-start.1) | collective-permute-done | bytes 65568 | tf_op jit(solution)/shard_map/ppermute | solution.py:273
  8.5 0.0 collective-permute-done.inner_ref
  8.5 0.0 copy-start
  8.5 0.8 %copy-done = s32[1,16,1024]{2,1,0:T(8,128)S(1)} copy-done((s32[1,16,1024]{2,1,0:T(8,128)S(1)}, s32[1,16,1024]{2,1,0:T(8,128)}, u32[]{:S(2)}) %copy-start) | copy-done | bytes 65560
  9.4 0.0 copy-start.1
  9.4 0.7 %copy-done.1 = s32[1,32,2]{1,2,0:T(2,128)S(1)} copy-done((s32[1,32,2]{1,2,0:T(2,128)S(1)}, s32[1,32,2]{1,2,0:T(2,128)}, u32[]{:S(2)}) %copy-start.1) | copy-done | bytes 280
  10.1 0.1 assemble.1.strip_ref
  10.1 2.8 %collective-permute-start.2 = (s32[32,1024]{1,0:T(8,128)S(1)}, s32[32,1024]{1,0:T(8,128)S(1)}, u32[]{:S(2)}, u32[]{:S(2)}) collective-permute-start(s32[32,1024]{1,0:T(8,128)S(1)} %assemble.1.strip_ref), channel_id=1, source_target_pairs={{64,0},{128,64},{192,128},{0,192},{65,1},{129,65},{193,129},{1,193... | collective-permute-start | bytes 393224 | tf_op jit(solution)/shard_map/ppermute | solution.py:284
  12.9 4.4 %own_trial.1 = (f32[4096,128]{1,0:T(8,128)S(1)}, f32[32,64]{1,0:T(8,128)S(1)}) custom-call(s32[32,1024]{1,0:T(8,128)S(1)} %assemble.1.strip_ref), custom_call_target="tpu_custom_call" | custom-call | flops 1073741824 | bytes 8388608 | tf_op jit(solution)/shard_map/own_trial/pallas_call | solution.py:293
  17.3 0.0 collective-permute-done.2.strip_ref
  17.3 3.8 %next_trial.1 = f32[32,128]{1,0:T(8,128)S(1)} custom-call(s32[32,1024]{1,0:T(8,128)S(1)} %collective-permute-done.2.strip_ref, f32[4096,128]{1,0:T(8,128)S(1)} %get-tuple-element.8.modes_ref, f32[32,64]{1,0:T(8,128)S(1)} %get-tuple-element.9.own_ref), custom_call_target="tpu_custom_call" | custom-call | flops 1073741824 | bytes 8388608 | tf_op jit(solution)/shard_map/next_trial/pallas_call | solution.py:303
  21.1 0.1 collective-permute-start.3
  21.2 1.2 %collective-permute-done.3 = f32[32,128]{1,0:T(8,128)S(1)} collective-permute-done((f32[32,128]{1,0:T(8,128)S(1)}, f32[32,128]{1,0:T(8,128)S(1)}, u32[]{:S(2)}, u32[]{:S(2)}) %collective-permute-start.3) | collective-permute-done | bytes 16416 | tf_op jit(solution)/shard_map/ppermute | solution.py:260
  22.4 2.2 %collective-permute-start.6 = (f32[32,128]{1,0:T(8,128)S(1)}, f32[32,128]{1,0:T(8,128)S(1)}, u32[]{:S(2)}, u32[]{:S(2)}) collective-permute-start(f32[32,128]{1,0:T(8,128)S(1)} %add.24), channel_id=1, source_target_pairs={{0,6},{1,7},{2,4},{3,5},{4,2},{5,3},{6,0},{7,1},{8,14},{9,15},{10,... | collective-permute-start | bytes 49160 | tf_op jit(solution)/shard_map/ppermute | solution.py:260
  24.6 0.0 collective-permute-start.5
  24.6 1.9 %collective-permute-start.4 = (f32[32,128]{1,0:T(8,128)S(1)}, f32[32,128]{1,0:T(8,128)S(1)}, u32[]{:S(2)}, u32[]{:S(2)}) collective-permute-start(f32[32,128]{1,0:T(8,128)S(1)} %add.24), channel_id=1, source_target_pairs={{0,2},{1,3},{2,0},{3,1},{4,6},{5,7},{6,4},{7,5},{8,10},{9,11},{10,... | collective-permute-start | bytes 49160 | tf_op jit(solution)/shard_map/ppermute | solution.py:260
  26.5 0.9 %collective-permute-done.6 = f32[32,128]{1,0:T(8,128)S(1)} collective-permute-done((f32[32,128]{1,0:T(8,128)S(1)}, f32[32,128]{1,0:T(8,128)S(1)}, u32[]{:S(2)}, u32[]{:S(2)}) %collective-permute-start.6) | collective-permute-done | bytes 16416 | tf_op jit(solution)/shard_map/ppermute | solution.py:260
  27.3 2.5 %collective-permute-done.5 = f32[32,128]{1,0:T(8,128)S(1)} collective-permute-done((f32[32,128]{1,0:T(8,128)S(1)}, f32[32,128]{1,0:T(8,128)S(1)}, u32[]{:S(2)}, u32[]{:S(2)}) %collective-permute-start.5) | collective-permute-done | bytes 16416 | tf_op jit(solution)/shard_map/ppermute | solution.py:260
  29.8 0.0 collective-permute-done.4
  29.9 0.2 collective-permute-start.9
  30.1 5.4 %collective-permute-start.8 = (f32[32,128]{1,0:T(8,128)S(1)}, f32[32,128]{1,0:T(8,128)S(1)}, u32[]{:S(2)}, u32[]{:S(2)}) collective-permute-start(f32[32,128]{1,0:T(8,128)S(1)} %add_add_fusion.1), channel_id=1, source_target_pairs={{0,16},{1,17},{2,18},{3,19},{4,20},{5,21},{6,22},{7,23},{8,24},{9,... | collective-permute-start | bytes 49160 | tf_op jit(solution)/shard_map/ppermute | solution.py:260
  35.4 0.0 collective-permute-start.7
  35.4 0.0 collective-permute-done.9
  35.4 1.9 %collective-permute-done.8 = f32[32,128]{1,0:T(8,128)S(1)} collective-permute-done((f32[32,128]{1,0:T(8,128)S(1)}, f32[32,128]{1,0:T(8,128)S(1)}, u32[]{:S(2)}, u32[]{:S(2)}) %collective-permute-start.8) | collective-permute-done | bytes 16416 | tf_op jit(solution)/shard_map/ppermute | solution.py:260
  37.3 1.9 %collective-permute-done.7 = f32[32,128]{1,0:T(8,128)S(1)} collective-permute-done((f32[32,128]{1,0:T(8,128)S(1)}, f32[32,128]{1,0:T(8,128)S(1)}, u32[]{:S(2)}, u32[]{:S(2)}) %collective-permute-start.7) | collective-permute-done | bytes 16416 | tf_op jit(solution)/shard_map/ppermute | solution.py:260
  39.2 2.9 %collective-permute-start.10 = (f32[32,128]{1,0:T(8,128)S(1)}, f32[32,128]{1,0:T(8,128)S(1)}, u32[]{:S(2)}, u32[]{:S(2)}) collective-permute-start(f32[32,128]{1,0:T(8,128)S(1)} %add_add_fusion), channel_id=1, source_target_pairs={{0,56},{1,57},{2,58},{3,59},{4,60},{5,61},{6,62},{7,63},{8,48},{9,... | collective-permute-start | bytes 49160 | tf_op jit(solution)/shard_map/ppermute | solution.py:260
  42.1 0.4 parts.1.parts_ref
  42.4 3.6 %collective-permute-done.10 = f32[32,128]{1,0:T(8,128)S(1)} collective-permute-done((f32[32,128]{1,0:T(8,128)S(1)}, f32[32,128]{1,0:T(8,128)S(1)}, u32[]{:S(2)}, u32[]{:S(2)}) %collective-permute-start.10) | collective-permute-done | bytes 16416 | tf_op jit(solution)/shard_map/ppermute | solution.py:260
  46.0 2.9 %finish.1 = (f32[32,16,1024]{2,1,0:T(8,128)}, f32[32,32]{1,0:T(8,128)}, f32[32,32]{1,0:T(8,128)}) custom-call(f32[32,128]{1,0:T(8,128)S(1)} %add.31.sums_ref, bf16[16,256,256]{2,1,0:T(8,128)(2,1)S(1)} %parts.1.parts_ref), custom_call_target="tpu_custom_call" | custom-call | flops 268435456 | bytes 8388608 | tf_op jit(solution)/shard_map/finish/pallas_call | solution.py:323
  (4 shorter events, 0.0 us)
Async XLA Ops:
  0.6 7.9 %collective-permute-start.1 = (s32[16,1024]{1,0:T(8,128)}, s32[16,1024]{1,0:T(8,128)S(1)}, u32[]{:S(2)}, u32[]{:S(2)}) collective-permute-start(s32[16,1024]{1,0:T(8,128)} %bitcast.7), channel_id=1, source_target_pairs={{1,2},{2,1},{3,4},{4,3},{5,6},{6,5},{7,8},{8,7},{9,10},{10,9},{11,... | collective-permute-start | bytes 196616 | tf_op jit(solution)/shard_map/ppermute | solution.py:273
  4.5 4.0 %collective-permute-start = (s32[16,1024]{1,0:T(8,128)}, s32[16,1024]{1,0:T(8,128)S(1)}, u32[]{:S(2)}, u32[]{:S(2)}) collective-permute-start(s32[16,1024]{1,0:T(8,128)} %bitcast.8), channel_id=1, source_target_pairs={{0,1},{1,0},{2,3},{3,2},{4,5},{5,4},{6,7},{7,6},{8,9},{9,8},{10,11... | collective-permute-start | bytes 196616 | tf_op jit(solution)/shard_map/ppermute | solution.py:272
  8.5 0.8 %copy-start = (s32[1,16,1024]{2,1,0:T(8,128)S(1)}, s32[1,16,1024]{2,1,0:T(8,128)}, u32[]{:S(2)}) copy-start(s32[1,16,1024]{2,1,0:T(8,128)} %param.2) | copy-start | bytes 196612
  9.4 0.7 %copy-start.1 = (s32[1,32,2]{1,2,0:T(2,128)S(1)}, s32[1,32,2]{1,2,0:T(2,128)}, u32[]{:S(2)}) copy-start(s32[1,32,2]{1,2,0:T(2,128)} %param.3) | copy-start | bytes 772
  10.1 7.2 %collective-permute-start.2 = (s32[32,1024]{1,0:T(8,128)S(1)}, s32[32,1024]{1,0:T(8,128)S(1)}, u32[]{:S(2)}, u32[]{:S(2)}) collective-permute-start(s32[32,1024]{1,0:T(8,128)S(1)} %assemble.1.strip_ref), channel_id=1, source_target_pairs={{64,0},{128,64},{192,128},{0,192},{65,1},{129,65},{193,129},{1,193... | collective-permute-start | bytes 393224 | tf_op jit(solution)/shard_map/ppermute | solution.py:284
  21.1 1.3 %collective-permute-start.3 = (f32[32,128]{1,0:T(8,128)S(1)}, f32[32,128]{1,0:T(8,128)S(1)}, u32[]{:S(2)}, u32[]{:S(2)}) collective-permute-start(f32[32,128]{1,0:T(8,128)S(1)} %next_trial.1), channel_id=1, source_target_pairs={{0,1},{1,0},{2,3},{3,2},{4,5},{5,4},{6,7},{7,6},{8,9},{9,8},{10,11... | collective-permute-start | bytes 49160 | tf_op jit(solution)/shard_map/ppermute | solution.py:260
  22.4 4.9 %collective-permute-start.6 = (f32[32,128]{1,0:T(8,128)S(1)}, f32[32,128]{1,0:T(8,128)S(1)}, u32[]{:S(2)}, u32[]{:S(2)}) collective-permute-start(f32[32,128]{1,0:T(8,128)S(1)} %add.24), channel_id=1, source_target_pairs={{0,6},{1,7},{2,4},{3,5},{4,2},{5,3},{6,0},{7,1},{8,14},{9,15},{10,... | collective-permute-start | bytes 49160 | tf_op jit(solution)/shard_map/ppermute | solution.py:260
  24.6 5.2 %collective-permute-start.5 = (f32[32,128]{1,0:T(8,128)S(1)}, f32[32,128]{1,0:T(8,128)S(1)}, u32[]{:S(2)}, u32[]{:S(2)}) collective-permute-start(f32[32,128]{1,0:T(8,128)S(1)} %add.24), channel_id=1, source_target_pairs={{0,4},{1,5},{2,6},{3,7},{4,0},{5,1},{6,2},{7,3},{8,12},{9,13},{10,... | collective-permute-start | bytes 49160 | tf_op jit(solution)/shard_map/ppermute | solution.py:260
  24.6 5.2 %collective-permute-start.4 = (f32[32,128]{1,0:T(8,128)S(1)}, f32[32,128]{1,0:T(8,128)S(1)}, u32[]{:S(2)}, u32[]{:S(2)}) collective-permute-start(f32[32,128]{1,0:T(8,128)S(1)} %add.24), channel_id=1, source_target_pairs={{0,2},{1,3},{2,0},{3,1},{4,6},{5,7},{6,4},{7,5},{8,10},{9,11},{10,... | collective-permute-start | bytes 49160 | tf_op jit(solution)/shard_map/ppermute | solution.py:260
  29.9 5.6 %collective-permute-start.9 = (f32[32,128]{1,0:T(8,128)S(1)}, f32[32,128]{1,0:T(8,128)S(1)}, u32[]{:S(2)}, u32[]{:S(2)}) collective-permute-start(f32[32,128]{1,0:T(8,128)S(1)} %add_add_fusion.1), channel_id=1, source_target_pairs={{0,24},{1,25},{2,26},{3,27},{4,28},{5,29},{6,30},{7,31},{8,16},{9,... | collective-permute-start | bytes 49160 | tf_op jit(solution)/shard_map/ppermute | solution.py:260
  30.1 7.3 %collective-permute-start.8 = (f32[32,128]{1,0:T(8,128)S(1)}, f32[32,128]{1,0:T(8,128)S(1)}, u32[]{:S(2)}, u32[]{:S(2)}) collective-permute-start(f32[32,128]{1,0:T(8,128)S(1)} %add_add_fusion.1), channel_id=1, source_target_pairs={{0,16},{1,17},{2,18},{3,19},{4,20},{5,21},{6,22},{7,23},{8,24},{9,... | collective-permute-start | bytes 49160 | tf_op jit(solution)/shard_map/ppermute | solution.py:260
  35.4 3.7 %collective-permute-start.7 = (f32[32,128]{1,0:T(8,128)S(1)}, f32[32,128]{1,0:T(8,128)S(1)}, u32[]{:S(2)}, u32[]{:S(2)}) collective-permute-start(f32[32,128]{1,0:T(8,128)S(1)} %add_add_fusion.1), channel_id=1, source_target_pairs={{0,8},{1,9},{2,10},{3,11},{4,12},{5,13},{6,14},{7,15},{8,0},{9,1},... | collective-permute-start | bytes 49160 | tf_op jit(solution)/shard_map/ppermute | solution.py:260
  39.2 6.8 %collective-permute-start.10 = (f32[32,128]{1,0:T(8,128)S(1)}, f32[32,128]{1,0:T(8,128)S(1)}, u32[]{:S(2)}, u32[]{:S(2)}) collective-permute-start(f32[32,128]{1,0:T(8,128)S(1)} %add_add_fusion), channel_id=1, source_target_pairs={{0,56},{1,57},{2,58},{3,59},{4,60},{5,61},{6,62},{7,63},{8,48},{9,... | collective-permute-start | bytes 49160 | tf_op jit(solution)/shard_map/ppermute | solution.py:260

commit v4 on v3

--- a/solution.py
+++ b/solution.py
@@ -31,35 +31,46 @@
     return lax.broadcasted_iota(jnp.int32, shape, axis)
 
 
-def assemble_kernel(inner_ref, outer_ref, pert_ref, seeds_ref, strip_ref):
-    even = lax.axis_index("xs") % 2 == 0
-    before = jnp.where(even, outer_ref[ROWS - HALO :, :], inner_ref[ROWS - HALO :, :])
-    after = jnp.where(even, inner_ref[:HALO, :], outer_ref[:HALO, :])
-    strip_ref[0:HALO, :] = before
-    strip_ref[HALO : HALO + ROWS, :] = pert_ref[...]
-    strip_ref[HALO + ROWS : EXT, :] = after
-    strip_ref[EXT : EXT + 2, 0:LANES] = jnp.concatenate([seeds_ref[...]] * GROUPS, axis=1)
-
-
-def first_trial(k, strip_ref, w_ref, pert_ref, out_ref):
+def sine_tables(k, first, second):
     unit = math.pi / (NX + 1)
-    first = strip_ref[EXT : EXT + 1, 0:LANES].astype(F32)
-    second = strip_ref[EXT + 1 : EXT + 2, 0:LANES].astype(F32)
-    shift = 2.0 * jnp.cos(unit * first) + 2.0 * jnp.cos(unit * second)
-
-    group, s = iota((8, LANES), 1) // M, iota((8, LANES), 0)
-    base = (group * SPAN + s * STEPS).astype(F32)
+    base = column_base().astype(F32)
     scale = 2.0 / math.sqrt((NX + 1) * (NY + 1))
     angle = unit * second * (base + 1.0)
     sin_base, cos_base = scale * jnp.sin(angle), scale * jnp.cos(angle)
     step = unit * second * iota((STEPS, LANES), 0).astype(F32)
     sin_step, cos_step = jnp.sin(step), jnp.cos(step)
+    sines = [sin_base * cos_step[q : q + 1] + cos_base * sin_step[q : q + 1] for q in range(STEPS)]
     row = iota((EXT, LANES), 0) + (k * ROWS - HALO)
     along_x = jnp.sin(unit * first * (row.astype(F32) + 1.0))
     along_x = jnp.where((row >= 0) & (row < NX), along_x, 0.0)
-    xpos = (row.astype(F32) + 0.5) / NX - 0.5
+    return sines, along_x, 2.0 * jnp.cos(unit * first) + 2.0 * jnp.cos(unit * second)
+
+
+def column_base():
+    return iota((8, LANES), 1) // M * SPAN + iota((8, LANES), 0) * STEPS
+
+
+def prepare_kernel(pert_ref, seeds_ref, strip_ref, sines_ref, along_ref, shift_ref):
+    strip_ref[HALO : HALO + ROWS, :] = pert_ref[...]
+    indices = jnp.concatenate([seeds_ref[...]] * GROUPS, axis=1)
+    strip_ref[EXT : EXT + 2, 0:LANES] = indices
+    first, second = indices[0:1].astype(F32), indices[1:2].astype(F32)
+    sines, along_ref[...], shift = sine_tables(lax.axis_index("xs"), first, second)
+    for q in range(STEPS):
+        sines_ref[q] = sines[q]
+    shift_ref[...] = jnp.broadcast_to(shift, (8, LANES))
+
+
+def assemble_kernel(inner_ref, outer_ref, middle_ref, strip_ref):
+    even = lax.axis_index("xs") % 2 == 0
+    strip_ref[...] = middle_ref[...]
+    strip_ref[0:HALO, :] = jnp.where(even, outer_ref[ROWS - HALO :, :], inner_ref[ROWS - HALO :, :])
+    strip_ref[HALO + ROWS : EXT, :] = jnp.where(even, inner_ref[:HALO, :], outer_ref[:HALO, :])
+
+
+def first_trial(k, strip_ref, sines, along_x, shift, w_ref, pert_ref, out_ref):
+    xpos = ((iota((EXT, LANES), 0) + (k * ROWS - HALO)).astype(F32) + 0.5) / NX - 0.5
     x_part = 9.0 - 4.0 * (xpos * xpos + 0.5 * xpos)
-
     pert = strip_ref[0:EXT, :].astype(F32)
     stacked = [pert[:, g * SPAN : (g + 1) * SPAN] for g in range(GROUPS)]
     stacked = jnp.concatenate(stacked + [jnp.zeros((LANES - GROUPS * EXT, SPAN), F32)], axis=0)
@@ -67,9 +78,9 @@
     spread = jnp.concatenate([pert_ref[pl.ds(q, 8, stride=STEPS), :] for q in range(STEPS)], axis=0).astype(BF16)
     source = iota((LANES, LANES), 0) - EXT * (iota((LANES, LANES), 1) // M)
 
-    sines, y_parts = [], []
+    base = column_base().astype(F32)
+    y_parts = []
     for q in range(STEPS):
-        sines.append(sin_base * cos_step[q : q + 1] + cos_base * sin_step[q : q + 1])
         ypos = (base + (q + 0.5)) / NY - 0.5
         y_parts.append(2.4 * ypos * ypos)
     for r in range(EXT):
@@ -132,9 +143,12 @@
     return lax.dot_general(a, b, (((0,), (0,)), ((), ())), preferred_element_type=F32)
 
 
-def own_kernel(strip_ref, modes_ref, sums_ref, w_ref, pert_ref, one_ref, two_ref):
+def own_kernel(
+    strip_ref, sines_ref, along_ref, shift_ref, modes_ref, sums_ref, w_ref, pert_ref, one_ref, two_ref
+):
     k = lax.axis_index("xs")
-    first_trial(k, strip_ref, w_ref, pert_ref, one_ref)
+    sines = [sines_ref[q] for q in range(STEPS)]
+    first_trial(k, strip_ref, sines, along_ref[...], shift_ref[...], w_ref, pert_ref, one_ref)
     sweep(k, 1, EXT - 2, one_ref, w_ref, two_ref)
     sweep(k, 2, EXT - 4, two_ref, w_ref, one_ref)
     sweep(k, 3, EXT - 6, one_ref, w_ref, two_ref)
@@ -154,7 +168,9 @@
 
 def next_kernel(strip_ref, modes_ref, own_ref, sums_ref, w_ref, pert_ref, one_ref, two_ref):
     k = lax.axis_index("xs")
-    first_trial(k, strip_ref, w_ref, pert_ref, one_ref)
+    first = strip_ref[EXT : EXT + 1, 0:LANES].astype(F32)
+    second = strip_ref[EXT + 1 : EXT + 2, 0:LANES].astype(F32)
+    first_trial(k, strip_ref, *sine_tables(k, first, second), w_ref, pert_ref, one_ref)
     sweep(k, 2, EXT - 4, one_ref, w_ref, two_ref)
     sweep(k, 3, EXT - 6, two_ref, w_ref, one_ref)
     sweep(k, 4, ROWS, one_ref, w_ref, two_ref)
@@ -273,14 +289,28 @@
     outer = lax.ppermute(pert, "xs", [(i, i - 1 if i % 2 == 0 else i + 1) for i in range(1, strips - 1)])
     vmem = pl.BlockSpec(memory_space=pltpu.VMEM)
     params = pltpu.CompilerParams(vmem_limit_bytes=28 * 2**20)
+    middle, *tables = pl.pallas_call(
+        prepare_kernel,
+        name="prepare",
+        out_shape=(
+            jax.ShapeDtypeStruct((32, NY), jnp.int32),
+            jax.ShapeDtypeStruct((STEPS, 8, LANES), F32),
+            jax.ShapeDtypeStruct((EXT, LANES), F32),
+            jax.ShapeDtypeStruct((8, LANES), F32),
+        ),
+        in_specs=[vmem, vmem],
+        out_specs=(vmem,) * 4,
+        compiler_params=pltpu.CompilerParams(vmem_limit_bytes=4 * 2**20),
+        cost_estimate=pl.CostEstimate(flops=2**20, bytes_accessed=2**20, transcendentals=2**14),
+    )(pert, seeds[0].T)
     strip = pl.pallas_call(
         assemble_kernel,
         name="assemble",
         out_shape=jax.ShapeDtypeStruct((32, NY), jnp.int32),
-        in_specs=[vmem, vmem, vmem, vmem],
+        in_specs=[vmem, vmem, vmem],
         out_specs=vmem,
         compiler_params=pltpu.CompilerParams(vmem_limit_bytes=4 * 2**20),
-    )(inner, outer, pert, seeds[0].T)
+    )(inner, outer, middle)
     following = lax.ppermute(strip, "slab", [((i + 1) % 4, i) for i in range(4)])
 
     scratch = [
@@ -294,12 +324,12 @@
         own_kernel,
         name="own_trial",
         out_shape=(jax.ShapeDtypeStruct((ROWS * SPAN, LANES), F32), jax.ShapeDtypeStruct((M, 2 * M), F32)),
-        in_specs=[vmem],
+        in_specs=[vmem, vmem, vmem, vmem],
         out_specs=(vmem, vmem),
         scratch_shapes=scratch,
         compiler_params=params,
         cost_estimate=cost,
-    )(strip)
+    )(strip, *tables)
     sums = pl.pallas_call(
         next_kernel,
         name="next_trial",

time: 49.1 us -> 47.3 us (0.963)
  waiting for transfers between devices: 15.7 us -> 14 us
    ppermute x1, waiting for transfers between devices: 3.89 us -> 2.13 us  [local(): lax.ppermute(pert, 'xs', [(i, i - 1 if i % 2 == 0 else i + 1) for i in ra...]
where the time goes in v4:
time: 47.3 us; the launch traced here: 47.2 us
  starting transfers between devices  19.5 us (41%)
  waiting for transfers between devices  14 us (30%)
  Pallas kernels  11.5 us (24%)
  local copies, waits for them, and re-layouts  1.51 us (3%)
  between operations  0.72 us (2%)
    ppermute x8, starting transfers between devices, others(): lax.ppermute(x, 'xs', [(i, i ^ mask) for i in range(64)])  12.7 us
    ppermute x8, waiting for transfers between devices, others(): lax.ppermute(x, 'xs', [(i, i ^ mask) for i in range(64)])  11.8 us
    pallas_call x1, Pallas kernels, local(): pl.pallas_call(own_kernel, name='own_trial', out_shape=(jax.ShapeDtypeStr...  4.18 us
    ppermute x1, starting transfers between devices, local(): lax.ppermute(pert, 'xs', [(i, i - 1 if i % 2 == 0 else i + 1) for i in ra...  3.91 us
    pallas_call x1, Pallas kernels, local(): pl.pallas_call(next_kernel, name='next_trial', out_shape=jax.ShapeDtypeSt...  3.77 us
    pallas_call x1, Pallas kernels, local(): pl.pallas_call(finish_kernel, name='finish', out_shape=(jax.ShapeDtypeStr...  2.88 us
    ppermute x1, starting transfers between devices, local(): lax.ppermute(strip, 'slab', [((i + 1) % 4, i) for i in range(4)])  2.84 us
    ppermute x1, waiting for transfers between devices, local(): lax.ppermute(pert, 'xs', [(i, i - 1 if i % 2 == 0 else i + 1) for i in ra...  2.13 us
  transfers between devices with their start and end apart: 11, of which 7 were waited for; matrix products, arithmetic and copies ran while one was open for 0% of the time, Pallas kernels for 10%

profile of v4, /device:TPU:64, one launch (start us, length us, event | category | flops | bytes accessed | tf_op | source)
XLA Modules:
  0.0 47.2 jit_solution(16841202467163092918)
XLA Ops:
  0.6 3.9 %collective-permute-start.1 = (s32[16,1024]{1,0:T(8,128)}, s32[16,1024]{1,0:T(8,128)S(1)}, u32[]{:S(2)}, u32[]{:S(2)}) collective-permute-start(s32[16,1024]{1,0:T(8,128)} %bitcast.7), channel_id=1, source_target_pairs={{1,2},{2,1},{3,4},{4,3},{5,6},{6,5},{7,8},{8,7},{9,10},{10,9},{11,... | collective-permute-start | bytes 196616 | tf_op jit(solution)/shard_map/ppermute | solution.py:289
  4.5 0.1 collective-permute-start
  4.6 0.0 copy-start
  4.7 0.8 %copy-done = s32[1,16,1024]{2,1,0:T(8,128)S(1)} copy-done((s32[1,16,1024]{2,1,0:T(8,128)S(1)}, s32[1,16,1024]{2,1,0:T(8,128)}, u32[]{:S(2)}) %copy-start) | copy-done | bytes 65560
  5.5 0.0 copy-start.1
  5.5 0.7 %copy-done.1 = s32[1,32,2]{1,2,0:T(2,128)S(1)} copy-done((s32[1,32,2]{1,2,0:T(2,128)S(1)}, s32[1,32,2]{1,2,0:T(2,128)}, u32[]{:S(2)}) %copy-start.1) | copy-done | bytes 280
  6.2 0.2 prepare.1
  6.4 2.1 %collective-permute-done.1.outer_ref = s32[16,1024]{1,0:T(8,128)S(1)} collective-permute-done((s32[16,1024]{1,0:T(8,128)}, s32[16,1024]{1,0:T(8,128)S(1)}, u32[]{:S(2)}, u32[]{:S(2)}) %collective-permute-start.1) | collective-permute-done | bytes 65568 | tf_op jit(solution)/shard_map/ppermute | solution.py:289
  8.5 0.0 collective-permute-done.inner_ref
  8.6 2.8 %collective-permute-start.2 = (s32[32,1024]{1,0:T(8,128)S(1)}, s32[32,1024]{1,0:T(8,128)S(1)}, u32[]{:S(2)}, u32[]{:S(2)}) collective-permute-start(s32[32,1024]{1,0:T(8,128)S(1)} %assemble.1.strip_ref), channel_id=1, source_target_pairs={{64,0},{128,64},{192,128},{0,192},{65,1},{129,65},{193,129},{1,193... | collective-permute-start | bytes 393224 | tf_op jit(solution)/shard_map/ppermute | solution.py:314
  11.4 4.2 %own_trial.1 = (f32[4096,128]{1,0:T(8,128)S(1)}, f32[32,64]{1,0:T(8,128)S(1)}) custom-call(s32[32,1024]{1,0:T(8,128)S(1)} %assemble.1.strip_ref, f32[32,8,128]{2,1,0:T(8,128)S(1)} %get-tuple-element.13.sines_ref, f32[24,128]{1,0:T(8,128)S(1)} %get-tuple-element.14.along_ref, f32[8,128]{1,0:T(8,128)S(1)} %get-tuple-element.15.shift_ref), custom_call_target="tpu_custom_call" | custom-call | flops 1073741824 | bytes 8388608 | tf_op jit(solution)/shard_map/own_trial/pallas_call | solution.py:323
  15.6 0.0 collective-permute-done.2.strip_ref
  15.6 3.8 %next_trial.1 = f32[32,128]{1,0:T(8,128)S(1)} custom-call(s32[32,1024]{1,0:T(8,128)S(1)} %collective-permute-done.2.strip_ref, f32[4096,128]{1,0:T(8,128)S(1)} %get-tuple-element.16.modes_ref, f32[32,64]{1,0:T(8,128)S(1)} %get-tuple-element.17.own_ref), custom_call_target="tpu_custom_call" | custom-call | flops 1073741824 | bytes 8388608 | tf_op jit(solution)/shard_map/next_trial/pallas_call | solution.py:333
  19.4 0.1 collective-permute-start.3
  19.5 1.2 %collective-permute-done.3 = f32[32,128]{1,0:T(8,128)S(1)} collective-permute-done((f32[32,128]{1,0:T(8,128)S(1)}, f32[32,128]{1,0:T(8,128)S(1)}, u32[]{:S(2)}, u32[]{:S(2)}) %collective-permute-start.3) | collective-permute-done | bytes 16416 | tf_op jit(solution)/shard_map/ppermute | solution.py:276
  20.7 2.2 %collective-permute-start.6 = (f32[32,128]{1,0:T(8,128)S(1)}, f32[32,128]{1,0:T(8,128)S(1)}, u32[]{:S(2)}, u32[]{:S(2)}) collective-permute-start(f32[32,128]{1,0:T(8,128)S(1)} %add.24), channel_id=1, source_target_pairs={{0,6},{1,7},{2,4},{3,5},{4,2},{5,3},{6,0},{7,1},{8,14},{9,15},{10,... | collective-permute-start | bytes 49160 | tf_op jit(solution)/shard_map/ppermute | solution.py:276
  22.9 0.0 collective-permute-start.5
  22.9 1.9 %collective-permute-start.4 = (f32[32,128]{1,0:T(8,128)S(1)}, f32[32,128]{1,0:T(8,128)S(1)}, u32[]{:S(2)}, u32[]{:S(2)}) collective-permute-start(f32[32,128]{1,0:T(8,128)S(1)} %add.24), channel_id=1, source_target_pairs={{0,2},{1,3},{2,0},{3,1},{4,6},{5,7},{6,4},{7,5},{8,10},{9,11},{10,... | collective-permute-start | bytes 49160 | tf_op jit(solution)/shard_map/ppermute | solution.py:276
  24.8 0.9 %collective-permute-done.6 = f32[32,128]{1,0:T(8,128)S(1)} collective-permute-done((f32[32,128]{1,0:T(8,128)S(1)}, f32[32,128]{1,0:T(8,128)S(1)}, u32[]{:S(2)}, u32[]{:S(2)}) %collective-permute-start.6) | collective-permute-done | bytes 16416 | tf_op jit(solution)/shard_map/ppermute | solution.py:276
  25.6 2.5 %collective-permute-done.5 = f32[32,128]{1,0:T(8,128)S(1)} collective-permute-done((f32[32,128]{1,0:T(8,128)S(1)}, f32[32,128]{1,0:T(8,128)S(1)}, u32[]{:S(2)}, u32[]{:S(2)}) %collective-permute-start.5) | collective-permute-done | bytes 16416 | tf_op jit(solution)/shard_map/ppermute | solution.py:276
  28.1 0.0 collective-permute-done.4
  28.1 0.2 collective-permute-start.9
  28.4 5.4 %collective-permute-start.8 = (f32[32,128]{1,0:T(8,128)S(1)}, f32[32,128]{1,0:T(8,128)S(1)}, u32[]{:S(2)}, u32[]{:S(2)}) collective-permute-start(f32[32,128]{1,0:T(8,128)S(1)} %add_add_fusion.1), channel_id=1, source_target_pairs={{0,16},{1,17},{2,18},{3,19},{4,20},{5,21},{6,22},{7,23},{8,24},{9,... | collective-permute-start | bytes 49160 | tf_op jit(solution)/shard_map/ppermute | solution.py:276
  33.7 0.0 collective-permute-start.7
  33.7 0.0 collective-permute-done.9
  33.7 1.9 %collective-permute-done.8 = f32[32,128]{1,0:T(8,128)S(1)} collective-permute-done((f32[32,128]{1,0:T(8,128)S(1)}, f32[32,128]{1,0:T(8,128)S(1)}, u32[]{:S(2)}, u32[]{:S(2)}) %collective-permute-start.8) | collective-permute-done | bytes 16416 | tf_op jit(solution)/shard_map/ppermute | solution.py:276
  35.6 1.9 %collective-permute-done.7 = f32[32,128]{1,0:T(8,128)S(1)} collective-permute-done((f32[32,128]{1,0:T(8,128)S(1)}, f32[32,128]{1,0:T(8,128)S(1)}, u32[]{:S(2)}, u32[]{:S(2)}) %collective-permute-start.7) | collective-permute-done | bytes 16416 | tf_op jit(solution)/shard_map/ppermute | solution.py:276
  37.5 2.9 %collective-permute-start.10 = (f32[32,128]{1,0:T(8,128)S(1)}, f32[32,128]{1,0:T(8,128)S(1)}, u32[]{:S(2)}, u32[]{:S(2)}) collective-permute-start(f32[32,128]{1,0:T(8,128)S(1)} %add_add_fusion), channel_id=1, source_target_pairs={{0,56},{1,57},{2,58},{3,59},{4,60},{5,61},{6,62},{7,63},{8,48},{9,... | collective-permute-start | bytes 49160 | tf_op jit(solution)/shard_map/ppermute | solution.py:276
  40.4 0.4 parts.1.parts_ref
  40.7 3.6 %collective-permute-done.10 = f32[32,128]{1,0:T(8,128)S(1)} collective-permute-done((f32[32,128]{1,0:T(8,128)S(1)}, f32[32,128]{1,0:T(8,128)S(1)}, u32[]{:S(2)}, u32[]{:S(2)}) %collective-permute-start.10) | collective-permute-done | bytes 16416 | tf_op jit(solution)/shard_map/ppermute | solution.py:276
  44.3 2.9 %finish.1 = (f32[32,16,1024]{2,1,0:T(8,128)}, f32[32,32]{1,0:T(8,128)}, f32[32,32]{1,0:T(8,128)}) custom-call(f32[32,128]{1,0:T(8,128)S(1)} %add.31.sums_ref, bf16[16,256,256]{2,1,0:T(8,128)(2,1)S(1)} %parts.1.parts_ref), custom_call_target="tpu_custom_call" | custom-call | flops 268435456 | bytes 8388608 | tf_op jit(solution)/shard_map/finish/pallas_call | solution.py:353
  (5 shorter events, 0.0 us)
Async XLA Ops:
  0.6 7.9 %collective-permute-start.1 = (s32[16,1024]{1,0:T(8,128)}, s32[16,1024]{1,0:T(8,128)S(1)}, u32[]{:S(2)}, u32[]{:S(2)}) collective-permute-start(s32[16,1024]{1,0:T(8,128)} %bitcast.7), channel_id=1, source_target_pairs={{1,2},{2,1},{3,4},{4,3},{5,6},{6,5},{7,8},{8,7},{9,10},{10,9},{11,... | collective-permute-start | bytes 196616 | tf_op jit(solution)/shard_map/ppermute | solution.py:289
  4.5 4.0 %collective-permute-start = (s32[16,1024]{1,0:T(8,128)}, s32[16,1024]{1,0:T(8,128)S(1)}, u32[]{:S(2)}, u32[]{:S(2)}) collective-permute-start(s32[16,1024]{1,0:T(8,128)} %bitcast.8), channel_id=1, source_target_pairs={{0,1},{1,0},{2,3},{3,2},{4,5},{5,4},{6,7},{7,6},{8,9},{9,8},{10,11... | collective-permute-start | bytes 196616 | tf_op jit(solution)/shard_map/ppermute | solution.py:288
  4.6 0.8 %copy-start = (s32[1,16,1024]{2,1,0:T(8,128)S(1)}, s32[1,16,1024]{2,1,0:T(8,128)}, u32[]{:S(2)}) copy-start(s32[1,16,1024]{2,1,0:T(8,128)} %param.2) | copy-start | bytes 196612
  5.5 0.7 %copy-start.1 = (s32[1,32,2]{1,2,0:T(2,128)S(1)}, s32[1,32,2]{1,2,0:T(2,128)}, u32[]{:S(2)}) copy-start(s32[1,32,2]{1,2,0:T(2,128)} %param.3) | copy-start | bytes 772
  8.6 7.0 %collective-permute-start.2 = (s32[32,1024]{1,0:T(8,128)S(1)}, s32[32,1024]{1,0:T(8,128)S(1)}, u32[]{:S(2)}, u32[]{:S(2)}) collective-permute-start(s32[32,1024]{1,0:T(8,128)S(1)} %assemble.1.strip_ref), channel_id=1, source_target_pairs={{64,0},{128,64},{192,128},{0,192},{65,1},{129,65},{193,129},{1,193... | collective-permute-start | bytes 393224 | tf_op jit(solution)/shard_map/ppermute | solution.py:314
  19.4 1.3 %collective-permute-start.3 = (f32[32,128]{1,0:T(8,128)S(1)}, f32[32,128]{1,0:T(8,128)S(1)}, u32[]{:S(2)}, u32[]{:S(2)}) collective-permute-start(f32[32,128]{1,0:T(8,128)S(1)} %next_trial.1), channel_id=1, source_target_pairs={{0,1},{1,0},{2,3},{3,2},{4,5},{5,4},{6,7},{7,6},{8,9},{9,8},{10,11... | collective-permute-start | bytes 49160 | tf_op jit(solution)/shard_map/ppermute | solution.py:276
  20.7 4.9 %collective-permute-start.6 = (f32[32,128]{1,0:T(8,128)S(1)}, f32[32,128]{1,0:T(8,128)S(1)}, u32[]{:S(2)}, u32[]{:S(2)}) collective-permute-start(f32[32,128]{1,0:T(8,128)S(1)} %add.24), channel_id=1, source_target_pairs={{0,6},{1,7},{2,4},{3,5},{4,2},{5,3},{6,0},{7,1},{8,14},{9,15},{10,... | collective-permute-start | bytes 49160 | tf_op jit(solution)/shard_map/ppermute | solution.py:276
  22.9 5.2 %collective-permute-start.5 = (f32[32,128]{1,0:T(8,128)S(1)}, f32[32,128]{1,0:T(8,128)S(1)}, u32[]{:S(2)}, u32[]{:S(2)}) collective-permute-start(f32[32,128]{1,0:T(8,128)S(1)} %add.24), channel_id=1, source_target_pairs={{0,4},{1,5},{2,6},{3,7},{4,0},{5,1},{6,2},{7,3},{8,12},{9,13},{10,... | collective-permute-start | bytes 49160 | tf_op jit(solution)/shard_map/ppermute | solution.py:276
  22.9 5.2 %collective-permute-start.4 = (f32[32,128]{1,0:T(8,128)S(1)}, f32[32,128]{1,0:T(8,128)S(1)}, u32[]{:S(2)}, u32[]{:S(2)}) collective-permute-start(f32[32,128]{1,0:T(8,128)S(1)} %add.24), channel_id=1, source_target_pairs={{0,2},{1,3},{2,0},{3,1},{4,6},{5,7},{6,4},{7,5},{8,10},{9,11},{10,... | collective-permute-start | bytes 49160 | tf_op jit(solution)/shard_map/ppermute | solution.py:276
  28.1 5.6 %collective-permute-start.9 = (f32[32,128]{1,0:T(8,128)S(1)}, f32[32,128]{1,0:T(8,128)S(1)}, u32[]{:S(2)}, u32[]{:S(2)}) collective-permute-start(f32[32,128]{1,0:T(8,128)S(1)} %add_add_fusion.1), channel_id=1, source_target_pairs={{0,24},{1,25},{2,26},{3,27},{4,28},{5,29},{6,30},{7,31},{8,16},{9,... | collective-permute-start | bytes 49160 | tf_op jit(solution)/shard_map/ppermute | solution.py:276
  28.4 7.3 %collective-permute-start.8 = (f32[32,128]{1,0:T(8,128)S(1)}, f32[32,128]{1,0:T(8,128)S(1)}, u32[]{:S(2)}, u32[]{:S(2)}) collective-permute-start(f32[32,128]{1,0:T(8,128)S(1)} %add_add_fusion.1), channel_id=1, source_target_pairs={{0,16},{1,17},{2,18},{3,19},{4,20},{5,21},{6,22},{7,23},{8,24},{9,... | collective-permute-start | bytes 49160 | tf_op jit(solution)/shard_map/ppermute | solution.py:276
  33.7 3.7 %collective-permute-start.7 = (f32[32,128]{1,0:T(8,128)S(1)}, f32[32,128]{1,0:T(8,128)S(1)}, u32[]{:S(2)}, u32[]{:S(2)}) collective-permute-start(f32[32,128]{1,0:T(8,128)S(1)} %add_add_fusion.1), channel_id=1, source_target_pairs={{0,8},{1,9},{2,10},{3,11},{4,12},{5,13},{6,14},{7,15},{8,0},{9,1},... | collective-permute-start | bytes 49160 | tf_op jit(solution)/shard_map/ppermute | solution.py:276
  37.5 6.8 %collective-permute-start.10 = (f32[32,128]{1,0:T(8,128)S(1)}, f32[32,128]{1,0:T(8,128)S(1)}, u32[]{:S(2)}, u32[]{:S(2)}) collective-permute-start(f32[32,128]{1,0:T(8,128)S(1)} %add_add_fusion), channel_id=1, source_target_pairs={{0,56},{1,57},{2,58},{3,59},{4,60},{5,61},{6,62},{7,63},{8,48},{9,... | collective-permute-start | bytes 49160 | tf_op jit(solution)/shard_map/ppermute | solution.py:276

commit v5 on v4

--- a/solution.py
+++ b/solution.py
@@ -18,6 +18,7 @@
 GROUPS = LANES // M
 SPAN = NY // GROUPS
 STEPS = SPAN // 8
+SENT = EXT
 F32 = jnp.float32
 BF16 = jnp.bfloat16
 
@@ -50,47 +51,71 @@
     return iota((8, LANES), 1) // M * SPAN + iota((8, LANES), 0) * STEPS
 
 
-def prepare_kernel(pert_ref, seeds_ref, strip_ref, sines_ref, along_ref, shift_ref):
-    strip_ref[HALO : HALO + ROWS, :] = pert_ref[...]
-    indices = jnp.concatenate([seeds_ref[...]] * GROUPS, axis=1)
-    strip_ref[EXT : EXT + 2, 0:LANES] = indices
-    first, second = indices[0:1].astype(F32), indices[1:2].astype(F32)
-    sines, along_ref[...], shift = sine_tables(lax.axis_index("xs"), first, second)
-    for q in range(STEPS):
-        sines_ref[q] = sines[q]
-    shift_ref[...] = jnp.broadcast_to(shift, (8, LANES))
-
-
-def assemble_kernel(inner_ref, outer_ref, middle_ref, strip_ref):
-    even = lax.axis_index("xs") % 2 == 0
-    strip_ref[...] = middle_ref[...]
-    strip_ref[0:HALO, :] = jnp.where(even, outer_ref[ROWS - HALO :, :], inner_ref[ROWS - HALO :, :])
-    strip_ref[HALO + ROWS : EXT, :] = jnp.where(even, inner_ref[:HALO, :], outer_ref[:HALO, :])
-
-
-def first_trial(k, strip_ref, sines, along_x, shift, w_ref, pert_ref, out_ref):
+def first_rows(k, pert, rows, sines, along_x, shift, turned_ref, write):
+    count = pert.shape[0]
     xpos = ((iota((EXT, LANES), 0) + (k * ROWS - HALO)).astype(F32) + 0.5) / NX - 0.5
     x_part = 9.0 - 4.0 * (xpos * xpos + 0.5 * xpos)
-    pert = strip_ref[0:EXT, :].astype(F32)
     stacked = [pert[:, g * SPAN : (g + 1) * SPAN] for g in range(GROUPS)]
-    stacked = jnp.concatenate(stacked + [jnp.zeros((LANES - GROUPS * EXT, SPAN), F32)], axis=0)
-    pert_ref[...] = jnp.transpose(stacked)
-    spread = jnp.concatenate([pert_ref[pl.ds(q, 8, stride=STEPS), :] for q in range(STEPS)], axis=0).astype(BF16)
-    source = iota((LANES, LANES), 0) - EXT * (iota((LANES, LANES), 1) // M)
+    stacked = jnp.concatenate(stacked + [jnp.zeros((LANES - GROUPS * count, SPAN), F32)], axis=0)
+    turned_ref[...] = jnp.transpose(stacked)
+    spread = jnp.concatenate([turned_ref[pl.ds(q, 8, stride=STEPS), :] for q in range(STEPS)], axis=0).astype(BF16)
+    source = iota((LANES, LANES), 0) - count * (iota((LANES, LANES), 1) // M)
 
     base = column_base().astype(F32)
     y_parts = []
     for q in range(STEPS):
         ypos = (base + (q + 0.5)) / NY - 0.5
         y_parts.append(2.4 * ypos * ypos)
-    for r in range(EXT):
-        here = jnp.dot(spread, (source == r).astype(BF16), preferred_element_type=F32)
-        x_row = jnp.broadcast_to(x_part[r : r + 1], (8, LANES))
-        sine_row = jnp.broadcast_to(along_x[r : r + 1], (8, LANES))
+    for i, e in rows:
+        here = jnp.dot(spread, (source == i).astype(BF16), preferred_element_type=F32)
+        x_row = jnp.broadcast_to(x_part[e : e + 1], (8, LANES))
+        sine_row = jnp.broadcast_to(along_x[e : e + 1], (8, LANES))
         for q in range(STEPS):
             w = (x_row - y_parts[q]) - 0.1 * here[8 * q : 8 * q + 8]
-            w_ref[r, q] = w
-            out_ref[r, q] = (w + shift) * (sine_row * sines[q])
+            write(i, e, q, w, (w + shift) * (sine_row * sines[q]))
+
+
+def prepare_kernel(
+    pert_hbm, seeds_hbm, strip_ref, sines_ref, along_ref, shift_ref, w_ref, out_ref, pert_ref, seeds_ref, turned_ref, sem
+):
+    k = lax.axis_index("xs")
+    pert_copy = pltpu.make_async_copy(pert_hbm, pert_ref, sem.at[0])
+    seeds_copy = pltpu.make_async_copy(seeds_hbm, seeds_ref, sem.at[1])
+    pert_copy.start()
+    seeds_copy.start()
+    seeds_copy.wait()
+    indices = jnp.concatenate([seeds_ref[...]] * GROUPS, axis=1)
+    first, second = indices[0:1].astype(F32), indices[1:2].astype(F32)
+    sines, along_x, shift = sine_tables(k, first, second)
+    for q in range(STEPS):
+        sines_ref[q] = sines[q]
+    along_ref[...] = along_x
+    shift_ref[...] = jnp.broadcast_to(shift, (8, LANES))
+    strip_ref[SENT - 2 : SENT - 1, 0:LANES] = indices[0:1]
+    strip_ref[SENT - 2 : SENT - 1, LANES : 2 * LANES] = indices[1:2]
+    pert_copy.wait()
+    strip_ref[HALO - 1 : HALO - 1 + ROWS, :] = pert_ref[...]
+
+    def write(i, e, q, w, value):
+        w_ref[i, q] = w
+        out_ref[i, q] = value
+
+    rows = [(i, i + HALO) for i in range(ROWS)]
+    first_rows(k, pert_ref[...].astype(F32), rows, sines, along_x, shift, turned_ref, write)
+
+
+def halo(inner_ref, outer_ref):
+    even = lax.axis_index("xs") % 2 == 0
+    before = jnp.where(even, outer_ref[ROWS - HALO :, :], inner_ref[ROWS - HALO :, :])
+    after = jnp.where(even, inner_ref[:HALO, :], outer_ref[:HALO, :])
+    return before, after
+
+
+def assemble_kernel(inner_ref, outer_ref, middle_ref, strip_ref):
+    before, after = halo(inner_ref, outer_ref)
+    strip_ref[...] = middle_ref[...]
+    strip_ref[0 : HALO - 1, :] = before[1:]
+    strip_ref[HALO - 1 + ROWS : SENT - 2, :] = after[: HALO - 1]
 
 
 def beyond(row_first, row_last):
@@ -102,37 +127,48 @@
     return left, right
 
 
-def sweep(k, first_row, count, in_ref, w_ref, out_ref, shifted=0, hamiltonian=False):
-    batch, chunk = count // 2, 4
-
-    def rows(i, carry):
-        r = first_row + i * batch
-        ends = [beyond(in_ref[r + j, 0], in_ref[r + j, STEPS - 1]) for j in range(batch)]
-        factor = {}
-        top, bottom = HALO - 1 - first_row, EXT - HALO - first_row - batch
-        if 0 <= top < batch:
-            factor[top] = jnp.where((i == 0) & (k == 0), 0.0, 1.0)
-        if 0 <= bottom < batch:
-            factor[bottom] = jnp.where((i == 1) & (k == NX // ROWS - 1), 0.0, 1.0) * factor.get(bottom, 1.0)
+def strip_row(i, j):
+    return j + i * (EXT - 1 - 2 * j)
+
+
+def whole(ref):
+    return lambda i, j, q: ref[strip_row(i, j), q]
+
+
+def parted(halo_ref, own_ref):
+    def get(i, j, q):
+        if j < HALO:
+            return halo_ref[j + i * (2 * HALO - 1 - 2 * j), q]
+        return own_ref[strip_row(i, j) - HALO, q]
+
+    return get
+
+
+def sweep(k, margin, source, weight, out_ref, hamiltonian=False):
+    first, stop, chunk = HALO - margin, EXT // 2, 4
+
+    def half(i, carry):
+        ends = {j: beyond(source(i, j, 0), source(i, j, STEPS - 1)) for j in range(first, stop)}
+        inside_grid = jnp.where(k == i * (NX // ROWS - 1), 0.0, 1.0)
         for q0 in range(0, STEPS, chunk):
             inside = range(q0, q0 + chunk)
-            x = {(j, q): in_ref[r + j, q] for j in range(-1, batch + 1) for q in inside}
-            for j in range(batch):
-                x[j, q0 - 1] = in_ref[r + j, q0 - 1] if q0 > 0 else ends[j][0]
-                x[j, q0 + chunk] = in_ref[r + j, q0 + chunk] if q0 + chunk < STEPS else ends[j][1]
-            for j in range(batch):
+            x = {(j, q): source(i, j, q) for j in range(first - 1, stop + 1) for q in inside}
+            for j in range(first, stop):
+                x[j, q0 - 1] = source(i, j, q0 - 1) if q0 > 0 else ends[j][0]
+                x[j, q0 + chunk] = source(i, j, q0 + chunk) if q0 + chunk < STEPS else ends[j][1]
+            for j in range(first, stop):
                 for q in inside:
                     near = (x[j, q - 1] + x[j, q + 1]) + (x[j - 1, q] + x[j + 1, q])
                     if hamiltonian:
-                        value = (13.0 - w_ref[r + j, q]) * x[j, q] - near
+                        value = (13.0 - weight(i, j, q)) * x[j, q] - near
                     else:
-                        value = w_ref[r + j, q] * x[j, q] + near
-                    if j in factor:
-                        value = value * factor[j]
-                    out_ref[r + j - shifted, q] = value
+                        value = weight(i, j, q) * x[j, q] + near
+                    if j == HALO - 1:
+                        value = value * inside_grid
+                    out_ref[strip_row(i, j), q] = value
         return carry
 
-    lax.fori_loop(0, 2, rows, 0)
+    lax.fori_loop(0, 2, half, 0)
 
 
 def blocks(product):
@@ -144,15 +180,24 @@
 
 
 def own_kernel(
-    strip_ref, sines_ref, along_ref, shift_ref, modes_ref, sums_ref, w_ref, pert_ref, one_ref, two_ref
+    inner_ref, outer_ref, sines_ref, along_ref, shift_ref, w_ref, first_ref,
+    modes_ref, sums_ref, halo_w_ref, halo_ref, turned_ref, one_ref, two_ref,
 ):
     k = lax.axis_index("xs")
+
+    def write(i, e, q, w, value):
+        halo_w_ref[i, q] = w
+        halo_ref[i, q] = value
+
+    pert = jnp.concatenate(halo(inner_ref, outer_ref), axis=0).astype(F32)
+    rows = [(i, i if i < HALO else i + ROWS) for i in range(2 * HALO)]
     sines = [sines_ref[q] for q in range(STEPS)]
-    first_trial(k, strip_ref, sines, along_ref[...], shift_ref[...], w_ref, pert_ref, one_ref)
-    sweep(k, 1, EXT - 2, one_ref, w_ref, two_ref)
-    sweep(k, 2, EXT - 4, two_ref, w_ref, one_ref)
-    sweep(k, 3, EXT - 6, one_ref, w_ref, two_ref)
-    sweep(k, 4, ROWS, two_ref, w_ref, one_ref, hamiltonian=True)
+    first_rows(k, pert, rows, sines, along_ref[...], shift_ref[...], turned_ref, write)
+    weight = parted(halo_w_ref, w_ref)
+    sweep(k, 3, parted(halo_ref, first_ref), weight, two_ref)
+    sweep(k, 2, whole(two_ref), weight, one_ref)
+    sweep(k, 1, whole(one_ref), weight, two_ref)
+    sweep(k, 0, whole(two_ref), weight, one_ref, hamiltonian=True)
     field = two_ref[HALO : HALO + ROWS].reshape(ROWS * SPAN, LANES)
     image = one_ref[HALO : HALO + ROWS].reshape(ROWS * SPAN, LANES)
     modes_ref[...] = field
@@ -166,14 +211,21 @@
     sums_ref[...] = jnp.concatenate([gram, ham], axis=1)
 
 
-def next_kernel(strip_ref, modes_ref, own_ref, sums_ref, w_ref, pert_ref, one_ref, two_ref):
+def next_kernel(strip_ref, modes_ref, own_ref, sums_ref, w_ref, turned_ref, one_ref, two_ref):
     k = lax.axis_index("xs")
-    first = strip_ref[EXT : EXT + 1, 0:LANES].astype(F32)
-    second = strip_ref[EXT + 1 : EXT + 2, 0:LANES].astype(F32)
-    first_trial(k, strip_ref, *sine_tables(k, first, second), w_ref, pert_ref, one_ref)
-    sweep(k, 2, EXT - 4, one_ref, w_ref, two_ref)
-    sweep(k, 3, EXT - 6, two_ref, w_ref, one_ref)
-    sweep(k, 4, ROWS, one_ref, w_ref, two_ref)
+    first = strip_ref[SENT - 2 : SENT - 1, 0:LANES].astype(F32)
+    second = strip_ref[SENT - 2 : SENT - 1, LANES : 2 * LANES].astype(F32)
+
+    def write(i, e, q, w, value):
+        w_ref[e, q] = w
+        one_ref[e, q] = value
+
+    rows = [(i, i + 1) for i in range(EXT - 2)]
+    first_rows(k, strip_ref[...].astype(F32), rows, *sine_tables(k, first, second), turned_ref, write)
+    weight = whole(w_ref)
+    sweep(k, 2, whole(one_ref), weight, two_ref)
+    sweep(k, 1, whole(two_ref), weight, one_ref)
+    sweep(k, 0, whole(one_ref), weight, two_ref)
     field = two_ref[HALO : HALO + ROWS].reshape(ROWS * SPAN, LANES)
     high, low = split(field)
     own_high, own_low = split(modes_ref[...])
@@ -289,54 +341,60 @@
     outer = lax.ppermute(pert, "xs", [(i, i - 1 if i % 2 == 0 else i + 1) for i in range(1, strips - 1)])
     vmem = pl.BlockSpec(memory_space=pltpu.VMEM)
     params = pltpu.CompilerParams(vmem_limit_bytes=28 * 2**20)
+    field_shape = (STEPS, 8, LANES)
     middle, *tables = pl.pallas_call(
         prepare_kernel,
         name="prepare",
         out_shape=(
-            jax.ShapeDtypeStruct((32, NY), jnp.int32),
-            jax.ShapeDtypeStruct((STEPS, 8, LANES), F32),
+            jax.ShapeDtypeStruct((SENT, NY), jnp.int32),
+            jax.ShapeDtypeStruct(field_shape, F32),
             jax.ShapeDtypeStruct((EXT, LANES), F32),
             jax.ShapeDtypeStruct((8, LANES), F32),
+            jax.ShapeDtypeStruct((ROWS, *field_shape), F32),
+            jax.ShapeDtypeStruct((ROWS, *field_shape), F32),
         ),
-        in_specs=[vmem, vmem],
-        out_specs=(vmem,) * 4,
-        compiler_params=pltpu.CompilerParams(vmem_limit_bytes=4 * 2**20),
-        cost_estimate=pl.CostEstimate(flops=2**20, bytes_accessed=2**20, transcendentals=2**14),
+        in_specs=[pl.BlockSpec(memory_space=pltpu.HBM)] * 2,
+        out_specs=(vmem,) * 6,
+        scratch_shapes=[
+            pltpu.VMEM((ROWS, NY), jnp.int32),
+            pltpu.VMEM((2, M), jnp.int32),
+            pltpu.VMEM((SPAN, LANES), F32),
+            pltpu.SemaphoreType.DMA((2,)),
+        ],
+        compiler_params=pltpu.CompilerParams(vmem_limit_bytes=12 * 2**20),
+        cost_estimate=pl.CostEstimate(flops=2**26, bytes_accessed=2**22, transcendentals=2**14),
     )(pert, seeds[0].T)
     strip = pl.pallas_call(
         assemble_kernel,
         name="assemble",
-        out_shape=jax.ShapeDtypeStruct((32, NY), jnp.int32),
+        out_shape=jax.ShapeDtypeStruct((SENT, NY), jnp.int32),
         in_specs=[vmem, vmem, vmem],
         out_specs=vmem,
         compiler_params=pltpu.CompilerParams(vmem_limit_bytes=4 * 2**20),
     )(inner, outer, middle)
     following = lax.ppermute(strip, "slab", [((i + 1) % 4, i) for i in range(4)])
 
-    scratch = [
-        pltpu.VMEM((EXT, STEPS, 8, LANES), F32),
-        pltpu.VMEM((SPAN, LANES), F32),
-        pltpu.VMEM((EXT, STEPS, 8, LANES), F32),
-        pltpu.VMEM((EXT, STEPS, 8, LANES), F32),
-    ]
+    trial = pltpu.VMEM((EXT, *field_shape), F32)
+    edges = pltpu.VMEM((2 * HALO, *field_shape), F32)
+    turned = pltpu.VMEM((SPAN, LANES), F32)
     cost = pl.CostEstimate(flops=2**30, bytes_accessed=2**23, transcendentals=0)
     field, own = pl.pallas_call(
         own_kernel,
         name="own_trial",
         out_shape=(jax.ShapeDtypeStruct((ROWS * SPAN, LANES), F32), jax.ShapeDtypeStruct((M, 2 * M), F32)),
-        in_specs=[vmem, vmem, vmem, vmem],
+        in_specs=[vmem] * 7,
         out_specs=(vmem, vmem),
-        scratch_shapes=scratch,
+        scratch_shapes=[edges, edges, turned, trial, trial],
         compiler_params=params,
         cost_estimate=cost,
-    )(strip, *tables)
+    )(inner, outer, *tables)
     sums = pl.pallas_call(
         next_kernel,
         name="next_trial",
         out_shape=jax.ShapeDtypeStruct((M, 4 * M), F32),
         in_specs=[vmem, vmem, vmem],
         out_specs=vmem,
-        scratch_shapes=scratch,
+        scratch_shapes=[trial, turned, trial, trial],
         compiler_params=params,
         cost_estimate=cost,
     )(following, field, own)

time: 47.3 us -> 46.8 us (0.989)
  waiting for transfers between devices: 14 us -> 13.1 us
    ppermute x1, waiting for transfers between devices: 2.13 us -> 1.28 us  [local(): lax.ppermute(pert, 'xs', [(i, i - 1 if i % 2 == 0 else i + 1) for i in ra...]
    pallas_call x1, Pallas kernels: 0.24 us -> 1.09 us  [local(): pl.pallas_call(prepare_kernel, name='prepare', out_shape=(jax.ShapeDtypeS...]
    pallas_call x1, Pallas kernels: 4.18 us -> 3.69 us  [local(): pl.pallas_call(own_kernel, name='own_trial', out_shape=(jax.ShapeDtypeStr...]
  transfers between devices with their start and end apart: 11 -> 11, of which waited for: 7 -> 7; matrix products, arithmetic and copies ran while one was open for 0% -> 0% of each run, Pallas kernels for 10% -> 11%
where the time goes in v5:
time: 46.8 us; the launch traced here: 46.7 us
  starting transfers between devices  19.5 us (42%)
  waiting for transfers between devices  13.1 us (28%)
  Pallas kernels  11.8 us (25%)
  local copies, waits for them, and re-layouts  1.51 us (3%)
  between operations  0.72 us (2%)
    ppermute x8, starting transfers between devices, others(): lax.ppermute(x, 'xs', [(i, i ^ mask) for i in range(64)])  12.7 us
    ppermute x8, waiting for transfers between devices, others(): lax.ppermute(x, 'xs', [(i, i ^ mask) for i in range(64)])  11.8 us
    ppermute x1, starting transfers between devices, local(): lax.ppermute(pert, 'xs', [(i, i - 1 if i % 2 == 0 else i + 1) for i in ra...  3.91 us
    pallas_call x1, Pallas kernels, local(): pl.pallas_call(next_kernel, name='next_trial', out_shape=jax.ShapeDtypeSt...  3.73 us
    pallas_call x1, Pallas kernels, local(): pl.pallas_call(own_kernel, name='own_trial', out_shape=(jax.ShapeDtypeStr...  3.69 us
    pallas_call x1, Pallas kernels, local(): pl.pallas_call(finish_kernel, name='finish', out_shape=(jax.ShapeDtypeStr...  2.89 us
    ppermute x1, starting transfers between devices, local(): lax.ppermute(strip, 'slab', [((i + 1) % 4, i) for i in range(4)])  2.84 us
    unnamed x4, local copies, waits for them, and re-layouts  1.51 us
  transfers between devices with their start and end apart: 11, of which 7 were waited for; matrix products, arithmetic and copies ran while one was open for 0% of the time, Pallas kernels for 11%

profile of v5, /device:TPU:64, one launch (start us, length us, event | category | flops | bytes accessed | tf_op | source)
XLA Modules:
  0.0 46.7 jit_solution(6322564186963902661)
XLA Ops:
  0.6 3.9 %collective-permute-start.1 = (s32[16,1024]{1,0:T(8,128)}, s32[16,1024]{1,0:T(8,128)S(1)}, u32[]{:S(2)}, u32[]{:S(2)}) collective-permute-start(s32[16,1024]{1,0:T(8,128)} %bitcast.7), channel_id=1, source_target_pairs={{1,2},{2,1},{3,4},{4,3},{5,6},{6,5},{7,8},{8,7},{9,10},{10,9},{11,... | collective-permute-start | bytes 196616 | tf_op jit(solution)/shard_map/ppermute | solution.py:341
  4.5 0.1 collective-permute-start
  4.6 0.0 copy-start
  4.7 0.8 %copy-done = s32[1,16,1024]{2,1,0:T(8,128)S(1)} copy-done((s32[1,16,1024]{2,1,0:T(8,128)S(1)}, s32[1,16,1024]{2,1,0:T(8,128)}, u32[]{:S(2)}) %copy-start) | copy-done | bytes 65560
  5.5 0.0 copy-start.1
  5.5 0.7 %copy-done.1 = s32[1,32,2]{1,2,0:T(2,128)S(1)} copy-done((s32[1,32,2]{1,2,0:T(2,128)S(1)}, s32[1,32,2]{1,2,0:T(2,128)}, u32[]{:S(2)}) %copy-start.1) | copy-done | bytes 280
  6.2 1.1 %prepare.1 = (s32[24,1024]{1,0:T(8,128)S(1)}, f32[32,8,128]{2,1,0:T(8,128)S(1)}, f32[24,128]{1,0:T(8,128)S(1)}, f32[8,128]{1,0:T(8,128)S(1)}, f32[16,32,8,128]{3...) custom-call(s32[16,1024]{1,0:T(8,128)S(1)} %bitcast.9, s32[2,32]{1,0:T(2,128)S(1)} %bitcast.10), custom_call_target="tpu_custom_call" | custom-call | flops 67108864 | bytes 4194304 | tf_op jit(solution)/shard_map/prepare/pallas_call | solution.py:345
  7.3 1.3 %collective-permute-done.1.outer_ref = s32[16,1024]{1,0:T(8,128)S(1)} collective-permute-done((s32[16,1024]{1,0:T(8,128)}, s32[16,1024]{1,0:T(8,128)S(1)}, u32[]{:S(2)}, u32[]{:S(2)}) %collective-permute-start.1) | collective-permute-done | bytes 65568 | tf_op jit(solution)/shard_map/ppermute | solution.py:341
  8.5 0.0 collective-permute-done.inner_ref
  8.6 2.8 %collective-permute-start.2 = (s32[24,1024]{1,0:T(8,128)S(1)}, s32[24,1024]{1,0:T(8,128)S(1)}, u32[]{:S(2)}, u32[]{:S(2)}) collective-permute-start(s32[24,1024]{1,0:T(8,128)S(1)} %assemble.1), channel_id=1, source_target_pairs={{64,0},{128,64},{192,128},{0,192},{65,1},{129,65},{193,129},{1,193... | collective-permute-start | bytes 294920 | tf_op jit(solution)/shard_map/ppermute | solution.py:375
  11.4 3.7 %own_trial.1 = (f32[4096,128]{1,0:T(8,128)S(1)}, f32[32,64]{1,0:T(8,128)S(1)}) custom-call(s32[16,1024]{1,0:T(8,128)S(1)} %collective-permute-done.inner_ref, s32[16,1024]{1,0:T(8,128)S(1)} %collective-permute-done.1.outer_ref, f32[32,8,128]{2,1,0:T(8,128)S(1)} %get-tuple-element.15.sines_ref, f32[24,128]{1,0:T(8,128)S(1)} %get-tuple-element.16.along_ref, ...), custom_call_target="tpu_custom_call" | custom-call | flops 1073741824 | bytes 8388608 | tf_op jit(solution)/shard_map/own_trial/pallas_call | solution.py:381
  15.1 0.0 collective-permute-done.2.strip_ref
  15.1 3.7 %next_trial.1 = f32[32,128]{1,0:T(8,128)S(1)} custom-call(s32[24,1024]{1,0:T(8,128)S(1)} %collective-permute-done.2.strip_ref, f32[4096,128]{1,0:T(8,128)S(1)} %get-tuple-element.20.modes_ref, f32[32,64]{1,0:T(8,128)S(1)} %get-tuple-element.21.own_ref), custom_call_target="tpu_custom_call" | custom-call | flops 1073741824 | bytes 8388608 | tf_op jit(solution)/shard_map/next_trial/pallas_call | solution.py:391
  18.9 0.1 collective-permute-start.3
  19.0 1.2 %collective-permute-done.3 = f32[32,128]{1,0:T(8,128)S(1)} collective-permute-done((f32[32,128]{1,0:T(8,128)S(1)}, f32[32,128]{1,0:T(8,128)S(1)}, u32[]{:S(2)}, u32[]{:S(2)}) %collective-permute-start.3) | collective-permute-done | bytes 16416 | tf_op jit(solution)/shard_map/ppermute | solution.py:328
  20.1 2.2 %collective-permute-start.6 = (f32[32,128]{1,0:T(8,128)S(1)}, f32[32,128]{1,0:T(8,128)S(1)}, u32[]{:S(2)}, u32[]{:S(2)}) collective-permute-start(f32[32,128]{1,0:T(8,128)S(1)} %add.24), channel_id=1, source_target_pairs={{0,6},{1,7},{2,4},{3,5},{4,2},{5,3},{6,0},{7,1},{8,14},{9,15},{10,... | collective-permute-start | bytes 49160 | tf_op jit(solution)/shard_map/ppermute | solution.py:328
  22.4 0.0 collective-permute-start.5
  22.4 1.9 %collective-permute-start.4 = (f32[32,128]{1,0:T(8,128)S(1)}, f32[32,128]{1,0:T(8,128)S(1)}, u32[]{:S(2)}, u32[]{:S(2)}) collective-permute-start(f32[32,128]{1,0:T(8,128)S(1)} %add.24), channel_id=1, source_target_pairs={{0,2},{1,3},{2,0},{3,1},{4,6},{5,7},{6,4},{7,5},{8,10},{9,11},{10,... | collective-permute-start | bytes 49160 | tf_op jit(solution)/shard_map/ppermute | solution.py:328
  24.2 0.9 %collective-permute-done.6 = f32[32,128]{1,0:T(8,128)S(1)} collective-permute-done((f32[32,128]{1,0:T(8,128)S(1)}, f32[32,128]{1,0:T(8,128)S(1)}, u32[]{:S(2)}, u32[]{:S(2)}) %collective-permute-start.6) | collective-permute-done | bytes 16416 | tf_op jit(solution)/shard_map/ppermute | solution.py:328
  25.1 2.5 %collective-permute-done.5 = f32[32,128]{1,0:T(8,128)S(1)} collective-permute-done((f32[32,128]{1,0:T(8,128)S(1)}, f32[32,128]{1,0:T(8,128)S(1)}, u32[]{:S(2)}, u32[]{:S(2)}) %collective-permute-start.5) | collective-permute-done | bytes 16416 | tf_op jit(solution)/shard_map/ppermute | solution.py:328
  27.6 0.0 collective-permute-done.4
  27.6 0.2 collective-permute-start.9
  27.8 5.4 %collective-permute-start.8 = (f32[32,128]{1,0:T(8,128)S(1)}, f32[32,128]{1,0:T(8,128)S(1)}, u32[]{:S(2)}, u32[]{:S(2)}) collective-permute-start(f32[32,128]{1,0:T(8,128)S(1)} %add_add_fusion.1), channel_id=1, source_target_pairs={{0,16},{1,17},{2,18},{3,19},{4,20},{5,21},{6,22},{7,23},{8,24},{9,... | collective-permute-start | bytes 49160 | tf_op jit(solution)/shard_map/ppermute | solution.py:328
  33.2 0.0 collective-permute-start.7
  33.2 0.0 collective-permute-done.9
  33.2 1.9 %collective-permute-done.8 = f32[32,128]{1,0:T(8,128)S(1)} collective-permute-done((f32[32,128]{1,0:T(8,128)S(1)}, f32[32,128]{1,0:T(8,128)S(1)}, u32[]{:S(2)}, u32[]{:S(2)}) %collective-permute-start.8) | collective-permute-done | bytes 16416 | tf_op jit(solution)/shard_map/ppermute | solution.py:328
  35.1 1.9 %collective-permute-done.7 = f32[32,128]{1,0:T(8,128)S(1)} collective-permute-done((f32[32,128]{1,0:T(8,128)S(1)}, f32[32,128]{1,0:T(8,128)S(1)}, u32[]{:S(2)}, u32[]{:S(2)}) %collective-permute-start.7) | collective-permute-done | bytes 16416 | tf_op jit(solution)/shard_map/ppermute | solution.py:328
  36.9 2.9 %collective-permute-start.10 = (f32[32,128]{1,0:T(8,128)S(1)}, f32[32,128]{1,0:T(8,128)S(1)}, u32[]{:S(2)}, u32[]{:S(2)}) collective-permute-start(f32[32,128]{1,0:T(8,128)S(1)} %add_add_fusion), channel_id=1, source_target_pairs={{0,56},{1,57},{2,58},{3,59},{4,60},{5,61},{6,62},{7,63},{8,48},{9,... | collective-permute-start | bytes 49160 | tf_op jit(solution)/shard_map/ppermute | solution.py:328
  39.8 0.4 parts.1.parts_ref
  40.2 3.6 %collective-permute-done.10 = f32[32,128]{1,0:T(8,128)S(1)} collective-permute-done((f32[32,128]{1,0:T(8,128)S(1)}, f32[32,128]{1,0:T(8,128)S(1)}, u32[]{:S(2)}, u32[]{:S(2)}) %collective-permute-start.10) | collective-permute-done | bytes 16416 | tf_op jit(solution)/shard_map/ppermute | solution.py:328
  43.8 2.9 %finish.1 = (f32[32,16,1024]{2,1,0:T(8,128)}, f32[32,32]{1,0:T(8,128)}, f32[32,32]{1,0:T(8,128)}) custom-call(f32[32,128]{1,0:T(8,128)S(1)} %add.31.sums_ref, bf16[16,256,256]{2,1,0:T(8,128)(2,1)S(1)} %parts.1.parts_ref), custom_call_target="tpu_custom_call" | custom-call | flops 268435456 | bytes 8388608 | tf_op jit(solution)/shard_map/finish/pallas_call | solution.py:411
  (5 shorter events, 0.0 us)
Async XLA Ops:
  0.6 7.9 %collective-permute-start.1 = (s32[16,1024]{1,0:T(8,128)}, s32[16,1024]{1,0:T(8,128)S(1)}, u32[]{:S(2)}, u32[]{:S(2)}) collective-permute-start(s32[16,1024]{1,0:T(8,128)} %bitcast.7), channel_id=1, source_target_pairs={{1,2},{2,1},{3,4},{4,3},{5,6},{6,5},{7,8},{8,7},{9,10},{10,9},{11,... | collective-permute-start | bytes 196616 | tf_op jit(solution)/shard_map/ppermute | solution.py:341
  4.5 4.0 %collective-permute-start = (s32[16,1024]{1,0:T(8,128)}, s32[16,1024]{1,0:T(8,128)S(1)}, u32[]{:S(2)}, u32[]{:S(2)}) collective-permute-start(s32[16,1024]{1,0:T(8,128)} %bitcast.8), channel_id=1, source_target_pairs={{0,1},{1,0},{2,3},{3,2},{4,5},{5,4},{6,7},{7,6},{8,9},{9,8},{10,11... | collective-permute-start | bytes 196616 | tf_op jit(solution)/shard_map/ppermute | solution.py:340
  4.6 0.8 %copy-start = (s32[1,16,1024]{2,1,0:T(8,128)S(1)}, s32[1,16,1024]{2,1,0:T(8,128)}, u32[]{:S(2)}) copy-start(s32[1,16,1024]{2,1,0:T(8,128)} %param.2) | copy-start | bytes 196612
  5.5 0.7 %copy-start.1 = (s32[1,32,2]{1,2,0:T(2,128)S(1)}, s32[1,32,2]{1,2,0:T(2,128)}, u32[]{:S(2)}) copy-start(s32[1,32,2]{1,2,0:T(2,128)} %param.3) | copy-start | bytes 772
  8.6 6.5 %collective-permute-start.2 = (s32[24,1024]{1,0:T(8,128)S(1)}, s32[24,1024]{1,0:T(8,128)S(1)}, u32[]{:S(2)}, u32[]{:S(2)}) collective-permute-start(s32[24,1024]{1,0:T(8,128)S(1)} %assemble.1), channel_id=1, source_target_pairs={{64,0},{128,64},{192,128},{0,192},{65,1},{129,65},{193,129},{1,193... | collective-permute-start | bytes 294920 | tf_op jit(solution)/shard_map/ppermute | solution.py:375
  18.9 1.3 %collective-permute-start.3 = (f32[32,128]{1,0:T(8,128)S(1)}, f32[32,128]{1,0:T(8,128)S(1)}, u32[]{:S(2)}, u32[]{:S(2)}) collective-permute-start(f32[32,128]{1,0:T(8,128)S(1)} %next_trial.1), channel_id=1, source_target_pairs={{0,1},{1,0},{2,3},{3,2},{4,5},{5,4},{6,7},{7,6},{8,9},{9,8},{10,11... | collective-permute-start | bytes 49160 | tf_op jit(solution)/shard_map/ppermute | solution.py:328
  20.1 4.9 %collective-permute-start.6 = (f32[32,128]{1,0:T(8,128)S(1)}, f32[32,128]{1,0:T(8,128)S(1)}, u32[]{:S(2)}, u32[]{:S(2)}) collective-permute-start(f32[32,128]{1,0:T(8,128)S(1)} %add.24), channel_id=1, source_target_pairs={{0,6},{1,7},{2,4},{3,5},{4,2},{5,3},{6,0},{7,1},{8,14},{9,15},{10,... | collective-permute-start | bytes 49160 | tf_op jit(solution)/shard_map/ppermute | solution.py:328
  22.4 5.2 %collective-permute-start.5 = (f32[32,128]{1,0:T(8,128)S(1)}, f32[32,128]{1,0:T(8,128)S(1)}, u32[]{:S(2)}, u32[]{:S(2)}) collective-permute-start(f32[32,128]{1,0:T(8,128)S(1)} %add.24), channel_id=1, source_target_pairs={{0,4},{1,5},{2,6},{3,7},{4,0},{5,1},{6,2},{7,3},{8,12},{9,13},{10,... | collective-permute-start | bytes 49160 | tf_op jit(solution)/shard_map/ppermute | solution.py:328
  22.4 5.2 %collective-permute-start.4 = (f32[32,128]{1,0:T(8,128)S(1)}, f32[32,128]{1,0:T(8,128)S(1)}, u32[]{:S(2)}, u32[]{:S(2)}) collective-permute-start(f32[32,128]{1,0:T(8,128)S(1)} %add.24), channel_id=1, source_target_pairs={{0,2},{1,3},{2,0},{3,1},{4,6},{5,7},{6,4},{7,5},{8,10},{9,11},{10,... | collective-permute-start | bytes 49160 | tf_op jit(solution)/shard_map/ppermute | solution.py:328
  27.6 5.6 %collective-permute-start.9 = (f32[32,128]{1,0:T(8,128)S(1)}, f32[32,128]{1,0:T(8,128)S(1)}, u32[]{:S(2)}, u32[]{:S(2)}) collective-permute-start(f32[32,128]{1,0:T(8,128)S(1)} %add_add_fusion.1), channel_id=1, source_target_pairs={{0,24},{1,25},{2,26},{3,27},{4,28},{5,29},{6,30},{7,31},{8,16},{9,... | collective-permute-start | bytes 49160 | tf_op jit(solution)/shard_map/ppermute | solution.py:328
  27.8 7.3 %collective-permute-start.8 = (f32[32,128]{1,0:T(8,128)S(1)}, f32[32,128]{1,0:T(8,128)S(1)}, u32[]{:S(2)}, u32[]{:S(2)}) collective-permute-start(f32[32,128]{1,0:T(8,128)S(1)} %add_add_fusion.1), channel_id=1, source_target_pairs={{0,16},{1,17},{2,18},{3,19},{4,20},{5,21},{6,22},{7,23},{8,24},{9,... | collective-permute-start | bytes 49160 | tf_op jit(solution)/shard_map/ppermute | solution.py:328
  33.2 3.7 %collective-permute-start.7 = (f32[32,128]{1,0:T(8,128)S(1)}, f32[32,128]{1,0:T(8,128)S(1)}, u32[]{:S(2)}, u32[]{:S(2)}) collective-permute-start(f32[32,128]{1,0:T(8,128)S(1)} %add_add_fusion.1), channel_id=1, source_target_pairs={{0,8},{1,9},{2,10},{3,11},{4,12},{5,13},{6,14},{7,15},{8,0},{9,1},... | collective-permute-start | bytes 49160 | tf_op jit(solution)/shard_map/ppermute | solution.py:328
  36.9 6.8 %collective-permute-start.10 = (f32[32,128]{1,0:T(8,128)S(1)}, f32[32,128]{1,0:T(8,128)S(1)}, u32[]{:S(2)}, u32[]{:S(2)}) collective-permute-start(f32[32,128]{1,0:T(8,128)S(1)} %add_add_fusion), channel_id=1, source_target_pairs={{0,56},{1,57},{2,58},{3,59},{4,60},{5,61},{6,62},{7,63},{8,48},{9,... | collective-permute-start | bytes 49160 | tf_op jit(solution)/shard_map/ppermute | solution.py:328

commit v6 on v5

--- a/solution.py
+++ b/solution.py
@@ -54,25 +54,42 @@
 def first_rows(k, pert, rows, sines, along_x, shift, turned_ref, write):
     count = pert.shape[0]
     xpos = ((iota((EXT, LANES), 0) + (k * ROWS - HALO)).astype(F32) + 0.5) / NX - 0.5
-    x_part = 9.0 - 4.0 * (xpos * xpos + 0.5 * xpos)
+    x_terms = thirds(10.0 * (9.0 - 4.0 * (xpos * xpos + 0.5 * xpos)))
     stacked = [pert[:, g * SPAN : (g + 1) * SPAN] for g in range(GROUPS)]
     stacked = jnp.concatenate(stacked + [jnp.zeros((LANES - GROUPS * count, SPAN), F32)], axis=0)
     turned_ref[...] = jnp.transpose(stacked)
-    spread = jnp.concatenate([turned_ref[pl.ds(q, 8, stride=STEPS), :] for q in range(STEPS)], axis=0).astype(BF16)
-    source = iota((LANES, LANES), 0) - count * (iota((LANES, LANES), 1) // M)
-
-    base = column_base().astype(F32)
-    y_parts = []
+
+    lane, s = iota((8, LANES), 1), iota((8, LANES), 0)
+    term = lane % 4
+    base = ((lane - 96) // 4 * SPAN + s * STEPS).astype(F32)
+    spread = []
     for q in range(STEPS):
         ypos = (base + (q + 0.5)) / NY - 0.5
-        y_parts.append(2.4 * ypos * ypos)
+        one, two, three = thirds(24.0 * ypos * ypos)
+        y_terms = jnp.where(term == 0, one, jnp.where(term == 1, two, jnp.where(term == 2, three, 0.0)))
+        extra = jnp.where(lane < 96, 0.0, jnp.where(lane < 112, y_terms, jnp.where(lane < 115, 1.0, 0.0)))
+        spread.append(turned_ref[pl.ds(q, 8, stride=STEPS), :] + extra)
+    spread = jnp.concatenate(spread, axis=0).astype(BF16)
+
+    line, group = iota((112, LANES), 0), iota((112, LANES), 1) // M
+    source = line - count * group
+    y_pick = jnp.where((line >= 96) & ((line - 96) // 4 == group), -1.0, 0.0)
     for i, e in rows:
-        here = jnp.dot(spread, (source == i).astype(BF16), preferred_element_type=F32)
-        x_row = jnp.broadcast_to(x_part[e : e + 1], (8, LANES))
+        pick = jnp.where(source == i, -1.0, y_pick)
+        parts = [jnp.broadcast_to(part[e : e + 1], (8, LANES)) for part in x_terms]
+        x_pick = jnp.where(s == 0, parts[0], jnp.where(s == 1, parts[1], jnp.where(s == 2, parts[2], 0.0)))
+        pick = jnp.concatenate([pick, x_pick, jnp.zeros((8, LANES), F32)], axis=0).astype(BF16)
+        here = jnp.dot(spread, pick, preferred_element_type=F32)
         sine_row = jnp.broadcast_to(along_x[e : e + 1], (8, LANES))
         for q in range(STEPS):
-            w = (x_row - y_parts[q]) - 0.1 * here[8 * q : 8 * q + 8]
+            w = 0.1 * here[8 * q : 8 * q + 8]
             write(i, e, q, w, (w + shift) * (sine_row * sines[q]))
+
+
+def thirds(x):
+    one = x.astype(BF16).astype(F32)
+    two = (x - one).astype(BF16).astype(F32)
+    return one, two, (x - one) - two
 
 
 def prepare_kernel(
@@ -229,11 +246,11 @@
     field = two_ref[HALO : HALO + ROWS].reshape(ROWS * SPAN, LANES)
     high, low = split(field)
     own_high, own_low = split(modes_ref[...])
-    main = dot_cells(jnp.concatenate([high, own_high], axis=1), jnp.concatenate([high, low], axis=1))
-    rest = blocks(dot_cells(own_low, high))
-    cross = blocks(main[0:LANES, LANES:])
-    gram = blocks(main[0:LANES, 0:LANES]) + (cross + cross.T)
-    across = blocks(main[LANES:, 0:LANES]) + (blocks(main[LANES:, LANES:]) + rest)
+    main = dot_cells(high, jnp.concatenate([high, low, own_high, own_low], axis=1))
+    rest = blocks(dot_cells(low, own_high))
+    cross = blocks(main[:, LANES : 2 * LANES])
+    gram = blocks(main[:, 0:LANES]) + (cross + cross.T)
+    across = blocks(main[:, 2 * LANES : 3 * LANES]) + (blocks(main[:, 3 * LANES :]) + rest)
     sums_ref[...] = jnp.concatenate([own_ref[...], gram, across], axis=1)
 
 
@@ -316,7 +333,7 @@
     image, across = sums[:, M : 2 * M], sums[:, 3 * M : 4 * M]
     small_ref[0] = exact(exact(own, image), own.T)
     has_next = lax.axis_index("slab") < lax.axis_size("slab") - 1
-    small_ref[1] = jnp.where(has_next, exact(exact(own, across), following.T), 0.0)
+    small_ref[1] = jnp.where(has_next, exact(exact(own, across.T), following.T), 0.0)
     send(small_ref.at[0], proj_ref)
     send(small_ref.at[1], corr_ref)
     for copy in copies:

time: 46.8 us -> 46.6 us (level)
  no operation moved by 1% of the time
where the time goes in v6:
time: 46.6 us; the launch traced here: 46.5 us
  starting transfers between devices  19.5 us (42%)
  waiting for transfers between devices  13.2 us (28%)
  Pallas kernels  11.5 us (25%)
  local copies, waits for them, and re-layouts  1.51 us (3%)
  between operations  0.72 us (2%)
    ppermute x8, starting transfers between devices, others(): lax.ppermute(x, 'xs', [(i, i ^ mask) for i in range(64)])  12.7 us
    ppermute x8, waiting for transfers between devices, others(): lax.ppermute(x, 'xs', [(i, i ^ mask) for i in range(64)])  11.8 us
    ppermute x1, starting transfers between devices, local(): lax.ppermute(pert, 'xs', [(i, i - 1 if i % 2 == 0 else i + 1) for i in ra...  3.91 us
    pallas_call x1, Pallas kernels, local(): pl.pallas_call(own_kernel, name='own_trial', out_shape=(jax.ShapeDtypeStr...  3.7 us
    pallas_call x1, Pallas kernels, local(): pl.pallas_call(next_kernel, name='next_trial', out_shape=jax.ShapeDtypeSt...  3.56 us
    pallas_call x1, Pallas kernels, local(): pl.pallas_call(finish_kernel, name='finish', out_shape=(jax.ShapeDtypeStr...  2.86 us
    ppermute x1, starting transfers between devices, local(): lax.ppermute(strip, 'slab', [((i + 1) % 4, i) for i in range(4)])  2.84 us
    unnamed x4, local copies, waits for them, and re-layouts  1.51 us
  transfers between devices with their start and end apart: 11, of which 7 were waited for; matrix products, arithmetic and copies ran while one was open for 0% of the time, Pallas kernels for 11%

profile of v6, /device:TPU:64, one launch (start us, length us, event | category | flops | bytes accessed | tf_op | source)
XLA Modules:
  0.0 46.5 jit_solution(11360984039636757467)
XLA Ops:
  0.6 3.9 %collective-permute-start.1 = (s32[16,1024]{1,0:T(8,128)}, s32[16,1024]{1,0:T(8,128)S(1)}, u32[]{:S(2)}, u32[]{:S(2)}) collective-permute-start(s32[16,1024]{1,0:T(8,128)} %bitcast.7), channel_id=1, source_target_pairs={{1,2},{2,1},{3,4},{4,3},{5,6},{6,5},{7,8},{8,7},{9,10},{10,9},{11,... | collective-permute-start | bytes 196616 | tf_op jit(solution)/shard_map/ppermute | solution.py:358
  4.5 0.1 collective-permute-start
  4.6 0.0 copy-start
  4.7 0.8 %copy-done = s32[1,16,1024]{2,1,0:T(8,128)S(1)} copy-done((s32[1,16,1024]{2,1,0:T(8,128)S(1)}, s32[1,16,1024]{2,1,0:T(8,128)}, u32[]{:S(2)}) %copy-start) | copy-done | bytes 65560
  5.5 0.0 copy-start.1
  5.5 0.7 %copy-done.1 = s32[1,32,2]{1,2,0:T(2,128)S(1)} copy-done((s32[1,32,2]{1,2,0:T(2,128)S(1)}, s32[1,32,2]{1,2,0:T(2,128)}, u32[]{:S(2)}) %copy-start.1) | copy-done | bytes 280
  6.2 1.0 %prepare.1 = (s32[24,1024]{1,0:T(8,128)S(1)}, f32[32,8,128]{2,1,0:T(8,128)S(1)}, f32[24,128]{1,0:T(8,128)S(1)}, f32[8,128]{1,0:T(8,128)S(1)}, f32[16,32,8,128]{3...) custom-call(s32[16,1024]{1,0:T(8,128)S(1)} %bitcast.9, s32[2,32]{1,0:T(2,128)S(1)} %bitcast.10), custom_call_target="tpu_custom_call" | custom-call | flops 67108864 | bytes 4194304 | tf_op jit(solution)/shard_map/prepare/pallas_call | solution.py:362
  7.2 1.4 %collective-permute-done.1.outer_ref = s32[16,1024]{1,0:T(8,128)S(1)} collective-permute-done((s32[16,1024]{1,0:T(8,128)}, s32[16,1024]{1,0:T(8,128)S(1)}, u32[]{:S(2)}, u32[]{:S(2)}) %collective-permute-start.1) | collective-permute-done | bytes 65568 | tf_op jit(solution)/shard_map/ppermute | solution.py:358
  8.5 0.0 collective-permute-done.inner_ref
  8.6 2.8 %collective-permute-start.2 = (s32[24,1024]{1,0:T(8,128)S(1)}, s32[24,1024]{1,0:T(8,128)S(1)}, u32[]{:S(2)}, u32[]{:S(2)}) collective-permute-start(s32[24,1024]{1,0:T(8,128)S(1)} %assemble.1), channel_id=1, source_target_pairs={{64,0},{128,64},{192,128},{0,192},{65,1},{129,65},{193,129},{1,193... | collective-permute-start | bytes 294920 | tf_op jit(solution)/shard_map/ppermute | solution.py:392
  11.4 3.7 %own_trial.1 = (f32[4096,128]{1,0:T(8,128)S(1)}, f32[32,64]{1,0:T(8,128)S(1)}) custom-call(s32[16,1024]{1,0:T(8,128)S(1)} %collective-permute-done.inner_ref, s32[16,1024]{1,0:T(8,128)S(1)} %collective-permute-done.1.outer_ref, f32[32,8,128]{2,1,0:T(8,128)S(1)} %get-tuple-element.15.sines_ref, f32[24,128]{1,0:T(8,128)S(1)} %get-tuple-element.16.along_ref, ...), custom_call_target="tpu_custom_call" | custom-call | flops 1073741824 | bytes 8388608 | tf_op jit(solution)/shard_map/own_trial/pallas_call | solution.py:398
  15.1 0.0 collective-permute-done.2.strip_ref
  15.1 3.6 %next_trial.1 = f32[32,128]{1,0:T(8,128)S(1)} custom-call(s32[24,1024]{1,0:T(8,128)S(1)} %collective-permute-done.2.strip_ref, f32[4096,128]{1,0:T(8,128)S(1)} %get-tuple-element.20.modes_ref, f32[32,64]{1,0:T(8,128)S(1)} %get-tuple-element.21.own_ref), custom_call_target="tpu_custom_call" | custom-call | flops 1073741824 | bytes 8388608 | tf_op jit(solution)/shard_map/next_trial/pallas_call | solution.py:408
  18.7 0.1 collective-permute-start.3
  18.8 1.2 %collective-permute-done.3 = f32[32,128]{1,0:T(8,128)S(1)} collective-permute-done((f32[32,128]{1,0:T(8,128)S(1)}, f32[32,128]{1,0:T(8,128)S(1)}, u32[]{:S(2)}, u32[]{:S(2)}) %collective-permute-start.3) | collective-permute-done | bytes 16416 | tf_op jit(solution)/shard_map/ppermute | solution.py:345
  20.0 2.2 %collective-permute-start.6 = (f32[32,128]{1,0:T(8,128)S(1)}, f32[32,128]{1,0:T(8,128)S(1)}, u32[]{:S(2)}, u32[]{:S(2)}) collective-permute-start(f32[32,128]{1,0:T(8,128)S(1)} %add.24), channel_id=1, source_target_pairs={{0,6},{1,7},{2,4},{3,5},{4,2},{5,3},{6,0},{7,1},{8,14},{9,15},{10,... | collective-permute-start | bytes 49160 | tf_op jit(solution)/shard_map/ppermute | solution.py:345
  22.2 0.0 collective-permute-start.5
  22.2 1.9 %collective-permute-start.4 = (f32[32,128]{1,0:T(8,128)S(1)}, f32[32,128]{1,0:T(8,128)S(1)}, u32[]{:S(2)}, u32[]{:S(2)}) collective-permute-start(f32[32,128]{1,0:T(8,128)S(1)} %add.24), channel_id=1, source_target_pairs={{0,2},{1,3},{2,0},{3,1},{4,6},{5,7},{6,4},{7,5},{8,10},{9,11},{10,... | collective-permute-start | bytes 49160 | tf_op jit(solution)/shard_map/ppermute | solution.py:345
  24.1 0.9 %collective-permute-done.6 = f32[32,128]{1,0:T(8,128)S(1)} collective-permute-done((f32[32,128]{1,0:T(8,128)S(1)}, f32[32,128]{1,0:T(8,128)S(1)}, u32[]{:S(2)}, u32[]{:S(2)}) %collective-permute-start.6) | collective-permute-done | bytes 16416 | tf_op jit(solution)/shard_map/ppermute | solution.py:345
  24.9 2.5 %collective-permute-done.5 = f32[32,128]{1,0:T(8,128)S(1)} collective-permute-done((f32[32,128]{1,0:T(8,128)S(1)}, f32[32,128]{1,0:T(8,128)S(1)}, u32[]{:S(2)}, u32[]{:S(2)}) %collective-permute-start.5) | collective-permute-done | bytes 16416 | tf_op jit(solution)/shard_map/ppermute | solution.py:345
  27.4 0.0 collective-permute-done.4
  27.5 0.2 collective-permute-start.9
  27.6 5.4 %collective-permute-start.8 = (f32[32,128]{1,0:T(8,128)S(1)}, f32[32,128]{1,0:T(8,128)S(1)}, u32[]{:S(2)}, u32[]{:S(2)}) collective-permute-start(f32[32,128]{1,0:T(8,128)S(1)} %add_add_fusion.1), channel_id=1, source_target_pairs={{0,16},{1,17},{2,18},{3,19},{4,20},{5,21},{6,22},{7,23},{8,24},{9,... | collective-permute-start | bytes 49160 | tf_op jit(solution)/shard_map/ppermute | solution.py:345
  33.0 0.0 collective-permute-start.7
  33.0 0.0 collective-permute-done.9
  33.0 1.9 %collective-permute-done.8 = f32[32,128]{1,0:T(8,128)S(1)} collective-permute-done((f32[32,128]{1,0:T(8,128)S(1)}, f32[32,128]{1,0:T(8,128)S(1)}, u32[]{:S(2)}, u32[]{:S(2)}) %collective-permute-start.8) | collective-permute-done | bytes 16416 | tf_op jit(solution)/shard_map/ppermute | solution.py:345
  34.9 1.9 %collective-permute-done.7 = f32[32,128]{1,0:T(8,128)S(1)} collective-permute-done((f32[32,128]{1,0:T(8,128)S(1)}, f32[32,128]{1,0:T(8,128)S(1)}, u32[]{:S(2)}, u32[]{:S(2)}) %collective-permute-start.7) | collective-permute-done | bytes 16416 | tf_op jit(solution)/shard_map/ppermute | solution.py:345
  36.8 2.9 %collective-permute-start.10 = (f32[32,128]{1,0:T(8,128)S(1)}, f32[32,128]{1,0:T(8,128)S(1)}, u32[]{:S(2)}, u32[]{:S(2)}) collective-permute-start(f32[32,128]{1,0:T(8,128)S(1)} %add_add_fusion), channel_id=1, source_target_pairs={{0,56},{1,57},{2,58},{3,59},{4,60},{5,61},{6,62},{7,63},{8,48},{9,... | collective-permute-start | bytes 49160 | tf_op jit(solution)/shard_map/ppermute | solution.py:345
  39.7 0.4 parts.1.parts_ref
  40.1 3.6 %collective-permute-done.10 = f32[32,128]{1,0:T(8,128)S(1)} collective-permute-done((f32[32,128]{1,0:T(8,128)S(1)}, f32[32,128]{1,0:T(8,128)S(1)}, u32[]{:S(2)}, u32[]{:S(2)}) %collective-permute-start.10) | collective-permute-done | bytes 16416 | tf_op jit(solution)/shard_map/ppermute | solution.py:345
  43.6 2.9 %finish.1 = (f32[32,16,1024]{2,1,0:T(8,128)}, f32[32,32]{1,0:T(8,128)}, f32[32,32]{1,0:T(8,128)}) custom-call(f32[32,128]{1,0:T(8,128)S(1)} %add.31.sums_ref, bf16[16,256,256]{2,1,0:T(8,128)(2,1)S(1)} %parts.1.parts_ref), custom_call_target="tpu_custom_call" | custom-call | flops 268435456 | bytes 8388608 | tf_op jit(solution)/shard_map/finish/pallas_call | solution.py:428
  (5 shorter events, 0.0 us)
Async XLA Ops:
  0.6 7.9 %collective-permute-start.1 = (s32[16,1024]{1,0:T(8,128)}, s32[16,1024]{1,0:T(8,128)S(1)}, u32[]{:S(2)}, u32[]{:S(2)}) collective-permute-start(s32[16,1024]{1,0:T(8,128)} %bitcast.7), channel_id=1, source_target_pairs={{1,2},{2,1},{3,4},{4,3},{5,6},{6,5},{7,8},{8,7},{9,10},{10,9},{11,... | collective-permute-start | bytes 196616 | tf_op jit(solution)/shard_map/ppermute | solution.py:358
  4.5 4.0 %collective-permute-start = (s32[16,1024]{1,0:T(8,128)}, s32[16,1024]{1,0:T(8,128)S(1)}, u32[]{:S(2)}, u32[]{:S(2)}) collective-permute-start(s32[16,1024]{1,0:T(8,128)} %bitcast.8), channel_id=1, source_target_pairs={{0,1},{1,0},{2,3},{3,2},{4,5},{5,4},{6,7},{7,6},{8,9},{9,8},{10,11... | collective-permute-start | bytes 196616 | tf_op jit(solution)/shard_map/ppermute | solution.py:357
  4.6 0.8 %copy-start = (s32[1,16,1024]{2,1,0:T(8,128)S(1)}, s32[1,16,1024]{2,1,0:T(8,128)}, u32[]{:S(2)}) copy-start(s32[1,16,1024]{2,1,0:T(8,128)} %param.2) | copy-start | bytes 196612
  5.5 0.7 %copy-start.1 = (s32[1,32,2]{1,2,0:T(2,128)S(1)}, s32[1,32,2]{1,2,0:T(2,128)}, u32[]{:S(2)}) copy-start(s32[1,32,2]{1,2,0:T(2,128)} %param.3) | copy-start | bytes 772
  8.6 6.6 %collective-permute-start.2 = (s32[24,1024]{1,0:T(8,128)S(1)}, s32[24,1024]{1,0:T(8,128)S(1)}, u32[]{:S(2)}, u32[]{:S(2)}) collective-permute-start(s32[24,1024]{1,0:T(8,128)S(1)} %assemble.1), channel_id=1, source_target_pairs={{64,0},{128,64},{192,128},{0,192},{65,1},{129,65},{193,129},{1,193... | collective-permute-start | bytes 294920 | tf_op jit(solution)/shard_map/ppermute | solution.py:392
  18.7 1.3 %collective-permute-start.3 = (f32[32,128]{1,0:T(8,128)S(1)}, f32[32,128]{1,0:T(8,128)S(1)}, u32[]{:S(2)}, u32[]{:S(2)}) collective-permute-start(f32[32,128]{1,0:T(8,128)S(1)} %next_trial.1), channel_id=1, source_target_pairs={{0,1},{1,0},{2,3},{3,2},{4,5},{5,4},{6,7},{7,6},{8,9},{9,8},{10,11... | collective-permute-start | bytes 49160 | tf_op jit(solution)/shard_map/ppermute | solution.py:345
  20.0 4.9 %collective-permute-start.6 = (f32[32,128]{1,0:T(8,128)S(1)}, f32[32,128]{1,0:T(8,128)S(1)}, u32[]{:S(2)}, u32[]{:S(2)}) collective-permute-start(f32[32,128]{1,0:T(8,128)S(1)} %add.24), channel_id=1, source_target_pairs={{0,6},{1,7},{2,4},{3,5},{4,2},{5,3},{6,0},{7,1},{8,14},{9,15},{10,... | collective-permute-start | bytes 49160 | tf_op jit(solution)/shard_map/ppermute | solution.py:345
  22.2 5.2 %collective-permute-start.5 = (f32[32,128]{1,0:T(8,128)S(1)}, f32[32,128]{1,0:T(8,128)S(1)}, u32[]{:S(2)}, u32[]{:S(2)}) collective-permute-start(f32[32,128]{1,0:T(8,128)S(1)} %add.24), channel_id=1, source_target_pairs={{0,4},{1,5},{2,6},{3,7},{4,0},{5,1},{6,2},{7,3},{8,12},{9,13},{10,... | collective-permute-start | bytes 49160 | tf_op jit(solution)/shard_map/ppermute | solution.py:345
  22.2 5.2 %collective-permute-start.4 = (f32[32,128]{1,0:T(8,128)S(1)}, f32[32,128]{1,0:T(8,128)S(1)}, u32[]{:S(2)}, u32[]{:S(2)}) collective-permute-start(f32[32,128]{1,0:T(8,128)S(1)} %add.24), channel_id=1, source_target_pairs={{0,2},{1,3},{2,0},{3,1},{4,6},{5,7},{6,4},{7,5},{8,10},{9,11},{10,... | collective-permute-start | bytes 49160 | tf_op jit(solution)/shard_map/ppermute | solution.py:345
  27.5 5.6 %collective-permute-start.9 = (f32[32,128]{1,0:T(8,128)S(1)}, f32[32,128]{1,0:T(8,128)S(1)}, u32[]{:S(2)}, u32[]{:S(2)}) collective-permute-start(f32[32,128]{1,0:T(8,128)S(1)} %add_add_fusion.1), channel_id=1, source_target_pairs={{0,24},{1,25},{2,26},{3,27},{4,28},{5,29},{6,30},{7,31},{8,16},{9,... | collective-permute-start | bytes 49160 | tf_op jit(solution)/shard_map/ppermute | solution.py:345
  27.6 7.3 %collective-permute-start.8 = (f32[32,128]{1,0:T(8,128)S(1)}, f32[32,128]{1,0:T(8,128)S(1)}, u32[]{:S(2)}, u32[]{:S(2)}) collective-permute-start(f32[32,128]{1,0:T(8,128)S(1)} %add_add_fusion.1), channel_id=1, source_target_pairs={{0,16},{1,17},{2,18},{3,19},{4,20},{5,21},{6,22},{7,23},{8,24},{9,... | collective-permute-start | bytes 49160 | tf_op jit(solution)/shard_map/ppermute | solution.py:345
  33.0 3.7 %collective-permute-start.7 = (f32[32,128]{1,0:T(8,128)S(1)}, f32[32,128]{1,0:T(8,128)S(1)}, u32[]{:S(2)}, u32[]{:S(2)}) collective-permute-start(f32[32,128]{1,0:T(8,128)S(1)} %add_add_fusion.1), channel_id=1, source_target_pairs={{0,8},{1,9},{2,10},{3,11},{4,12},{5,13},{6,14},{7,15},{8,0},{9,1},... | collective-permute-start | bytes 49160 | tf_op jit(solution)/shard_map/ppermute | solution.py:345
  36.8 6.8 %collective-permute-start.10 = (f32[32,128]{1,0:T(8,128)S(1)}, f32[32,128]{1,0:T(8,128)S(1)}, u32[]{:S(2)}, u32[]{:S(2)}) collective-permute-start(f32[32,128]{1,0:T(8,128)S(1)} %add_add_fusion), channel_id=1, source_target_pairs={{0,56},{1,57},{2,58},{3,59},{4,60},{5,61},{6,62},{7,63},{8,48},{9,... | collective-permute-start | bytes 49160 | tf_op jit(solution)/shard_map/ppermute | solution.py:345

commit v7 on v6

--- a/solution.py
+++ b/solution.py
@@ -198,7 +198,7 @@
 
 def own_kernel(
     inner_ref, outer_ref, sines_ref, along_ref, shift_ref, w_ref, first_ref,
-    modes_ref, sums_ref, halo_w_ref, halo_ref, turned_ref, one_ref, two_ref,
+    two_ref, sums_ref, halo_w_ref, halo_ref, turned_ref, one_ref,
 ):
     k = lax.axis_index("xs")
 
@@ -217,7 +217,6 @@
     sweep(k, 0, whole(two_ref), weight, one_ref, hamiltonian=True)
     field = two_ref[HALO : HALO + ROWS].reshape(ROWS * SPAN, LANES)
     image = one_ref[HALO : HALO + ROWS].reshape(ROWS * SPAN, LANES)
-    modes_ref[...] = field
     high, low = split(field)
     image_high, image_low = split(image)
     main = dot_cells(high, jnp.concatenate([high, low, image_high, image_low], axis=1))
@@ -245,7 +244,7 @@
     sweep(k, 0, whole(one_ref), weight, two_ref)
     field = two_ref[HALO : HALO + ROWS].reshape(ROWS * SPAN, LANES)
     high, low = split(field)
-    own_high, own_low = split(modes_ref[...])
+    own_high, own_low = split(modes_ref[HALO : HALO + ROWS].reshape(ROWS * SPAN, LANES))
     main = dot_cells(high, jnp.concatenate([high, low, own_high, own_low], axis=1))
     rest = blocks(dot_cells(low, own_high))
     cross = blocks(main[:, LANES : 2 * LANES])
@@ -259,7 +258,7 @@
         for j in range(4):
             r = i * 4 + j
             pieces = [
-                modes_ref[pl.ds(r * SPAN + q * 8 + s, 8, stride=8), :] for s in range(8) for q in range(0, STEPS, 8)
+                modes_ref[pl.ds((r + HALO) * SPAN + q * 8 + s, 8, stride=8), :] for s in range(8) for q in range(0, STEPS, 8)
             ]
             parts_ref[r] = jnp.concatenate(split(jnp.concatenate(pieces, axis=0)), axis=1)
         return carry
@@ -345,7 +344,7 @@
         return [lax.ppermute(x, "xs", [(i, i ^ mask) for i in range(64)]) for mask in masks]
 
     v = v + others(v, 1)[0]
-    for unit in (2, 8):
+    for unit in (8, 2):
         one, two, three = others(v, unit, 2 * unit, 3 * unit)
         v = (v + one) + (two + three)
     return v + others(v, 7 * 8)[0]
@@ -398,10 +397,10 @@
     field, own = pl.pallas_call(
         own_kernel,
         name="own_trial",
-        out_shape=(jax.ShapeDtypeStruct((ROWS * SPAN, LANES), F32), jax.ShapeDtypeStruct((M, 2 * M), F32)),
+        out_shape=(jax.ShapeDtypeStruct((EXT, *field_shape), F32), jax.ShapeDtypeStruct((M, 2 * M), F32)),
         in_specs=[vmem] * 7,
         out_specs=(vmem, vmem),
-        scratch_shapes=[edges, edges, turned, trial, trial],
+        scratch_shapes=[edges, edges, turned, trial],
         compiler_params=params,
         cost_estimate=cost,
     )(inner, outer, *tables)
@@ -423,7 +422,7 @@
         out_specs=vmem,
         compiler_params=pltpu.CompilerParams(vmem_limit_bytes=12 * 2**20),
         cost_estimate=pl.CostEstimate(flops=2**20, bytes_accessed=2**22, transcendentals=0),
-    )(field)
+    )(field.reshape(EXT * SPAN, LANES))
     sums = add_over_strips(sums)
     modes, projected, correlations = pl.pallas_call(
         finish_kernel,

time: 46.6 us -> 46.6 us (level)
  waiting for transfers between devices: 13.2 us -> 14.1 us
  starting transfers between devices: 19.5 us -> 18.6 us
    ppermute x8, waiting for transfers between devices: 11.8 us -> 12.8 us  [others(): lax.ppermute(x, 'xs', [(i, i ^ mask) for i in range(64)])]
    ppermute x8, starting transfers between devices: 12.7 us -> 11.8 us  [others(): lax.ppermute(x, 'xs', [(i, i ^ mask) for i in range(64)])]
where the time goes in v7:
time: 46.6 us; the launch traced here: 46.4 us
  starting transfers between devices  18.6 us (40%)
  waiting for transfers between devices  14.1 us (30%)
  Pallas kernels  11.5 us (25%)
  local copies, waits for them, and re-layouts  1.51 us (3%)
  between operations  0.72 us (2%)
    ppermute x8, waiting for transfers between devices, others(): lax.ppermute(x, 'xs', [(i, i ^ mask) for i in range(64)])  12.8 us
    ppermute x8, starting transfers between devices, others(): lax.ppermute(x, 'xs', [(i, i ^ mask) for i in range(64)])  11.8 us
    ppermute x1, starting transfers between devices, local(): lax.ppermute(pert, 'xs', [(i, i - 1 if i % 2 == 0 else i + 1) for i in ra...  3.91 us
    pallas_call x1, Pallas kernels, local(): pl.pallas_call(own_kernel, name='own_trial', out_shape=(jax.ShapeDtypeStr...  3.67 us
    pallas_call x1, Pallas kernels, local(): pl.pallas_call(next_kernel, name='next_trial', out_shape=jax.ShapeDtypeSt...  3.56 us
    pallas_call x1, Pallas kernels, local(): pl.pallas_call(finish_kernel, name='finish', out_shape=(jax.ShapeDtypeStr...  2.85 us
    ppermute x1, starting transfers between devices, local(): lax.ppermute(strip, 'slab', [((i + 1) % 4, i) for i in range(4)])  2.84 us
    unnamed x4, local copies, waits for them, and re-layouts  1.51 us
  transfers between devices with their start and end apart: 11, of which 7 were waited for; matrix products, arithmetic and copies ran while one was open for 0% of the time, Pallas kernels for 11%

profile of v7, /device:TPU:64, one launch (start us, length us, event | category | flops | bytes accessed | tf_op | source)
XLA Modules:
  0.0 46.4 jit_solution(9802438151411059394)
XLA Ops:
  0.6 3.9 %collective-permute-start.1 = (s32[16,1024]{1,0:T(8,128)}, s32[16,1024]{1,0:T(8,128)S(1)}, u32[]{:S(2)}, u32[]{:S(2)}) collective-permute-start(s32[16,1024]{1,0:T(8,128)} %bitcast.9), channel_id=1, source_target_pairs={{1,2},{2,1},{3,4},{4,3},{5,6},{6,5},{7,8},{8,7},{9,10},{10,9},{11,... | collective-permute-start | bytes 196616 | tf_op jit(solution)/shard_map/ppermute | solution.py:357
  4.5 0.1 collective-permute-start
  4.6 0.0 copy-start
  4.7 0.8 %copy-done = s32[1,16,1024]{2,1,0:T(8,128)S(1)} copy-done((s32[1,16,1024]{2,1,0:T(8,128)S(1)}, s32[1,16,1024]{2,1,0:T(8,128)}, u32[]{:S(2)}) %copy-start) | copy-done | bytes 65560
  5.5 0.0 copy-start.1
  5.5 0.7 %copy-done.1 = s32[1,32,2]{1,2,0:T(2,128)S(1)} copy-done((s32[1,32,2]{1,2,0:T(2,128)S(1)}, s32[1,32,2]{1,2,0:T(2,128)}, u32[]{:S(2)}) %copy-start.1) | copy-done | bytes 280
  6.2 1.0 %prepare.1 = (s32[24,1024]{1,0:T(8,128)S(1)}, f32[32,8,128]{2,1,0:T(8,128)S(1)}, f32[24,128]{1,0:T(8,128)S(1)}, f32[8,128]{1,0:T(8,128)S(1)}, f32[16,32,8,128]{3...) custom-call(s32[16,1024]{1,0:T(8,128)S(1)} %bitcast.11, s32[2,32]{1,0:T(2,128)S(1)} %bitcast.12), custom_call_target="tpu_custom_call" | custom-call | flops 67108864 | bytes 4194304 | tf_op jit(solution)/shard_map/prepare/pallas_call | solution.py:361
  7.2 1.4 %collective-permute-done.1.outer_ref = s32[16,1024]{1,0:T(8,128)S(1)} collective-permute-done((s32[16,1024]{1,0:T(8,128)}, s32[16,1024]{1,0:T(8,128)S(1)}, u32[]{:S(2)}, u32[]{:S(2)}) %collective-permute-start.1) | collective-permute-done | bytes 65568 | tf_op jit(solution)/shard_map/ppermute | solution.py:357
  8.5 0.0 collective-permute-done.inner_ref
  8.6 2.8 %collective-permute-start.2 = (s32[24,1024]{1,0:T(8,128)S(1)}, s32[24,1024]{1,0:T(8,128)S(1)}, u32[]{:S(2)}, u32[]{:S(2)}) collective-permute-start(s32[24,1024]{1,0:T(8,128)S(1)} %assemble.1), channel_id=1, source_target_pairs={{64,0},{128,64},{192,128},{0,192},{65,1},{129,65},{193,129},{1,193... | collective-permute-start | bytes 294920 | tf_op jit(solution)/shard_map/ppermute | solution.py:391
  11.4 3.7 %own_trial.1 = (f32[24,32,8,128]{3,2,1,0:T(8,128)S(1)}, f32[32,64]{1,0:T(8,128)S(1)}) custom-call(s32[16,1024]{1,0:T(8,128)S(1)} %collective-permute-done.inner_ref, s32[16,1024]{1,0:T(8,128)S(1)} %collective-permute-done.1.outer_ref, f32[32,8,128]{2,1,0:T(8,128)S(1)} %get-tuple-element.15.sines_ref, f32[24,128]{1,0:T(8,128)S(1)} %get-tuple-element.16.along_ref, ...), custom_call_target="tpu_custom_call" | custom-call | flops 1073741824 | bytes 8388608 | tf_op jit(solution)/shard_map/own_trial/pallas_call | solution.py:397
  15.1 0.0 collective-permute-done.2.strip_ref
  15.1 3.6 %next_trial.1 = f32[32,128]{1,0:T(8,128)S(1)} custom-call(s32[24,1024]{1,0:T(8,128)S(1)} %collective-permute-done.2.strip_ref, f32[24,32,8,128]{3,2,1,0:T(8,128)S(1)} %get-tuple-element.20.modes_ref, f32[32,64]{1,0:T(8,128)S(1)} %get-tuple-element.21.own_ref), custom_call_target="tpu_custom_call" | custom-call | flops 1073741824 | bytes 8388608 | tf_op jit(solution)/shard_map/next_trial/pallas_call | solution.py:407
  18.7 0.1 collective-permute-start.3
  18.8 1.2 %collective-permute-done.3 = f32[32,128]{1,0:T(8,128)S(1)} collective-permute-done((f32[32,128]{1,0:T(8,128)S(1)}, f32[32,128]{1,0:T(8,128)S(1)}, u32[]{:S(2)}, u32[]{:S(2)}) %collective-permute-start.3) | collective-permute-done | bytes 16416 | tf_op jit(solution)/shard_map/ppermute | solution.py:344
  19.9 0.1 collective-permute-start.6
  20.0 4.2 %collective-permute-start.5 = (f32[32,128]{1,0:T(8,128)S(1)}, f32[32,128]{1,0:T(8,128)S(1)}, u32[]{:S(2)}, u32[]{:S(2)}) collective-permute-start(f32[32,128]{1,0:T(8,128)S(1)} %add.24), channel_id=1, source_target_pairs={{0,16},{1,17},{2,18},{3,19},{4,20},{5,21},{6,22},{7,23},{8,24},{9,... | collective-permute-start | bytes 49160 | tf_op jit(solution)/shard_map/ppermute | solution.py:344
  24.2 0.0 collective-permute-start.4
  24.2 0.0 collective-permute-done.6
  24.2 1.9 %collective-permute-done.5 = f32[32,128]{1,0:T(8,128)S(1)} collective-permute-done((f32[32,128]{1,0:T(8,128)S(1)}, f32[32,128]{1,0:T(8,128)S(1)}, u32[]{:S(2)}, u32[]{:S(2)}) %collective-permute-start.5) | collective-permute-done | bytes 16416 | tf_op jit(solution)/shard_map/ppermute | solution.py:344
  26.1 1.9 %collective-permute-done.4 = f32[32,128]{1,0:T(8,128)S(1)} collective-permute-done((f32[32,128]{1,0:T(8,128)S(1)}, f32[32,128]{1,0:T(8,128)S(1)}, u32[]{:S(2)}, u32[]{:S(2)}) %collective-permute-start.4) | collective-permute-done | bytes 16416 | tf_op jit(solution)/shard_map/ppermute | solution.py:344
  28.0 3.5 %collective-permute-start.9 = (f32[32,128]{1,0:T(8,128)S(1)}, f32[32,128]{1,0:T(8,128)S(1)}, u32[]{:S(2)}, u32[]{:S(2)}) collective-permute-start(f32[32,128]{1,0:T(8,128)S(1)} %add_add_fusion.1), channel_id=1, source_target_pairs={{0,6},{1,7},{2,4},{3,5},{4,2},{5,3},{6,0},{7,1},{8,14},{9,15},{10,... | collective-permute-start | bytes 49160 | tf_op jit(solution)/shard_map/ppermute | solution.py:344
  31.5 0.0 collective-permute-start.8
  31.5 1.0 %collective-permute-start.7 = (f32[32,128]{1,0:T(8,128)S(1)}, f32[32,128]{1,0:T(8,128)S(1)}, u32[]{:S(2)}, u32[]{:S(2)}) collective-permute-start(f32[32,128]{1,0:T(8,128)S(1)} %add_add_fusion.1), channel_id=1, source_target_pairs={{0,2},{1,3},{2,0},{3,1},{4,6},{5,7},{6,4},{7,5},{8,10},{9,11},{10,... | collective-permute-start | bytes 49160 | tf_op jit(solution)/shard_map/ppermute | solution.py:344
  32.4 0.8 %collective-permute-done.9 = f32[32,128]{1,0:T(8,128)S(1)} collective-permute-done((f32[32,128]{1,0:T(8,128)S(1)}, f32[32,128]{1,0:T(8,128)S(1)}, u32[]{:S(2)}, u32[]{:S(2)}) %collective-permute-start.9) | collective-permute-done | bytes 16416 | tf_op jit(solution)/shard_map/ppermute | solution.py:344
  33.2 3.5 %collective-permute-done.8 = f32[32,128]{1,0:T(8,128)S(1)} collective-permute-done((f32[32,128]{1,0:T(8,128)S(1)}, f32[32,128]{1,0:T(8,128)S(1)}, u32[]{:S(2)}, u32[]{:S(2)}) %collective-permute-start.8) | collective-permute-done | bytes 16416 | tf_op jit(solution)/shard_map/ppermute | solution.py:344
  36.7 0.0 collective-permute-done.7
  36.7 2.9 %collective-permute-start.10 = (f32[32,128]{1,0:T(8,128)S(1)}, f32[32,128]{1,0:T(8,128)S(1)}, u32[]{:S(2)}, u32[]{:S(2)}) collective-permute-start(f32[32,128]{1,0:T(8,128)S(1)} %add_add_fusion), channel_id=1, source_target_pairs={{0,56},{1,57},{2,58},{3,59},{4,60},{5,61},{6,62},{7,63},{8,48},{9,... | collective-permute-start | bytes 49160 | tf_op jit(solution)/shard_map/ppermute | solution.py:344
  39.6 0.4 parts.1.parts_ref
  40.0 3.6 %collective-permute-done.10 = f32[32,128]{1,0:T(8,128)S(1)} collective-permute-done((f32[32,128]{1,0:T(8,128)S(1)}, f32[32,128]{1,0:T(8,128)S(1)}, u32[]{:S(2)}, u32[]{:S(2)}) %collective-permute-start.10) | collective-permute-done | bytes 16416 | tf_op jit(solution)/shard_map/ppermute | solution.py:344
  43.6 2.9 %finish.1 = (f32[32,16,1024]{2,1,0:T(8,128)}, f32[32,32]{1,0:T(8,128)}, f32[32,32]{1,0:T(8,128)}) custom-call(f32[32,128]{1,0:T(8,128)S(1)} %add.31.sums_ref, bf16[16,256,256]{2,1,0:T(8,128)(2,1)S(1)} %parts.1.parts_ref), custom_call_target="tpu_custom_call" | custom-call | flops 268435456 | bytes 8388608 | tf_op jit(solution)/shard_map/finish/pallas_call | solution.py:427
  (5 shorter events, 0.0 us)
Async XLA Ops:
  0.6 7.9 %collective-permute-start.1 = (s32[16,1024]{1,0:T(8,128)}, s32[16,1024]{1,0:T(8,128)S(1)}, u32[]{:S(2)}, u32[]{:S(2)}) collective-permute-start(s32[16,1024]{1,0:T(8,128)} %bitcast.9), channel_id=1, source_target_pairs={{1,2},{2,1},{3,4},{4,3},{5,6},{6,5},{7,8},{8,7},{9,10},{10,9},{11,... | collective-permute-start | bytes 196616 | tf_op jit(solution)/shard_map/ppermute | solution.py:357
  4.5 4.0 %collective-permute-start = (s32[16,1024]{1,0:T(8,128)}, s32[16,1024]{1,0:T(8,128)S(1)}, u32[]{:S(2)}, u32[]{:S(2)}) collective-permute-start(s32[16,1024]{1,0:T(8,128)} %bitcast.10), channel_id=1, source_target_pairs={{0,1},{1,0},{2,3},{3,2},{4,5},{5,4},{6,7},{7,6},{8,9},{9,8},{10,11... | collective-permute-start | bytes 196616 | tf_op jit(solution)/shard_map/ppermute | solution.py:356
  4.6 0.8 %copy-start = (s32[1,16,1024]{2,1,0:T(8,128)S(1)}, s32[1,16,1024]{2,1,0:T(8,128)}, u32[]{:S(2)}) copy-start(s32[1,16,1024]{2,1,0:T(8,128)} %param.2) | copy-start | bytes 196612
  5.5 0.7 %copy-start.1 = (s32[1,32,2]{1,2,0:T(2,128)S(1)}, s32[1,32,2]{1,2,0:T(2,128)}, u32[]{:S(2)}) copy-start(s32[1,32,2]{1,2,0:T(2,128)} %param.3) | copy-start | bytes 772
  8.6 6.5 %collective-permute-start.2 = (s32[24,1024]{1,0:T(8,128)S(1)}, s32[24,1024]{1,0:T(8,128)S(1)}, u32[]{:S(2)}, u32[]{:S(2)}) collective-permute-start(s32[24,1024]{1,0:T(8,128)S(1)} %assemble.1), channel_id=1, source_target_pairs={{64,0},{128,64},{192,128},{0,192},{65,1},{129,65},{193,129},{1,193... | collective-permute-start | bytes 294920 | tf_op jit(solution)/shard_map/ppermute | solution.py:391
  18.7 1.3 %collective-permute-start.3 = (f32[32,128]{1,0:T(8,128)S(1)}, f32[32,128]{1,0:T(8,128)S(1)}, u32[]{:S(2)}, u32[]{:S(2)}) collective-permute-start(f32[32,128]{1,0:T(8,128)S(1)} %next_trial.1), channel_id=1, source_target_pairs={{0,1},{1,0},{2,3},{3,2},{4,5},{5,4},{6,7},{7,6},{8,9},{9,8},{10,11... | collective-permute-start | bytes 49160 | tf_op jit(solution)/shard_map/ppermute | solution.py:344
  19.9 4.3 %collective-permute-start.6 = (f32[32,128]{1,0:T(8,128)S(1)}, f32[32,128]{1,0:T(8,128)S(1)}, u32[]{:S(2)}, u32[]{:S(2)}) collective-permute-start(f32[32,128]{1,0:T(8,128)S(1)} %add.24), channel_id=1, source_target_pairs={{0,24},{1,25},{2,26},{3,27},{4,28},{5,29},{6,30},{7,31},{8,16},{9,... | collective-permute-start | bytes 49160 | tf_op jit(solution)/shard_map/ppermute | solution.py:344
  20.0 6.1 %collective-permute-start.5 = (f32[32,128]{1,0:T(8,128)S(1)}, f32[32,128]{1,0:T(8,128)S(1)}, u32[]{:S(2)}, u32[]{:S(2)}) collective-permute-start(f32[32,128]{1,0:T(8,128)S(1)} %add.24), channel_id=1, source_target_pairs={{0,16},{1,17},{2,18},{3,19},{4,20},{5,21},{6,22},{7,23},{8,24},{9,... | collective-permute-start | bytes 49160 | tf_op jit(solution)/shard_map/ppermute | solution.py:344
  24.2 3.7 %collective-permute-start.4 = (f32[32,128]{1,0:T(8,128)S(1)}, f32[32,128]{1,0:T(8,128)S(1)}, u32[]{:S(2)}, u32[]{:S(2)}) collective-permute-start(f32[32,128]{1,0:T(8,128)S(1)} %add.24), channel_id=1, source_target_pairs={{0,8},{1,9},{2,10},{3,11},{4,12},{5,13},{6,14},{7,15},{8,0},{9,1},... | collective-permute-start | bytes 49160 | tf_op jit(solution)/shard_map/ppermute | solution.py:344
  28.0 5.2 %collective-permute-start.9 = (f32[32,128]{1,0:T(8,128)S(1)}, f32[32,128]{1,0:T(8,128)S(1)}, u32[]{:S(2)}, u32[]{:S(2)}) collective-permute-start(f32[32,128]{1,0:T(8,128)S(1)} %add_add_fusion.1), channel_id=1, source_target_pairs={{0,6},{1,7},{2,4},{3,5},{4,2},{5,3},{6,0},{7,1},{8,14},{9,15},{10,... | collective-permute-start | bytes 49160 | tf_op jit(solution)/shard_map/ppermute | solution.py:344
  31.5 5.2 %collective-permute-start.8 = (f32[32,128]{1,0:T(8,128)S(1)}, f32[32,128]{1,0:T(8,128)S(1)}, u32[]{:S(2)}, u32[]{:S(2)}) collective-permute-start(f32[32,128]{1,0:T(8,128)S(1)} %add_add_fusion.1), channel_id=1, source_target_pairs={{0,4},{1,5},{2,6},{3,7},{4,0},{5,1},{6,2},{7,3},{8,12},{9,13},{10,... | collective-permute-start | bytes 49160 | tf_op jit(solution)/shard_map/ppermute | solution.py:344
  31.5 5.2 %collective-permute-start.7 = (f32[32,128]{1,0:T(8,128)S(1)}, f32[32,128]{1,0:T(8,128)S(1)}, u32[]{:S(2)}, u32[]{:S(2)}) collective-permute-start(f32[32,128]{1,0:T(8,128)S(1)} %add_add_fusion.1), channel_id=1, source_target_pairs={{0,2},{1,3},{2,0},{3,1},{4,6},{5,7},{6,4},{7,5},{8,10},{9,11},{10,... | collective-permute-start | bytes 49160 | tf_op jit(solution)/shard_map/ppermute | solution.py:344
  36.7 6.8 %collective-permute-start.10 = (f32[32,128]{1,0:T(8,128)S(1)}, f32[32,128]{1,0:T(8,128)S(1)}, u32[]{:S(2)}, u32[]{:S(2)}) collective-permute-start(f32[32,128]{1,0:T(8,128)S(1)} %add_add_fusion), channel_id=1, source_target_pairs={{0,56},{1,57},{2,58},{3,59},{4,60},{5,61},{6,62},{7,63},{8,48},{9,... | collective-permute-start | bytes 49160 | tf_op jit(solution)/shard_map/ppermute | solution.py:344
